TPU v7x, 32 devices: a whole 2x2x4 slice. The times are simulated.
32 devices in a mesh: items: 8 (over y, x, core), band: 4 (over z).
Axes of the slice: x: 2, y: 2, z: 4, core: 2. Of those that a mesh axis runs over, the one named last changes fastest.
Arguments:
- tokens: bfloat16 [16, 1024, 1024], P('items', 'band'), may hold values from -17 to 17
- cotangent: bfloat16 [16, 1024, 1024], P('items', 'band'), may hold values from -6 to 6
- running_mean: float32 [1024], replicated, may hold values from -3 to 3
- running_var: float32 [1024], replicated, may hold values from 0.5 to 4
- slot_table: int32 [16], replicated, may hold values from 0 to 15, as said below
- patch_counts: int32 [16], replicated, may hold values from 128 to 1024, as said below
- ln1_gain: bfloat16 [1024], replicated, may hold values from 0.5 to 1.5
- ln1_bias: bfloat16 [1024], replicated, may hold values from -1.75 to 1.75
- w_query: bfloat16 [1024, 1024], replicated, may hold values from -0.1875 to 0.1875
- b_query: bfloat16 [1024], replicated, may hold values from -1.75 to 1.75
- w_key: bfloat16 [1024, 1024], replicated, may hold values from -0.1875 to 0.1875
- w_value: bfloat16 [1024, 1024], replicated, may hold values from -0.1875 to 0.1875
- b_value: bfloat16 [1024], replicated, may hold values from -1.75 to 1.75
- w_out: bfloat16 [1024, 1024], replicated, may hold values from -0.75 to 0.75
- b_out: bfloat16 [1024], replicated, may hold values from -1.75 to 1.75
- ln2_gain: bfloat16 [1024], replicated, may hold values from 0.5 to 1.5
- ln2_bias: bfloat16 [1024], replicated, may hold values from -1.75 to 1.75
- w_up: bfloat16 [1024, 4096], replicated, may hold values from -0.1875 to 0.1875
- b_up: bfloat16 [4096], replicated, may hold values from -1.75 to 1.75
- w_down: bfloat16 [4096, 1024], replicated, may hold values from -0.09375 to 0.09375
- b_down: bfloat16 [1024], replicated, may hold values from -1.75 to 1.75
Outputs:
- output: bfloat16 [16, 1024, 1024], P('items', 'band')
- d_tokens: bfloat16 [16, 1024, 1024], P('items', 'band')
- new_mean: float32 [1024], replicated
- new_var: float32 [1024], replicated
- d_ln1_gain: float32 [1024], replicated
- d_ln1_bias: float32 [1024], replicated
- d_w_query: float32 [1024, 1024], P('items', 'band')
- d_b_query: float32 [1024], replicated
- d_w_key: float32 [1024, 1024], P('items', 'band')
- d_w_value: float32 [1024, 1024], P('items', 'band')
- d_b_value: float32 [1024], replicated
- d_w_out: float32 [1024, 1024], P('items', 'band')
- d_b_out: float32 [1024], replicated
- d_ln2_gain: float32 [1024], replicated
- d_ln2_bias: float32 [1024], replicated
- d_w_up: float32 [1024, 4096], P('items', 'band')
- d_b_up: float32 [4096], replicated
- d_w_down: float32 [4096, 1024], P('items', 'band')
- d_b_down: float32 [1024], replicated
Inputs may be any that keep to these rules, and one draw needn't show every extreme that they name: `slot_table`: a permutation: each group of 2 slots 2g, 2g + 1 holds one item of 1024 patches and one shorter item. `patch_counts`: the items named in the first half of the ids have 1024 patches.
All inputs are finite; a program needn't handle non-finite values.
Results may differ from a plain program's by a relative error of at most 0.024.
Values may be sent and summed in bfloat16 or wider, within the bound.
A program may use at most 320 MiB of HBM per device.

v0:
```python
import jax
import jax.numpy as jnp
from jax import lax
from jax.sharding import PartitionSpec as P

HEADS = 16
HEAD_DIM = 64


epsilon = 1e-05
score_scale = 0.125
masked_score = -1e30
momentum = 0.5


def layer_norm(value, gain, shift):
    centre = value - jnp.mean(value, -1, keepdims=True)
    spread = jnp.mean(centre * centre, -1, keepdims=True)
    return centre * lax.rsqrt(spread + epsilon) * gain + shift


def gelu_tanh(value):
    return (
        0.5
        * value
        * (1.0 + jnp.tanh(0.7978845608028654 * (value + 0.044715 * value * value * value)))
    )


def head_layout():
    heads_per = 4
    return (heads_per, HEADS // heads_per, heads_per * HEAD_DIM)


def group_scores(q_part, k_part, key_mask):
    scores = (
        jnp.einsum("rhd,khd->hrk", q_part, k_part, preferred_element_type=jnp.float32) * score_scale
    )
    return jnp.where(key_mask[None, None, :], scores, masked_score)


def attend_forward(q_slot, keys_slot, values_slot, key_mask):
    heads_per, groups, group_width = head_layout()
    band_rows = q_slot.shape[0]
    seq_length = keys_slot.shape[0]

    def head_block(group_index):
        begin = group_index * group_width
        q_part = lax.dynamic_slice_in_dim(q_slot, begin, group_width, 1).reshape(
            band_rows, heads_per, HEAD_DIM
        )
        k_part = lax.dynamic_slice_in_dim(keys_slot, begin, group_width, 1).reshape(
            seq_length, heads_per, HEAD_DIM
        )
        v_part = lax.dynamic_slice_in_dim(values_slot, begin, group_width, 1).reshape(
            seq_length, heads_per, HEAD_DIM
        )
        scores = group_scores(q_part, k_part, key_mask)
        top_score = jnp.max(scores, -1, keepdims=True)
        log_total = top_score + jnp.log(jnp.sum(jnp.exp(scores - top_score), -1, keepdims=True))
        probs_low = jnp.exp(scores - log_total).astype(jnp.bfloat16)
        attended = jnp.einsum("hrk,khd->rhd", probs_low, v_part, preferred_element_type=jnp.float32)
        return (attended.reshape(band_rows, group_width), log_total[..., 0])

    attended, log_totals = lax.map(head_block, jnp.arange(groups, dtype=jnp.int32))
    return (attended.transpose(1, 0, 2).reshape(band_rows, groups * group_width), log_totals)


def attend_backward(q_slot, keys_slot, values_slot, key_mask, d_attn_slot, row_delta, log_totals):
    heads_per, groups, group_width = head_layout()
    query_rows = q_slot.shape[0]
    seq_length = keys_slot.shape[0]
    deltas = jnp.transpose(row_delta).reshape(groups, heads_per, query_rows)

    def head_block(inputs):
        group_index, log_total, delta_part = inputs
        begin = group_index * group_width
        q_part = lax.dynamic_slice_in_dim(q_slot, begin, group_width, 1).reshape(
            query_rows, heads_per, HEAD_DIM
        )
        k_part = lax.dynamic_slice_in_dim(keys_slot, begin, group_width, 1).reshape(
            seq_length, heads_per, HEAD_DIM
        )
        v_part = lax.dynamic_slice_in_dim(values_slot, begin, group_width, 1).reshape(
            seq_length, heads_per, HEAD_DIM
        )
        d_part = lax.dynamic_slice_in_dim(d_attn_slot, begin, group_width, 1).reshape(
            query_rows, heads_per, HEAD_DIM
        )
        scores = group_scores(q_part, k_part, key_mask)
        probs = jnp.exp(scores - log_total[..., None])
        d_probs = jnp.einsum("rhd,khd->hrk", d_part, v_part, preferred_element_type=jnp.float32)
        d_scores = (probs * (d_probs - delta_part[..., None])).astype(jnp.bfloat16)
        results = []
        d_q_part = (
            jnp.einsum("hrk,khd->rhd", d_scores, k_part, preferred_element_type=jnp.float32)
            * score_scale
        )
        results.append(d_q_part.reshape(query_rows, group_width))
        probs_low = probs.astype(jnp.bfloat16)
        d_k_part = (
            jnp.einsum("hrk,rhd->khd", d_scores, q_part, preferred_element_type=jnp.float32)
            * score_scale
        )
        d_v_part = jnp.einsum("hrk,rhd->khd", probs_low, d_part, preferred_element_type=jnp.float32)
        results.append(d_k_part.reshape(seq_length, group_width))
        results.append(d_v_part.reshape(seq_length, group_width))
        return tuple(results)

    mapped = lax.map(head_block, (jnp.arange(groups, dtype=jnp.int32), log_totals, deltas))
    full_width = groups * group_width
    return tuple((piece.transpose(1, 0, 2).reshape(piece.shape[1], full_width) for piece in mapped))


def local(
    tokens,
    cotangent,
    running_mean,
    running_var,
    slot_table,
    patch_counts,
    ln1_gain,
    ln1_bias,
    w_query,
    b_query,
    w_key,
    w_value,
    b_value,
    w_out,
    b_out,
    ln2_gain,
    ln2_bias,
    w_up,
    b_up,
    w_down,
    b_down,
):
    slot_count, band_rows, model_width = tokens.shape
    seq_length = band_rows * lax.axis_size("band")
    item_rank = lax.axis_index("items")
    band_rank = lax.axis_index("band")
    every_slot = jnp.arange(slot_table.shape[0], dtype=jnp.int32)
    my_slots = item_rank * slot_count + jnp.arange(slot_count, dtype=jnp.int32)
    item_ids = jnp.sum(
        jnp.where(every_slot[None, :] == my_slots[:, None], slot_table[None, :], 0), 1
    )
    lengths = jnp.sum(
        jnp.where(every_slot[None, :] == item_ids[:, None], patch_counts[None, :], 0), 1
    )
    key_mask = jnp.arange(seq_length, dtype=jnp.int32)[None, :] < lengths[:, None]
    row_mask = (band_rank * band_rows + jnp.arange(band_rows, dtype=jnp.int32))[None, :] < lengths[
        :, None
    ]
    row_keep = row_mask.astype(jnp.float32).reshape(-1, 1)
    raw_flat = tokens.astype(jnp.float32).reshape(-1, model_width)
    part_one = jnp.sum(row_keep * raw_flat, 0)
    part_two = jnp.sum(row_keep * raw_flat * raw_flat, 0)
    total_one, total_two = lax.psum((part_one, part_two), ("items", "band"))
    patch_total = jnp.sum(patch_counts).astype(jnp.float32)
    batch_mean = total_one / patch_total
    batch_var = total_two / patch_total - batch_mean * batch_mean
    new_mean = momentum * running_mean + momentum * batch_mean
    new_var = momentum * running_var + momentum * batch_var
    inverse = lax.rsqrt(new_var + epsilon)
    normed_in = (raw_flat - new_mean) * inverse
    gain_one = ln1_gain.astype(jnp.float32)
    shift_one = ln1_bias.astype(jnp.float32)
    gain_two = ln2_gain.astype(jnp.float32)
    shift_two = ln2_bias.astype(jnp.float32)
    h_one_full, norm_one_back = jax.vjp(layer_norm, normed_in, gain_one, shift_one)
    h_one = h_one_full.astype(jnp.bfloat16)
    queries = (
        jnp.dot(h_one, w_query, preferred_element_type=jnp.float32) + b_query.astype(jnp.float32)
    ).astype(jnp.bfloat16)
    key_local = (
        jnp.dot(h_one, w_key, preferred_element_type=jnp.float32)
        .astype(jnp.bfloat16)
        .reshape(slot_count, band_rows, model_width)
    )
    value_local = (
        (jnp.dot(h_one, w_value, preferred_element_type=jnp.float32) + b_value.astype(jnp.float32))
        .astype(jnp.bfloat16)
        .reshape(slot_count, band_rows, model_width)
    )
    keys_all, values_all = (
        lax.all_gather(key_local, "band", axis=1, tiled=True),
        lax.all_gather(value_local, "band", axis=1, tiled=True),
    )
    q_slots = queries.reshape(slot_count, band_rows, model_width)
    attended_list = []
    totals_list = []
    for slot_index in range(slot_count):
        attended, log_totals = attend_forward(
            q_slots[slot_index], keys_all[slot_index], values_all[slot_index], key_mask[slot_index]
        )
        attended_list.append(attended)
        totals_list.append(log_totals)
    attn_full = jnp.concatenate(attended_list, 0)
    attn_low = attn_full.astype(jnp.bfloat16)
    residual = (
        normed_in
        + jnp.dot(attn_low, w_out, preferred_element_type=jnp.float32)
        + b_out.astype(jnp.float32)
    )
    h_two_full, norm_two_back = jax.vjp(layer_norm, residual, gain_two, shift_two)
    h_two = h_two_full.astype(jnp.bfloat16)
    up_proj = jnp.dot(h_two, w_up, preferred_element_type=jnp.float32) + b_up.astype(jnp.float32)
    activated_full, gelu_back = jax.vjp(gelu_tanh, up_proj)
    activated = activated_full.astype(jnp.bfloat16)
    result = (
        residual
        + jnp.dot(activated, w_down, preferred_element_type=jnp.float32)
        + b_down.astype(jnp.float32)
    )
    output = result.astype(jnp.bfloat16).reshape(slot_count, band_rows, model_width)
    cot_low = cotangent.reshape(-1, model_width)
    cot_full = cot_low.astype(jnp.float32)
    d_w_down = jnp.einsum("tf,td->fd", activated, cot_low, preferred_element_type=jnp.float32)
    d_b_down = jnp.sum(cot_full, 0)
    d_activated = jnp.einsum("td,fd->tf", cot_low, w_down, preferred_element_type=jnp.float32)
    (d_up_full,) = gelu_back(d_activated)
    d_up = d_up_full.astype(jnp.bfloat16)
    d_w_up = jnp.einsum("td,tf->df", h_two, d_up, preferred_element_type=jnp.float32)
    d_b_up = jnp.sum(d_up, 0, dtype=jnp.float32)
    d_h_two = jnp.einsum("tf,df->td", d_up, w_up, preferred_element_type=jnp.float32)
    d_res_norm, d_gain_two, d_shift_two = norm_two_back(d_h_two)
    d_residual = cot_full + d_res_norm
    d_branch = d_residual.astype(jnp.bfloat16)
    d_w_out = jnp.einsum("td,te->de", attn_low, d_branch, preferred_element_type=jnp.float32)
    d_b_out = jnp.sum(d_branch, 0, dtype=jnp.float32)
    d_attn = jnp.einsum("te,de->td", d_branch, w_out, preferred_element_type=jnp.float32).astype(
        jnp.bfloat16
    )
    row_delta = jnp.sum(
        (d_attn.astype(jnp.float32) * attn_full).reshape(slot_count, band_rows, HEADS, HEAD_DIM), -1
    )
    d_attn_slots = d_attn.reshape(slot_count, band_rows, model_width)
    back_keys, back_values = (keys_all, values_all)
    d_q_list = []
    d_k_list = []
    d_v_list = []
    for slot_index in range(slot_count):
        d_q_slot, d_k_slot, d_v_slot = attend_backward(
            q_slots[slot_index],
            back_keys[slot_index],
            back_values[slot_index],
            key_mask[slot_index],
            d_attn_slots[slot_index],
            row_delta[slot_index],
            totals_list[slot_index],
        )
        d_q_list.append(d_q_slot)
        d_k_list.append(d_k_slot)
        d_v_list.append(d_v_slot)
    d_keys_mine, d_values_mine = (
        lax.psum_scatter(
            jnp.stack(d_k_list).astype(jnp.bfloat16), "band", scatter_dimension=1, tiled=True
        ).astype(jnp.float32),
        lax.psum_scatter(
            jnp.stack(d_v_list).astype(jnp.bfloat16), "band", scatter_dimension=1, tiled=True
        ).astype(jnp.float32),
    )
    d_queries = jnp.concatenate(d_q_list, 0).astype(jnp.bfloat16)
    d_keys = d_keys_mine.reshape(-1, model_width).astype(jnp.bfloat16)
    d_values = d_values_mine.reshape(-1, model_width).astype(jnp.bfloat16)
    d_w_query = jnp.einsum("td,te->de", h_one, d_queries, preferred_element_type=jnp.float32)
    d_b_query = jnp.sum(d_queries, 0, dtype=jnp.float32)
    d_w_key = jnp.einsum("td,te->de", h_one, d_keys, preferred_element_type=jnp.float32)
    d_w_value = jnp.einsum("td,te->de", h_one, d_values, preferred_element_type=jnp.float32)
    d_b_value = jnp.sum(d_values, 0, dtype=jnp.float32)
    d_h_one = jnp.einsum("te,de->td", d_queries, w_query, preferred_element_type=jnp.float32)
    d_h_one = d_h_one + jnp.einsum("te,de->td", d_keys, w_key, preferred_element_type=jnp.float32)
    d_h_one = d_h_one + jnp.einsum(
        "te,de->td", d_values, w_value, preferred_element_type=jnp.float32
    )
    d_start_norm, d_gain_one, d_shift_one = norm_one_back(d_h_one)
    d_start = d_residual + d_start_norm
    centred = raw_flat - new_mean
    small_sums = lax.psum(
        (
            jnp.sum(d_start, 0),
            jnp.sum(d_start * centred, 0),
            d_gain_one,
            d_shift_one,
            d_b_query,
            d_b_value,
            d_b_out,
            d_gain_two,
            d_shift_two,
            d_b_up,
            d_b_down,
        ),
        ("items", "band"),
    )
    sum_g = small_sums[0]
    sum_gx = small_sums[1]
    cube = inverse * inverse * inverse
    d_raw = d_start * inverse + row_keep * (
        -0.5 * inverse * sum_g / patch_total
        - 0.5 * cube * sum_gx * (raw_flat - batch_mean) / patch_total
    )
    d_tokens = d_raw.astype(jnp.bfloat16).reshape(slot_count, band_rows, model_width)
    weight_grads = (
        lax.psum_scatter(
            d_w_query.astype(jnp.bfloat16), "items", scatter_dimension=0, tiled=True
        ).astype(jnp.float32),
        lax.psum_scatter(
            d_w_key.astype(jnp.bfloat16), "items", scatter_dimension=0, tiled=True
        ).astype(jnp.float32),
        lax.psum_scatter(
            d_w_value.astype(jnp.bfloat16), "items", scatter_dimension=0, tiled=True
        ).astype(jnp.float32),
        lax.psum_scatter(
            d_w_out.astype(jnp.bfloat16), "items", scatter_dimension=0, tiled=True
        ).astype(jnp.float32),
        lax.psum_scatter(
            d_w_up.astype(jnp.bfloat16), "items", scatter_dimension=0, tiled=True
        ).astype(jnp.float32),
        lax.psum_scatter(
            d_w_down.astype(jnp.bfloat16), "items", scatter_dimension=0, tiled=True
        ).astype(jnp.float32),
    )
    weight_grads = (
        lax.psum_scatter(
            weight_grads[0].astype(jnp.bfloat16), "band", scatter_dimension=1, tiled=True
        ).astype(jnp.float32),
        lax.psum_scatter(
            weight_grads[1].astype(jnp.bfloat16), "band", scatter_dimension=1, tiled=True
        ).astype(jnp.float32),
        lax.psum_scatter(
            weight_grads[2].astype(jnp.bfloat16), "band", scatter_dimension=1, tiled=True
        ).astype(jnp.float32),
        lax.psum_scatter(
            weight_grads[3].astype(jnp.bfloat16), "band", scatter_dimension=1, tiled=True
        ).astype(jnp.float32),
        lax.psum_scatter(
            weight_grads[4].astype(jnp.bfloat16), "band", scatter_dimension=1, tiled=True
        ).astype(jnp.float32),
        lax.psum_scatter(
            weight_grads[5].astype(jnp.bfloat16), "band", scatter_dimension=1, tiled=True
        ).astype(jnp.float32),
    )
    return (
        output,
        d_tokens,
        new_mean,
        new_var,
        small_sums[2],
        small_sums[3],
        weight_grads[0],
        small_sums[4],
        weight_grads[1],
        weight_grads[2],
        small_sums[5],
        weight_grads[3],
        small_sums[6],
        small_sums[7],
        small_sums[8],
        weight_grads[4],
        small_sums[9],
        weight_grads[5],
        small_sums[10],
    )


def solution(mesh):
    return jax.shard_map(
        local,
        mesh=mesh,
        in_specs=(
            P("items", "band", None),
            P("items", "band", None),
            P(),
            P(),
            P(),
            P(),
            P(),
            P(),
            P(),
            P(),
            P(),
            P(),
            P(),
            P(),
            P(),
            P(),
            P(),
            P(),
            P(),
            P(),
            P(),
        ),
        out_specs=(
            P("items", "band", None),
            P("items", "band", None),
            P(),
            P(),
            P(),
            P(),
            P("items", "band"),
            P(),
            P("items", "band"),
            P("items", "band"),
            P(),
            P("items", "band"),
            P(),
            P(),
            P(),
            P("items", "band"),
            P(),
            P("items", "band"),
            P(),
        ),
        check_vma=False,
    )
```

profile of v0, /device:TPU:0, one launch (start us, length us, event | category | flops | bytes accessed | tf_op | source)
XLA Modules:
  0.0 1112.2 jit_solution(17755140195578103394)
XLA Ops:
  13.4 42.1 %all-reduce.1 = (f32[1024]{0:T(1024)S(1)}, f32[1024]{0:T(1024)S(1)}) all-reduce(f32[1024]{0:T(1024)S(1)} %get-tuple-element.413, f32[1024]{0:T(1024)S(1)} %get-tuple-element.412), channel_id=1, replica_groups=mesh['items'=8,'band'=4] {'items','band'}, use_global_device_ids=true, to_apply=%region_3.4 | all-reduce | flops 2048 | bytes 16384 | tf_op jit(solution)/shard_map/psum | solution.py:158
  81.5 65.8 %all-gather.3.cloned.1.call-done = bf16[2,1024,1024]{1,2,0:T(8,128)(2,1)} async-done(((bf16[2,256,1024]{1,2,0:T(8,128)(2,1)}), bf16[2,1024,1024]{1,2,0:T(8,128)(2,1)}) %all-gather.3.cloned.1.call-update) | async-done | bytes 4194320 | tf_op jit(solution)/shard_map/all_gather | solution.py:187
  151.9 75.7 %all-gather.5.cloned.1.call-done = bf16[2,1024,1024]{1,2,0:T(8,128)(2,1)} async-done(((bf16[2,256,1024]{1,2,0:T(8,128)(2,1)}), bf16[2,1024,1024]{1,2,0:T(8,128)(2,1)}) %all-gather.5.cloned.1.call-update) | async-done | bytes 4194320 | tf_op jit(solution)/shard_map/all_gather | solution.py:186
  233.3 28.9 %while.52 = (s32[]{:T(128)}, f32[4,256,256]{1,2,0:T(8,128)}, f32[4,4,256]{2,1,0:T(4,128)S(1)}, s32[4]{0:T(128)S(1)}, bf16[1024,1024]{0,1:T(8,128)(2,1)}, /*index...) while((s32[]{:T(128)}, f32[4,256,256]{1,2,0:T(8,128)}, ...), condition=%wide.region_12.13_spmd, body=%wide.region_9.12_spmd.sunk | while | flops 279968768 | bytes 16946884 | solution.py:65
  265.8 28.4 %while.53 = (s32[]{:T(128)}, f32[4,256,256]{1,2,0:T(8,128)}, f32[4,4,256]{2,1,0:T(4,128)S(1)}, s32[4]{0:T(128)S(1)}, bf16[1024,1024]{0,1:T(8,128)(2,1)}, /*index...) while((s32[]{:T(128)}, f32[4,256,256]{1,2,0:T(8,128)}, ...), condition=%wide.region_16.17_spmd, body=%wide.region_13.16_spmd.sunk | while | flops 279968768 | bytes 16946884 | solution.py:65
  300.2 10.7 fusion.80
  311.0 16.7 %convert_reduce_fusion = (f32[4096]{0:T(1024)}, bf16[512,4096]{1,0:T(8,128)(2,1)}) fusion(f32[512,4096]{1,0:T(8,128)} %fusion.80, f32[4096]{0:T(1024)S(1)} %convert_element_type.206, bf16[512,1024]{1,0:T(8,128)(2,1)S(1)} %bitcast.352, bf16[4096,1024]{1,0:T(8,128)(2,1)} %param.48), kind=kOutput, calls=%fused_computation.74 | convolution fusion | flops 4351586304 | bytes 22052864 | tf_op jit(solution)/shard_map/td,fd->tf/dot_general | solution.py:220
  352.6 56.1 %while.54 = (s32[]{:T(128)}, bf16[4,256,256]{1,2,0:T(8,128)(2,1)}, bf16[4,1024,256]{1,2,0:T(8,128)(2,1)}, bf16[4,1024,256]{1,2,0:T(8,128)(2,1)}, s32[4]{0:T(128)...) while((s32[]{:T(128)}, bf16[4,256,256]{1,2,0:T(8,128)(2,1)}, ...), condition=%wide.region_23.24_spmd, body=%wide.region_22.23_spmd.sunk | while | flops 682229760 | bytes 44205828 | solution.py:110
  412.0 57.9 %while.55 = (s32[]{:T(128)}, bf16[4,256,256]{1,2,0:T(8,128)(2,1)S(1)}, bf16[4,1024,256]{1,2,0:T(8,128)(2,1)}, bf16[4,1024,256]{1,2,0:T(8,128)(2,1)}, s32[4]{0:T(...) while((s32[]{:T(128)}, ...), condition=%wide.region_25.26_spmd, body=%wide.region_24.25_spmd.sunk | while | flops 682229760 | bytes 44205320 | solution.py:110
  502.5 54.5 %reduce-scatter.15.cloned.1.call-done = bf16[2,256,1024]{2,1,0:T(8,128)(2,1)} async-done(((bf16[2,1024,1024]{2,1,0:T(8,128)(2,1)}), bf16[2,256,1024]{2,1,0:T(8,128)(2,1)}) %reduce-scatter.15.cloned.1.call-update) | async-done | bytes 1048592 | tf_op jit(solution)/shard_map/reduce_scatter | solution.py:256
  561.1 75.5 %reduce-scatter.17.cloned.1.call-done = bf16[2,256,1024]{2,1,0:T(8,128)(2,1)} async-done(((bf16[2,1024,1024]{2,1,0:T(8,128)(2,1)}), bf16[2,256,1024]{2,1,0:T(8,128)(2,1)}) %reduce-scatter.17.cloned.1.call-update) | async-done | bytes 1048592 | tf_op jit(solution)/shard_map/reduce_scatter | solution.py:259
  642.2 9.2 convolution_convert_fusion.1
  651.4 30.1 %reduce-scatter.19.cloned.1.call-done = bf16[128,1024]{1,0:T(8,128)(2,1)} async-done(((bf16[1024,1024]{1,0:T(8,128)(2,1)}), bf16[128,1024]{1,0:T(8,128)(2,1)}) %reduce-scatter.19.cloned.1.call-update) | async-done | bytes 262160 | tf_op jit(solution)/shard_map/reduce_scatter | solution.py:304
  681.5 44.7 %reduce-scatter.31.cloned.1.call-done = bf16[128,1024]{1,0:T(8,128)(2,1)} async-done(((bf16[1024,1024]{1,0:T(8,128)(2,1)}), bf16[128,1024]{1,0:T(8,128)(2,1)}) %reduce-scatter.31.cloned.1.call-update) | async-done | bytes 262160 | tf_op jit(solution)/shard_map/reduce_scatter | solution.py:313
  726.3 13.4 %convolution_convert_fusion = bf16[4096,1024]{1,0:T(8,128)(2,1)} fusion(bf16[512,1024]{1,0:T(8,128)(2,1)S(1)} %bitcast.353, f32[512,4096]{1,0:T(8,128)} %fusion.80, f32[4096]{0:T(1024)S(1)} %convert_element_type.206), kind=kOutput, calls=%fused_computation.76 | convolution fusion | flops 4320133120 | bytes 17842176 | tf_op jit(solution)/shard_map/tf,td->fd/dot_general | solution.py:218
  739.8 31.0 %reduce-scatter.23.cloned.1.call-done = bf16[128,1024]{1,0:T(8,128)(2,1)} async-done(((bf16[1024,1024]{1,0:T(8,128)(2,1)}), bf16[128,1024]{1,0:T(8,128)(2,1)}) %reduce-scatter.23.cloned.1.call-update) | async-done | bytes 262160 | tf_op jit(solution)/shard_map/reduce_scatter | solution.py:307
  770.9 44.8 %reduce-scatter.27.cloned.1.call-done = bf16[128,1024]{1,0:T(8,128)(2,1)} async-done(((bf16[1024,1024]{1,0:T(8,128)(2,1)}), bf16[128,1024]{1,0:T(8,128)(2,1)}) %reduce-scatter.27.cloned.1.call-update) | async-done | bytes 262160 | tf_op jit(solution)/shard_map/reduce_scatter | solution.py:310
  816.0 74.5 %reduce-scatter.35.cloned.1.call-done = bf16[128,4096]{1,0:T(8,128)(2,1)} async-done(((bf16[1024,4096]{1,0:T(8,128)(2,1)}), bf16[128,4096]{1,0:T(8,128)(2,1)}) %reduce-scatter.35.cloned.1.call-update) | async-done | bytes 1048592 | tf_op jit(solution)/shard_map/reduce_scatter | solution.py:316
  890.8 12.9 %add_convert_fusion = bf16[512,1024]{1,0:T(8,128)(2,1)} fusion(f32[512,1024]{1,0:T(8,128)} %copy-done.11, bf16[4096,1024]{1,0:T(8,128)(2,1)} %param.48, f32[1024]{0:T(1024)S(1)} %convert_element_type.208, f32[512,4096]{1,0:T(8,128)} %fusion.80, f32[4096]{0:T(1024)S(1)} %convert_element_type.206), kind=kOutput, calls=%fused_computation.134 | convolution fusion | flops 4317511680 | bytes 19943424 | tf_op jit(solution)/shard_map/dot_general | solution.py:212
  913.9 18.6 %reduce-scatter.33.cloned.1.call-done = bf16[128,256]{1,0:T(8,128)(2,1)} async-done(((bf16[128,1024]{1,0:T(8,128)(2,1)}), bf16[128,256]{1,0:T(8,128)(2,1)}) %reduce-scatter.33.cloned.1.call-update) | async-done | bytes 65552 | tf_op jit(solution)/shard_map/reduce_scatter | solution.py:333
  940.3 65.5 %reduce-scatter.39.cloned.1.call-done = bf16[512,1024]{1,0:T(8,128)(2,1)} async-done(((bf16[4096,1024]{1,0:T(8,128)(2,1)}), bf16[512,1024]{1,0:T(8,128)(2,1)}) %reduce-scatter.39.cloned.1.call-update) | async-done | bytes 1048592 | tf_op jit(solution)/shard_map/reduce_scatter | solution.py:319
  1013.9 41.1 %all-reduce = (f32[1024]{0:T(1024)S(1)}, f32[1024]{0:T(1024)S(1)}, f32[1024]{0:T(1024)}, f32[1024]{0:T(1024)}, f32[1024]{0:T(1024)}, /*index=5*/f32[1024]{0:T(10...) all-reduce(f32[1024]{0:T(1024)S(1)} %get-tuple-element.411, ...), channel_id=1, replica_groups=mesh['items'=8,'band'=4] {'items','band'}, use_global_device_ids=true, to_apply=%region_33.34 | all-reduce | flops 14336 | bytes 114688 | tf_op jit(solution)/shard_map/psum | solution.py:279
  1061.4 14.2 %reduce-scatter.37.cloned.1.call-done = bf16[128,1024]{1,0:T(8,128)(2,1)} async-done(((bf16[128,4096]{1,0:T(8,128)(2,1)}), bf16[128,1024]{1,0:T(8,128)(2,1)}) %reduce-scatter.37.cloned.1.call-update) | async-done | bytes 262160 | tf_op jit(solution)/shard_map/reduce_scatter | solution.py:336
  1077.4 26.3 %reduce-scatter.41.cloned.1.call-done = bf16[512,256]{1,0:T(8,128)(2,1)} async-done(((bf16[512,1024]{1,0:T(8,128)(2,1)}), bf16[512,256]{1,0:T(8,128)(2,1)}) %reduce-scatter.41.cloned.1.call-update) | async-done | bytes 262160 | tf_op jit(solution)/shard_map/reduce_scatter | solution.py:339
  (487 shorter events, 317.7 us)
Async XLA Ops:
  7.2 289.7 %copy-start = (bf16[1024,1024]{1,0:T(8,128)(2,1)S(1)}, bf16[1024,1024]{1,0:T(8,128)(2,1)}, u32[]{:S(2)}) copy-start(bf16[1024,1024]{1,0:T(8,128)(2,1)} %param.42) | copy-start | bytes 6291460
  7.2 140.1 %all-gather.3.cloned.1.call-start = ((), (), s32[]{:S(2)}) async-start(), calls=%async_computation.14 | async-start | bytes 5242880 | tf_op jit(solution)/shard_map/all_gather | solution.py:187
  56.2 953.9 %copy-start.31 = (f32[1024]{0:T(1024)}, f32[1024]{0:T(1024)S(1)}, u32[]{:S(2)}) copy-start(f32[1024]{0:T(1024)S(1)} %get-tuple-element.518) | copy-start | bytes 12292
  66.8 160.9 %all-gather.5.cloned.1.call-start = ((), (), s32[]{:S(2)}) async-start(), calls=%async_computation.15 | async-start | bytes 5242880 | tf_op jit(solution)/shard_map/all_gather | solution.py:186
  73.0 484.1 %reduce-scatter.15.cloned.1.call-start = ((), (), s32[]{:S(2)}) async-start(), calls=%async_computation.16 | async-start | bytes 5242880 | tf_op jit(solution)/shard_map/reduce_scatter | solution.py:256
  81.4 218.8 %copy-start.55 = (f32[1024]{0:T(1024)}, f32[1024]{0:T(1024)S(1)}, u32[]{:S(2)}) copy-start(f32[1024]{0:T(1024)S(1)} %convert_element_type.204) | copy-start | bytes 12292
  481.9 154.6 %reduce-scatter.17.cloned.1.call-start = ((), (), s32[]{:S(2)}) async-start(), calls=%async_computation.17 | async-start | bytes 5242880 | tf_op jit(solution)/shard_map/reduce_scatter | solution.py:259
  492.8 188.6 %reduce-scatter.19.cloned.1.call-start = ((), (), s32[]{:S(2)}) async-start(), calls=%async_computation.18 | async-start | bytes 2359296 | tf_op jit(solution)/shard_map/reduce_scatter | solution.py:304
  497.0 229.2 %reduce-scatter.31.cloned.1.call-start = ((), (), s32[]{:S(2)}) async-start(), calls=%async_computation.24 | async-start | bytes 2359296 | tf_op jit(solution)/shard_map/reduce_scatter | solution.py:313
  502.5 268.3 %reduce-scatter.23.cloned.1.call-start = ((), (), s32[]{:S(2)}) async-start(), calls=%async_computation.20 | async-start | bytes 2359296 | tf_op jit(solution)/shard_map/reduce_scatter | solution.py:307
  561.0 254.7 %reduce-scatter.27.cloned.1.call-start = ((), (), s32[]{:S(2)}) async-start(), calls=%async_computation.22 | async-start | bytes 2359296 | tf_op jit(solution)/shard_map/reduce_scatter | solution.py:310
  640.6 249.9 %reduce-scatter.35.cloned.1.call-start = ((), (), s32[]{:S(2)}) async-start(), calls=%async_computation.26 | async-start | bytes 9437184 | tf_op jit(solution)/shard_map/reduce_scatter | solution.py:316
  651.3 75.0 %copy-start.9 = (bf16[2,256,1024]{2,1,0:T(8,128)(2,1)S(1)}, bf16[2,256,1024]{2,1,0:T(8,128)(2,1)}, u32[]{:S(2)}) copy-start(bf16[2,256,1024]{2,1,0:T(8,128)(2,1)} %param.30) | copy-start | bytes 3145732
  651.4 261.0 %reduce-scatter.21.cloned.1.call-start = ((), (), s32[]{:S(2)}) async-start(), calls=%async_computation.19 | async-start | bytes 327680 | tf_op jit(solution)/shard_map/reduce_scatter | solution.py:324
  681.5 251.0 %reduce-scatter.33.cloned.1.call-start = ((), (), s32[]{:S(2)}) async-start(), calls=%async_computation.25 | async-start | bytes 327680 | tf_op jit(solution)/shard_map/reduce_scatter | solution.py:333
  726.3 279.5 %reduce-scatter.39.cloned.1.call-start = ((), (), s32[]{:S(2)}) async-start(), calls=%async_computation.28 | async-start | bytes 9437184 | tf_op jit(solution)/shard_map/reduce_scatter | solution.py:319
  739.7 76.1 %copy-start.52 = (f32[1,2,2,128]{3,2,1,0:T(2,128)S(1)}, f32[1,2,2,128]{3,2,1,0:T(2,128)}, u32[]{:S(2)}) copy-start(f32[1,2,2,128]{3,2,1,0:T(2,128)} %get-tuple-element.558) | copy-start | bytes 6148
  739.7 76.1 %copy-start.64 = (bf16[1024]{0:T(1024)(128)(2,1)S(1)}, bf16[1024]{0:T(1024)(128)(2,1)}, u32[]{:S(2)}) copy-start(bf16[1024]{0:T(1024)(128)(2,1)} %param.49) | copy-start | bytes 6148
  739.7 318.7 %reduce-scatter.25.cloned.1.call-start = ((), (), s32[]{:S(2)}) async-start(), calls=%async_computation.21 | async-start | bytes 327680 | tf_op jit(solution)/shard_map/reduce_scatter | solution.py:327
  770.8 289.1 %reduce-scatter.29.cloned.1.call-start = ((), (), s32[]{:S(2)}) async-start(), calls=%async_computation.23 | async-start | bytes 327680 | tf_op jit(solution)/shard_map/reduce_scatter | solution.py:330
  815.7 259.9 %reduce-scatter.37.cloned.1.call-start = ((), (), s32[]{:S(2)}) async-start(), calls=%async_computation.27 | async-start | bytes 1310720 | tf_op jit(solution)/shard_map/reduce_scatter | solution.py:336
  890.5 213.2 %reduce-scatter.41.cloned.1.call-start = ((), (), s32[]{:S(2)}) async-start(), calls=%async_computation.29 | async-start | bytes 1310720 | tf_op jit(solution)/shard_map/reduce_scatter | solution.py:339
  940.3 67.1 %copy-start.43 = (f32[1,2,2,128]{3,1,2,0:T(2,128)S(1)}, f32[1,2,2,128]{3,1,2,0:T(2,128)}, u32[]{:S(2)}) copy-start(f32[1,2,2,128]{3,1,2,0:T(2,128)} %copy-done.42) | copy-start | bytes 6148
  940.3 67.1 %copy-start.37 = (f32[512]{0:T(512)S(1)}, f32[512]{0:T(512)}, u32[]{:S(2)}) copy-start(f32[512]{0:T(512)} %copy-done.36) | copy-start | bytes 6148
  (71 other events, 881.8 us)
Sparse Core Ops, SparseCore 0:
  66.9 80.3 all-gather.2
  148.9 78.7 all-gather.4
  482.0 74.9 reduce-scatter.14
  559.3 77.2 reduce-scatter.16
  639.7 41.7 reduce-scatter.18
  685.0 41.2 reduce-scatter.30
  729.5 41.2 reduce-scatter.22
  774.4 41.2 reduce-scatter.26
  819.2 71.2 reduce-scatter.34
  892.7 19.6 reduce-scatter.20
  914.7 17.8 reduce-scatter.32
  936.2 69.5 reduce-scatter.38
  1008.1 19.5 reduce-scatter.24
  1029.9 18.1 reduce-scatter.28
  1050.2 25.3 reduce-scatter.36
  1077.9 25.7 reduce-scatter.40
where the time goes:
time: 1120 us; the launch traced here: 1110 us
  waiting for transfers between devices  627 us (56%)
  matrix products  188 us (17%)
  local copies, waits for them, and re-layouts  131 us (12%)
  blocking collectives  83.3 us (7%)
  other arithmetic  53.6 us (5%)
  between operations  15.7 us (1%)
  loops' own time  11.5 us (1%)
    all_gather x1, waiting for transfers between devices, local(): lax.all_gather(key_local, 'band', axis=1, tiled=True)  75.7 us
    reduce_scatter x1, waiting for transfers between devices, local(): lax.psum_scatter(jnp.stack(d_v_list).astype(jnp.bfloat16), 'band', scatte...  75.5 us
    reduce_scatter x1, waiting for transfers between devices, local(): lax.psum_scatter(d_w_up.astype(jnp.bfloat16), 'items', scatter_dimension=...  74.5 us
    all_gather x1, waiting for transfers between devices, local(): lax.all_gather(value_local, 'band', axis=1, tiled=True)  65.8 us
    reduce_scatter x1, waiting for transfers between devices, local(): lax.psum_scatter(d_w_down.astype(jnp.bfloat16), 'items', scatter_dimensio...  65.5 us
    reduce_scatter x1, waiting for transfers between devices, local(): lax.psum_scatter(jnp.stack(d_k_list).astype(jnp.bfloat16), 'band', scatte...  54.5 us
    reduce_scatter x1, waiting for transfers between devices, local(): lax.psum_scatter(d_w_value.astype(jnp.bfloat16), 'items', scatter_dimensi...  44.8 us
    reduce_scatter x1, waiting for transfers between devices, local(): lax.psum_scatter(d_w_out.astype(jnp.bfloat16), 'items', scatter_dimension...  44.7 us
  transfers between devices with their start and end apart: 16, of which 14 were waited for; matrix products, arithmetic and copies ran while one was open for 10% of the time, Pallas kernels for 0%

commit v1 on v0

--- a/solution.py
+++ b/solution.py
@@ -1,16 +1,822 @@
+import functools
 import jax
 import jax.numpy as jnp
 from jax import lax
+from jax.experimental import pallas as pl
+from jax.experimental.pallas import tpu as pltpu
 from jax.sharding import PartitionSpec as P
 
 HEADS = 16
 HEAD_DIM = 64
-
-
 epsilon = 1e-05
 score_scale = 0.125
 masked_score = -1e30
 momentum = 0.5
+f32 = jnp.float32
+bf16 = jnp.bfloat16
+VMEM_LIMIT = 60 * 2**20
+
+
+def dot(a, b, ca=1, cb=0):
+    return lax.dot_general(a, b, (((ca,), (cb,)), ((), ())), preferred_element_type=f32)
+
+
+def params(**kw):
+    return pltpu.CompilerParams(vmem_limit_bytes=VMEM_LIMIT, **kw)
+
+
+def project_kernel(core, tok, mean, inv, gain, shift, wq, wk, wv, bq, bv, h1, q, k, v):
+    start = (tok[...].astype(f32) - mean[...]) * inv[...]
+    centre = start - jnp.mean(start, -1, keepdims=True)
+    spread = jnp.mean(centre * centre, -1, keepdims=True)
+    h = (centre * lax.rsqrt(spread + epsilon) * gain[...] + shift[...]).astype(bf16)
+    h1[...] = h
+    q[...] = ((dot(h, wq[...]) + bq[...]).astype(bf16) * score_scale).astype(bf16)
+    k[...] = dot(h, wk[...]).astype(bf16)
+    v[...] = (dot(h, wv[...]) + bv[...]).astype(bf16)
+
+
+def project(core, tok, mean, inv, gain, shift, wq, wk, wv, bq, bv, block=256):
+    rows, width = tok.shape
+    half = width // 2
+    row = lambda i, c: (i, 0)
+    one = lambda i, c: (0, 0)
+    mine = lambda i, c: (0, c[0])
+    vec = pl.BlockSpec((1, width), one)
+    w = pl.BlockSpec((width, half), mine)
+    bias = pl.BlockSpec((1, half), mine)
+    return pl.pallas_call(
+        project_kernel,
+        name="project",
+        grid_spec=pltpu.PrefetchScalarGridSpec(
+            num_scalar_prefetch=1,
+            grid=(rows // block,),
+            in_specs=[pl.BlockSpec((block, width), row), vec, vec, vec, vec, w, w, w, bias, bias],
+            out_specs=[pl.BlockSpec((block, width), row)] + [pl.BlockSpec((block, half), row)] * 3,
+        ),
+        out_shape=[jax.ShapeDtypeStruct((rows, width), bf16)]
+        + [jax.ShapeDtypeStruct((rows, half), bf16)] * 3,
+        compiler_params=params(),
+        cost_estimate=pl.CostEstimate(
+            flops=2 * rows * width * 3 * half, bytes_accessed=12 * 2**20, transcendentals=0
+        ),
+    )(core, tok, mean, inv, gain, shift, wq, wk, wv, bq, bv)
+
+
+def head_lanes(array, head, lane):
+    keep = (lane >= head * HEAD_DIM) & (lane < (head + 1) * HEAD_DIM)
+    return jnp.where(keep, array, jnp.zeros_like(array))
+
+
+def scores_keys(k_pair, bias, head, lane):
+    spare = (1 - head) * HEAD_DIM
+    return jnp.where(lane == spare, bias, head_lanes(k_pair, head, lane))
+
+
+def scores_queries(q_pair, head, lane):
+    spare = (1 - head) * HEAD_DIM
+    return jnp.where(lane == spare, jnp.ones_like(q_pair), head_lanes(q_pair, head, lane))
+
+
+def attend_kernel(qt, q, k, v, bias, out, log_total):
+    rows, lanes = q.shape
+    lane_k = lax.broadcasted_iota(jnp.int32, (rows, lanes), 1)
+    lane_q = lax.broadcasted_iota(jnp.int32, (qt, lanes), 1)
+    row_out = lax.broadcasted_iota(jnp.int32, (lanes, qt), 0)
+    keys = [scores_keys(k[...], bias[...], hd, lane_k) for hd in range(2)]
+    values = [scores_queries(v[...], hd, lane_k).T for hd in range(2)]
+    for t in range(rows // qt):
+        at = slice(t * qt, (t + 1) * qt)
+        scores = [dot(keys[hd], scores_queries(q[at, :], hd, lane_q), 1, 1) for hd in range(2)]
+        tops = [jnp.max(s, 0, keepdims=True) for s in scores]
+        weights = [jnp.exp(s - top).astype(bf16) for s, top in zip(scores, tops)]
+        parts = []
+        for hd in range(2):
+            part = dot(values[hd], weights[hd])
+            spare = (1 - hd) * HEAD_DIM
+            total = part[spare : spare + 1, :]
+            log_total[0, hd : hd + 1, at] = tops[hd] + jnp.log(total)
+            parts.append(part * (1.0 / total))
+        out[at, :] = jnp.where(row_out < HEAD_DIM, parts[0], parts[1]).T.astype(bf16)
+
+
+def attend(q, k, v, bias, qt=512):
+    rows, width = q.shape
+    pairs = width // 128
+    blk = pl.BlockSpec((rows, 128), lambda i: (0, i))
+    return pl.pallas_call(
+        functools.partial(attend_kernel, qt),
+        name="attend",
+        grid=(pairs,),
+        in_specs=[blk, blk, blk, pl.BlockSpec((rows, 128), lambda i: (0, 0))],
+        out_specs=[blk, pl.BlockSpec((1, 2, rows), lambda i: (i, 0, 0))],
+        out_shape=[
+            jax.ShapeDtypeStruct((rows, width), bf16),
+            jax.ShapeDtypeStruct((pairs, 2, rows), f32),
+        ],
+        compiler_params=params(),
+        cost_estimate=pl.CostEstimate(
+            flops=16 * rows * rows * width, bytes_accessed=5 * 2**20, transcendentals=0
+        ),
+    )(q, k, v, bias)
+
+
+def attend_back_kernel(qt, q, k, v, bias, d_attn, log_total, dq, dk, dv, dk_acc, dv_acc):
+    rows, lanes = q.shape
+    lane_k = lax.broadcasted_iota(jnp.int32, (rows, lanes), 1)
+    lane_q = lax.broadcasted_iota(jnp.int32, (qt, lanes), 1)
+    keys = [scores_keys(k[...], bias[...], hd, lane_k) for hd in range(2)]
+    keys_only = [head_lanes(k[...], hd, lane_k) for hd in range(2)]
+    values = [head_lanes(v[...], hd, lane_k) for hd in range(2)]
+    for t in range(rows // qt):
+        at = slice(t * qt, (t + 1) * qt)
+        q_tile = q[at, :]
+        d_tile = d_attn[at, :]
+        dq_both = None
+        for hd in range(2):
+            q_head = head_lanes(q_tile, hd, lane_q)
+            d_head = head_lanes(d_tile, hd, lane_q)
+            s = dot(keys[hd], scores_queries(q_tile, hd, lane_q), 1, 1)
+            p = jnp.exp(s - log_total[0, hd : hd + 1, at])
+            d_p = dot(values[hd], d_tile, 1, 1)
+            weighted = p * d_p
+            delta = jnp.sum(weighted, 0, keepdims=True)
+            ds = (weighted - p * delta).astype(bf16)
+            dv_part = dot(p.astype(bf16), d_head)
+            dk_part = dot(ds, q_head)
+            if t == 0 and hd == 0:
+                dv_acc[...] = dv_part
+                dk_acc[...] = dk_part
+            else:
+                dv_acc[...] += dv_part
+                dk_acc[...] += dk_part
+            part = dot(keys_only[hd], ds, 0, 0)
+            dq_both = part if dq_both is None else dq_both + part
+        dq[at, :] = (dq_both.T * score_scale).astype(bf16)
+    dk[...] = dk_acc[...].astype(bf16)
+    dv[...] = dv_acc[...].astype(bf16)
+
+
+def attend_back(q, k, v, bias, d_attn, log_total, qt=512):
+    rows, width = q.shape
+    pairs = width // 128
+    blk = pl.BlockSpec((rows, 128), lambda i: (0, i))
+    return pl.pallas_call(
+        functools.partial(attend_back_kernel, qt),
+        name="attend_back",
+        grid=(pairs,),
+        in_specs=[
+            blk,
+            blk,
+            blk,
+            pl.BlockSpec((rows, 128), lambda i: (0, 0)),
+            blk,
+            pl.BlockSpec((1, 2, rows), lambda i: (i, 0, 0)),
+        ],
+        out_specs=[blk] * 3,
+        out_shape=[jax.ShapeDtypeStruct((rows, width), bf16)] * 3,
+        scratch_shapes=[pltpu.VMEM((rows, 128), f32)] * 2,
+        compiler_params=params(),
+        cost_estimate=pl.CostEstimate(
+            flops=40 * rows * rows * width, bytes_accessed=8 * 2**20, transcendentals=0
+        ),
+    )(q, k, v, bias, d_attn, log_total)
+
+
+def gelu_and_slope(u):
+    u2 = u * u
+    t = jnp.tanh(u * (0.7978845608028654 + (0.7978845608028654 * 0.044715) * u2))
+    half = 0.5 + 0.5 * t
+    slope = half * (
+        1.0 + u * (1.0 - t) * (0.7978845608028654 + (3 * 0.7978845608028654 * 0.044715) * u2)
+    )
+    return u * half, slope
+
+
+def mlp_kernel(core, h2, h2p, cot, out_in, dh_in, *refs):
+    (wu_a, bu_a, wd_a, wu_b, bu_b, wd_b) = refs[:6]
+    (out, dh, dwd_a, dwu_ak, dwu_as, dbu_a, dwd_b, dwu_bk, dwu_bs, dbu_b) = refs[6:]
+    step = pl.program_id(0)
+    half = h2.shape[1] // 2
+
+    @pl.when(step == 0)
+    def _():
+        out[...] = out_in[...]
+        dh[...] = dh_in[...]
+
+    for wu, bu, wd, dwd, dwu_k, dwu_s, dbu in (
+        (wu_a, bu_a, wd_a, dwd_a, dwu_ak, dwu_as, dbu_a),
+        (wu_b, bu_b, wd_b, dwd_b, dwu_bk, dwu_bs, dbu_b),
+    ):
+        up = dot(h2[...], wu[...]) + bu[...]
+        d_act = dot(cot[...], wd[...], 1, 1)
+        act, slope = gelu_and_slope(up)
+        act = act.astype(bf16)
+        d_up32 = d_act * slope
+        d_up = d_up32.astype(bf16)
+        dbu[0] = jnp.sum(d_up32, 0, keepdims=True)
+        dwd[0] = dot(cot[...], act, 0, 0).astype(bf16)
+        d_wu = dot(h2p[...], d_up, 0, 0).astype(bf16)
+        dwu_k[0] = d_wu[:half]
+        dwu_s[0] = d_wu[half:]
+        out[...] += dot(act, wd[...])
+        dh[...] += dot(d_up, wu[...], 1, 1)
+
+
+def mlp(core, h2, h2p, cot, out_in, dh_in, w_up, b_up, w_down, first, steps):
+    rows, width = h2.shape
+    ff = w_up.shape[1]
+    tile = ff // 8
+    half = width // 2
+    whole = pl.BlockSpec((rows, width), lambda i, c: (0, 0))
+    at_a = lambda i, c: 2 * (first + i) + 1 - c[0]
+    at_b = lambda i, c: 2 * (first + i) + c[0]
+    w_specs = []
+    for at in (at_a, at_b):
+        w_specs += [
+            pl.BlockSpec((width, tile), lambda i, c, at=at: (0, at(i, c))),
+            pl.BlockSpec((1, tile), lambda i, c, at=at: (0, at(i, c))),
+            pl.BlockSpec((tile, width), lambda i, c, at=at: (at(i, c), 0)),
+        ]
+    out_specs = [whole, whole]
+    out_shape = [jax.ShapeDtypeStruct((rows, width), f32)] * 2
+    for _ in range(2):
+        out_specs += [
+            pl.BlockSpec((1, width, tile), lambda i, c: (i, 0, 0)),
+            pl.BlockSpec((1, half, tile), lambda i, c: (i, 0, 0)),
+            pl.BlockSpec((1, half, tile), lambda i, c: (i, 0, 0)),
+            pl.BlockSpec((1, 1, tile), lambda i, c: (i, 0, 0)),
+        ]
+        out_shape += [
+            jax.ShapeDtypeStruct((steps, width, tile), bf16),
+            jax.ShapeDtypeStruct((steps, half, tile), bf16),
+            jax.ShapeDtypeStruct((steps, half, tile), bf16),
+            jax.ShapeDtypeStruct((steps, 1, tile), f32),
+        ]
+    return pl.pallas_call(
+        mlp_kernel,
+        name="mlp",
+        grid_spec=pltpu.PrefetchScalarGridSpec(
+            num_scalar_prefetch=1,
+            grid=(steps,),
+            in_specs=[whole] * 5 + w_specs,
+            out_specs=out_specs,
+        ),
+        out_shape=out_shape,
+        compiler_params=params(),
+        cost_estimate=pl.CostEstimate(
+            flops=2 * 6 * rows * width * 2 * tile * steps, bytes_accessed=20 * 2**20, transcendentals=0
+        ),
+    )(core, h2, h2p, cot, out_in, dh_in, w_up, b_up, w_down, w_up, b_up, w_down)
+
+
+def all_sum_kernel(n_items, n_band, x, total, buf_i, buf_b, part, send_i, recv_i, send_b, recv_b):
+    it = lax.axis_index("items")
+    bd = lax.axis_index("band")
+    barrier = pltpu.get_barrier_semaphore()
+    for o in range(1, n_items):
+        peer = (lax.rem(it + o, n_items), bd)
+        pl.semaphore_signal(barrier, inc=1, device_id=peer, device_id_type=pl.DeviceIdType.MESH)
+    for o in range(1, n_band):
+        peer = (it, lax.rem(bd + o, n_band))
+        pl.semaphore_signal(barrier, inc=1, device_id=peer, device_id_type=pl.DeviceIdType.MESH)
+    pl.semaphore_wait(barrier, n_items + n_band - 2)
+
+    def share(n, rank, peer_of, src, buf, send, recv):
+        copies = []
+        for o in range(1, n):
+            copy = pltpu.make_async_remote_copy(
+                src_ref=src,
+                dst_ref=buf.at[rank],
+                send_sem=send.at[o],
+                recv_sem=recv.at[o],
+                device_id=peer_of(lax.rem(rank + o, n)),
+                device_id_type=pl.DeviceIdType.MESH,
+            )
+            copy.start()
+            copies.append(copy)
+        buf[rank] = src[...]
+        for copy in copies:
+            copy.wait()
+        added = buf[0]
+        for i in range(1, n):
+            added = added + buf[i]
+        return added
+
+    part[...] = share(n_items, it, lambda p: (p, bd), x, buf_i, send_i, recv_i)
+    total[...] = share(n_band, bd, lambda p: (it, p), part, buf_b, send_b, recv_b)
+
+
+def all_sum(x, collective_id):
+    n_items, n_band = lax.axis_size("items"), lax.axis_size("band")
+    vmem = pl.BlockSpec(memory_space=pltpu.VMEM)
+    return pl.pallas_call(
+        functools.partial(all_sum_kernel, n_items, n_band),
+        name=f"all_sum_{collective_id}",
+        out_shape=jax.ShapeDtypeStruct(x.shape, f32),
+        in_specs=[vmem],
+        out_specs=vmem,
+        scratch_shapes=[
+            pltpu.VMEM((n_items,) + x.shape, f32),
+            pltpu.VMEM((n_band,) + x.shape, f32),
+            pltpu.VMEM(x.shape, f32),
+            pltpu.SemaphoreType.DMA((n_items,)),
+            pltpu.SemaphoreType.DMA((n_items,)),
+            pltpu.SemaphoreType.DMA((n_band,)),
+            pltpu.SemaphoreType.DMA((n_band,)),
+        ],
+        compiler_params=params(collective_id=collective_id, has_side_effects=True),
+    )(x)
+
+
+def stats_kernel(left, tok, sums):
+    slots, rows, width = tok.shape
+    row = lax.broadcasted_iota(jnp.int32, (rows, width), 0)
+    one = jnp.zeros((1, width), f32)
+    two = jnp.zeros((1, width), f32)
+    for s in range(slots):
+        x = jnp.where(row < left[s], tok[s].astype(f32), 0.0)
+        one = one + jnp.sum(x, 0, keepdims=True)
+        two = two + jnp.sum(x * x, 0, keepdims=True)
+    sums[0:1, :] = one
+    sums[1:2, :] = two
+
+
+def stats(left, tok):
+    width = tok.shape[2]
+    vmem = pl.BlockSpec(memory_space=pltpu.VMEM)
+    return pl.pallas_call(
+        stats_kernel,
+        name="stats",
+        in_specs=[pl.BlockSpec(memory_space=pltpu.SMEM), vmem],
+        out_specs=vmem,
+        out_shape=jax.ShapeDtypeStruct((2, width), f32),
+        compiler_params=params(),
+    )(left, tok)
+
+
+def join_kernel(core, attn_a, attn_b, wo_a, wo_b, tok, mean, inv, bo, gain, shift, res, h2, h2p):
+    start = (tok[...].astype(f32) - mean[...]) * inv[...]
+    r = start + (dot(attn_a[...], wo_a[...]) + dot(attn_b[...], wo_b[...])) + bo[...]
+    res[...] = r
+    centre = r - jnp.mean(r, -1, keepdims=True)
+    spread = jnp.mean(centre * centre, -1, keepdims=True)
+    h = (centre * lax.rsqrt(spread + epsilon) * gain[...] + shift[...]).astype(bf16)
+    h2[...] = h
+    half = h.shape[1] // 2
+    width = h.shape[1] // 8
+    even = core[0] == 0
+    for x in range(4):
+        first = h[:, 2 * x * width : (2 * x + 1) * width]
+        second = h[:, (2 * x + 1) * width : (2 * x + 2) * width]
+        h2p[:, x * width : (x + 1) * width] = jnp.where(even, first, second)
+        h2p[:, half + x * width : half + (x + 1) * width] = jnp.where(even, second, first)
+
+
+def join(core, attn, attn_recv, w_out, tok, mean, inv, bo, gain, shift, block=256):
+    rows, half = attn_recv.shape
+    width = 2 * half
+    row = lambda i, c: (i, 0)
+    one = lambda i, c: (0, 0)
+    vec = pl.BlockSpec((1, width), one)
+    act = pl.BlockSpec((block, half), row)
+    full = pl.BlockSpec((block, width), row)
+    return pl.pallas_call(
+        join_kernel,
+        name="join",
+        grid_spec=pltpu.PrefetchScalarGridSpec(
+            num_scalar_prefetch=1,
+            grid=(rows // block,),
+            in_specs=[
+                act,
+                act,
+                pl.BlockSpec((half, width), lambda i, c: (c[0], 0)),
+                pl.BlockSpec((half, width), lambda i, c: (1 - c[0], 0)),
+                full,
+                vec,
+                vec,
+                vec,
+                vec,
+                vec,
+            ],
+            out_specs=[full] * 3,
+        ),
+        out_shape=[
+            jax.ShapeDtypeStruct((rows, width), f32),
+            jax.ShapeDtypeStruct((rows, width), bf16),
+            jax.ShapeDtypeStruct((rows, width), bf16),
+        ],
+        compiler_params=params(),
+        cost_estimate=pl.CostEstimate(
+            flops=2 * rows * width * width, bytes_accessed=8 * 2**20, transcendentals=0
+        ),
+    )(core, attn, attn_recv, w_out, w_out, tok, mean, inv, bo, gain, shift)
+
+
+def unjoin_kernel(
+    core, res, dh, cot, gain, attn_a, attn_b, wo_a, wo_b, d_res, da_a, da_b, dwo_a, dwo_b, sums, acc_a, acc_b
+):
+    step = pl.program_id(0)
+    last = pl.num_programs(0) - 1
+    r = res[...]
+    centre = r - jnp.mean(r, -1, keepdims=True)
+    spread = jnp.mean(centre * centre, -1, keepdims=True)
+    scale = lax.rsqrt(spread + epsilon)
+    z = centre * scale
+    d_h = dh[...]
+    dz = d_h * gain[...]
+    dv = scale * (dz - jnp.mean(dz, -1, keepdims=True) - z * jnp.mean(dz * z, -1, keepdims=True))
+    c32 = cot[...].astype(f32)
+    full = c32 + dv
+    d_res[...] = full
+    low = full.astype(bf16)
+    add_rows(step, sums, (d_h * z, d_h, low.astype(f32), c32))
+    da_a[...] = dot(low, wo_a[...], 1, 1).astype(bf16)
+    da_b[...] = dot(low, wo_b[...], 1, 1).astype(bf16)
+    part_a = dot(attn_a[...], low, 0, 0)
+    part_b = dot(attn_b[...], low, 0, 0)
+
+    @pl.when(step == 0)
+    def _():
+        acc_a[...] = part_a
+        acc_b[...] = part_b
+
+    @pl.when(step > 0)
+    def _():
+        acc_a[...] += part_a
+        acc_b[...] += part_b
+
+    @pl.when(step == last)
+    def _():
+        dwo_a[...] = acc_a[...].astype(bf16)
+        dwo_b[...] = acc_b[...].astype(bf16)
+
+
+def add_rows(step, sums, arrays):
+    for i, a in enumerate(arrays):
+        total = jnp.sum(a, 0, keepdims=True)
+
+        @pl.when(step == 0)
+        def _():
+            sums[i : i + 1, :] = total
+
+        @pl.when(step > 0)
+        def _():
+            sums[i : i + 1, :] += total
+
+
+def unjoin(core, res, dh, cot, gain, attn, attn_recv, w_out, block=256):
+    rows, half = attn_recv.shape
+    width = 2 * half
+    row = lambda i, c: (i, 0)
+    one = lambda i, c: (0, 0)
+    act = pl.BlockSpec((block, half), row)
+    full = pl.BlockSpec((block, width), row)
+    grad = pl.BlockSpec((half, width), one)
+    return pl.pallas_call(
+        unjoin_kernel,
+        name="unjoin",
+        grid_spec=pltpu.PrefetchScalarGridSpec(
+            num_scalar_prefetch=1,
+            grid=(rows // block,),
+            in_specs=[
+                full,
+                full,
+                full,
+                pl.BlockSpec((1, width), one),
+                act,
+                act,
+                pl.BlockSpec((half, width), lambda i, c: (c[0], 0)),
+                pl.BlockSpec((half, width), lambda i, c: (1 - c[0], 0)),
+            ],
+            out_specs=[full, act, act, grad, grad, pl.BlockSpec((4, width), one)],
+            scratch_shapes=[pltpu.VMEM((half, width), f32)] * 2,
+        ),
+        out_shape=[
+            jax.ShapeDtypeStruct((rows, width), f32),
+            jax.ShapeDtypeStruct((rows, half), bf16),
+            jax.ShapeDtypeStruct((rows, half), bf16),
+            jax.ShapeDtypeStruct((half, width), bf16),
+            jax.ShapeDtypeStruct((half, width), bf16),
+            jax.ShapeDtypeStruct((4, width), f32),
+        ],
+        compiler_params=params(),
+        cost_estimate=pl.CostEstimate(
+            flops=4 * rows * width * width, bytes_accessed=12 * 2**20, transcendentals=0
+        ),
+    )(core, res, dh, cot, gain, attn, attn_recv, w_out, w_out)
+
+
+def unproject_kernel(core, h1, dq, dk, dv, dq_r, dk_r, dv_r, wq, wk, wv, dw, dh, sums):
+    step = pl.program_id(0)
+    for i, d in enumerate((dq, dk, dv)):
+        dw[i] = dot(h1[...], d[...], 0, 0).astype(bf16)
+    total = dot(dq_r[...], wq[...], 1, 1)
+    total = total + dot(dk_r[...], wk[...], 1, 1)
+    total = total + dot(dv_r[...], wv[...], 1, 1)
+    dh[...] = total.astype(bf16)
+
+    @pl.when(step == 0)
+    def _():
+        sums[0:1, :] = jnp.sum(dq[...].astype(f32), 0, keepdims=True)
+        sums[1:2, :] = jnp.sum(dv[...].astype(f32), 0, keepdims=True)
+
+
+def unproject(core, h1, dq, dk, dv, wq, wk, wv, blocks=4):
+    rows, width = h1.shape
+    half = width // 2
+    rb, cb = rows // blocks, width // blocks
+    one = lambda i, c: (0, 0)
+    whole = pl.BlockSpec((rows, half), one)
+    part = pl.BlockSpec((rb, half), lambda i, c: (i, 0))
+    w = pl.BlockSpec((width, half), lambda i, c: (0, c[0]))
+    return pl.pallas_call(
+        unproject_kernel,
+        name="unproject",
+        grid_spec=pltpu.PrefetchScalarGridSpec(
+            num_scalar_prefetch=1,
+            grid=(blocks,),
+            in_specs=[pl.BlockSpec((rows, cb), lambda i, c: (0, i))]
+            + [whole] * 3
+            + [part] * 3
+            + [w] * 3,
+            out_specs=[
+                pl.BlockSpec((3, cb, half), lambda i, c: (0, i, 0)),
+                pl.BlockSpec((rb, width), lambda i, c: (i, 0)),
+                pl.BlockSpec((2, half), one),
+            ],
+        ),
+        out_shape=[
+            jax.ShapeDtypeStruct((3, width, half), bf16),
+            jax.ShapeDtypeStruct((rows, width), bf16),
+            jax.ShapeDtypeStruct((2, half), f32),
+        ],
+        compiler_params=params(),
+        cost_estimate=pl.CostEstimate(
+            flops=12 * rows * width * half, bytes_accessed=14 * 2**20, transcendentals=0
+        ),
+    )(core, h1, dq, dk, dv, dq, dk, dv, wq, wk, wv)
+
+
+def start_back_kernel(tok, mean, inv, gain, dh_a, dh_b, d_res, g_out, sums):
+    step = pl.program_id(0)
+    centred = tok[...].astype(f32) - mean[...]
+    start = centred * inv[...]
+    centre = start - jnp.mean(start, -1, keepdims=True)
+    spread = jnp.mean(centre * centre, -1, keepdims=True)
+    scale = lax.rsqrt(spread + epsilon)
+    z = centre * scale
+    d_h = dh_a[...].astype(f32) + dh_b[...].astype(f32)
+    dz = d_h * gain[...]
+    dv = scale * (dz - jnp.mean(dz, -1, keepdims=True) - z * jnp.mean(dz * z, -1, keepdims=True))
+    d_start = d_res[...] + dv
+    g_out[...] = (d_start * inv[...]).astype(bf16)
+    add_rows(step, sums, (d_start, d_start * centred, d_h * z, d_h))
+
+
+def start_back(tok, mean, inv, gain, dh, dh_recv, d_res, block=256):
+    rows, width = d_res.shape
+    full = pl.BlockSpec((block, width), lambda i: (i, 0))
+    vec = pl.BlockSpec((1, width), lambda i: (0, 0))
+    return pl.pallas_call(
+        start_back_kernel,
+        name="start_back",
+        grid=(rows // block,),
+        in_specs=[full, vec, vec, vec, full, full, full],
+        out_specs=[full, pl.BlockSpec((4, width), lambda i: (0, 0))],
+        out_shape=[
+            jax.ShapeDtypeStruct((rows, width), bf16),
+            jax.ShapeDtypeStruct((4, width), f32),
+        ],
+        compiler_params=params(),
+        cost_estimate=pl.CostEstimate(flops=2**22, bytes_accessed=8 * 2**20, transcendentals=0),
+    )(tok, mean, inv, gain, dh, dh_recv, d_res)
+
+
+def pick(array, index, axis=0):
+    return lax.dynamic_index_in_dim(array, index, axis, keepdims=False)
+
+
+def column_layer(
+    tokens, cotangent, running_mean, running_var, slot_table, patch_counts,
+    ln1_gain, ln1_bias, w_query, b_query, w_key, w_value, b_value, w_out, b_out,
+    ln2_gain, ln2_bias, w_up, b_up, w_down, b_down,
+):
+    n_items, n_band = lax.axis_size("items"), lax.axis_size("band")
+    slots, band_rows, width = tokens.shape
+    cut = band_rows // 2
+    it = lax.axis_index("items")
+    bd = lax.axis_index("band")
+    c, yx = lax.rem(it, 2), it // 2
+    x, y = lax.rem(yx, 2), yx // 2
+    core = c.astype(jnp.int32).reshape(1)
+    devices = [(i, b) for i in range(n_items) for b in range(n_band)]
+
+    def permute(array, to):
+        pairs = []
+        for i, b in devices:
+            j, d = to(i, b)
+            pairs.append((i * n_band + b, j * n_band + d))
+        return lax.ppermute(array, ("items", "band"), pairs)
+
+    to_core = lambda i, b: (i ^ 1, b)
+    to_x = lambda i, b: (i ^ 2, b)
+    to_y = lambda i, b: (i ^ 4, b)
+    to_z1 = lambda i, b: (i, b ^ 1)
+    to_z2 = lambda i, b: (i, b ^ 2)
+
+    def out_round(r):
+        def to(i, b):
+            q = b ^ r
+            return ((i // 2) * 2 + (q & 1), 2 * (i % 2) + (q >> 1))
+
+        return to
+
+    def back_round(r):
+        there = {out_round(r)(i, b): (i, b) for i, b in devices}
+        return lambda i, b: there[(i, b)]
+
+    def gather_rows(array):
+        blocks = array.reshape(slots * 2, cut, width)
+        return [permute(pick(blocks, bd ^ r), out_round(r)) for r in range(4)]
+
+    def return_rows(rows):
+        blocks = rows.reshape(4, cut, width)
+        got = jnp.stack([permute(blocks[r], back_round(r)) for r in range(4)])
+        return jnp.stack([pick(got, bd ^ q) for q in range(4)]).reshape(slots, band_rows, width)
+
+    counts = patch_counts[slot_table]
+    my_counts = lax.dynamic_slice_in_dim(counts, it * slots, slots)
+    left = my_counts - bd * band_rows
+    item_count = pick(counts, yx * 4 + bd)
+
+    tok_rows = jnp.concatenate(gather_rows(tokens))
+    sums = all_sum(stats(left, tokens), 1)
+    tok_sib = permute(tok_rows, to_core)
+    cot_rows = jnp.concatenate(gather_rows(cotangent))
+
+    patch_total = jnp.sum(patch_counts).astype(f32)
+    batch_mean = sums[0] / patch_total
+    batch_var = sums[1] / patch_total - batch_mean * batch_mean
+    new_mean = momentum * running_mean + momentum * batch_mean
+    new_var = momentum * running_var + momentum * batch_var
+    inverse = lax.rsqrt(new_var + epsilon)
+    mean_row, inv_row = new_mean.reshape(1, -1), inverse.reshape(1, -1)
+    as_row = lambda a: a.astype(f32).reshape(1, -1)
+
+    round_of = jnp.arange(4 * cut, dtype=jnp.int32) // cut
+    at = jnp.arange(4 * cut, dtype=jnp.int32) % cut
+    base = 2 * lax.rem(bd, 2)
+    own = ((base + c) ^ round_of) * band_rows + c * cut + at
+    sib = ((base + 1 - c) ^ round_of) * band_rows + (1 - c) * cut + at
+    bias = jnp.where(jnp.concatenate([own, sib]) < item_count, 0.0, masked_score).astype(bf16)
+    bias = jnp.broadcast_to(bias[:, None], (8 * cut, 128))
+
+    tok = jnp.concatenate([tok_rows, tok_sib])
+    h1, q, k, v = project(
+        core, tok, mean_row, inv_row, as_row(ln1_gain), as_row(ln1_bias),
+        w_query, w_key, w_value, as_row(b_query), as_row(b_value),
+    )
+    attn, log_total = attend(q, k, v, bias)
+    rows = 4 * cut
+    attn_recv = permute(attn[rows:], to_core)
+    res, h2, h2p = join(
+        core, attn, attn_recv, w_out, tok, mean_row, inv_row, as_row(b_out), as_row(ln2_gain), as_row(ln2_bias)
+    )
+    up_bias = as_row(b_up)
+    zero = jnp.zeros_like(res)
+    d_down_part, d_up_part, d_bias_up = [], [], []
+    total, d_h2 = res, zero
+    for j in range(2):
+        (total, d_h2, dwd_a, dwu_ak, dwu_as, dbu_a, dwd_b, dwu_bk, dwu_bs, dbu_b) = mlp(
+            core, h2, h2p, cot_rows, total, d_h2, w_up, up_bias, w_down, 2 * j, 2
+        )
+        d_down = (dwd_b, permute(dwd_a, to_core))
+        got_a, got_b = permute(dwu_as, to_core), permute(dwu_bs, to_core)
+        d_up = (jnp.stack([dwu_ak, dwu_bk]), jnp.stack([got_b, got_a]))
+        d_bias_up.append(jnp.stack([dbu_a, dbu_b]))
+        send = pick(d_down[0], 1 - x) + pick(d_down[1], 1 - x)
+        keep = pick(d_down[0], x) + pick(d_down[1], x)
+        d_down_part.append((keep, permute(send, to_x)))
+        d_up = [a.reshape(2, 2, 2, 2, -1, a.shape[-1]) for a in d_up]
+        send = pick(d_up[0], 1 - y, 2) + pick(d_up[1], 1 - y, 2)
+        keep = pick(d_up[0], y, 2) + pick(d_up[1], y, 2)
+        got = permute(send, to_y)
+        send = pick(keep, 1 - x, 2) + pick(got, 1 - x, 2)
+        keep = pick(keep, x, 2) + pick(got, x, 2)
+        got = permute(send, to_x)
+        b_low = lax.rem(bd, 2)
+        send = pick(keep, 1 - b_low, 1) + pick(got, 1 - b_low, 1)
+        keep = pick(keep, b_low, 1) + pick(got, b_low, 1)
+        d_up_part.append((keep, permute(send, to_z1)))
+    b_low, b_high = lax.rem(bd, 2), bd // 2
+
+    def add(pair):
+        return pair[0] + pair[1]
+
+    def pick_pair(pairs, index):
+        keep = jnp.stack([p[0] for p in pairs])
+        got = jnp.stack([p[1] for p in pairs])
+        return pick(keep, index) + pick(got, index)
+
+    send = pick_pair(d_down_part, 1 - y)
+    keep = pick_pair(d_down_part, y)
+    got = permute(send, to_y)
+    tile = keep.shape[-1]
+    keep, got = (a.reshape(2, 2, -1, tile) for a in (keep, got))
+    send = pick(keep, 1 - b_low, 1) + pick(got, 1 - b_low, 1)
+    keep = pick(keep, b_low, 1) + pick(got, b_low, 1)
+    got = permute(send, to_z1)
+    send = pick(keep, 1 - b_high) + pick(got, 1 - b_high)
+    keep = pick(keep, b_high) + pick(got, b_high)
+    got = permute(send, to_z2)
+    d_w_down = (keep.astype(f32) + got.astype(f32)).T
+    send = pick_pair(d_up_part, 1 - b_high)
+    keep = pick_pair(d_up_part, b_high)
+    got = permute(send, to_z2)
+    d_w_up = keep.astype(f32) + got.astype(f32)
+    d_w_up = jnp.where(
+        c == 0,
+        jnp.concatenate([d_w_up[1], d_w_up[0]], 1),
+        jnp.concatenate([d_w_up[0], d_w_up[1]], 1),
+    )
+    d_bias_up = jnp.stack(d_bias_up)[:, :, :, 0]
+    d_bias_up = jnp.where(c == 0, d_bias_up[:, ::-1], d_bias_up)
+    d_bias_up = d_bias_up.transpose(0, 2, 1, 3).reshape(-1, width)
+
+    output = return_rows((total + as_row(b_down)).astype(bf16))
+
+    d_res, da_own, da_send, dwo_a, dwo_b, sums_two = unjoin(
+        core, res, d_h2, cot_rows, as_row(ln2_gain), attn, attn_recv, w_out
+    )
+    da_recv = permute(da_send, to_core)
+    dq, dk, dv = attend_back(q, k, v, bias, jnp.concatenate([da_own, da_recv]), log_total)
+    dw, dh1, sums_qv = unproject(core, h1, dq, dk, dv, w_query, w_key, w_value)
+
+    dwo = jnp.stack([dwo_a, dwo_b]).reshape(2, 2, 2, -1, width)
+    got = permute(pick(dwo, 1 - c, 2), to_core)[::-1]
+    keep = pick(dwo, c, 2)
+    rel = y ^ c
+    send = pick(keep, 1 - rel) + pick(got, 1 - rel)
+    keep = pick(keep, rel) + pick(got, rel)
+    got = permute(send, to_y)
+    send = pick(keep, 1 - x) + pick(got, 1 - x)
+    keep = pick(keep, x) + pick(got, x)
+    got = permute(send, to_x)
+    fourth = width // 4
+    keep, got = (a.reshape(-1, 2, 2, fourth) for a in (keep, got))
+    send = pick(keep, 1 - b_low, 2) + pick(got, 1 - b_low, 2)
+    keep = pick(keep, b_low, 2) + pick(got, b_low, 2)
+    got = permute(send, to_z1)
+    send = pick(keep, 1 - b_high, 1) + pick(got, 1 - b_high, 1)
+    keep = pick(keep, b_high, 1) + pick(got, b_high, 1)
+    got = permute(send, to_z2)
+    d_w_out = keep.astype(f32) + got.astype(f32)
+
+    dw = dw.reshape(3, 2, 2, 2, -1, width // 2)
+    got = permute(pick(dw, 1 - c, 3), to_core)
+    dw = jnp.stack([pick(dw, c, 3), got])
+    send, keep = pick(dw, 1 - x, 3), pick(dw, x, 3)
+    got = permute(send, to_x)
+    send = pick(keep, 1 - y, 2) + pick(got, 1 - y, 2)
+    keep = pick(keep, y, 2) + pick(got, y, 2)
+    got = permute(send, to_y)
+    rel = b_high ^ c
+    keep, got = (a.reshape(2, 3, -1, 2, fourth) for a in (keep, got))
+    send = pick(keep, 1 - b_low, 3) + pick(got, 1 - b_low, 3)
+    keep = pick(keep, b_low, 3) + pick(got, b_low, 3)
+    got = permute(send, to_z1)
+    send = pick(keep, 1 - rel) + pick(got, 1 - rel)
+    keep = pick(keep, rel) + pick(got, rel)
+    got = permute(send, to_z2)
+    d_qkv = keep.astype(f32) + got.astype(f32)
+
+    dh_recv = permute(dh1[rows:], to_core)
+    g_rows, sums_one = start_back(tok, mean_row, inv_row, as_row(ln1_gain), dh1, dh_recv, d_res)
+    g_home = return_rows(g_rows)
+    empty = jnp.zeros_like(sums_qv)
+    halves = jnp.where(
+        c == 0,
+        jnp.concatenate([sums_qv, empty], 1),
+        jnp.concatenate([empty, sums_qv], 1),
+    )
+    small = all_sum(jnp.concatenate([sums_one, halves, sums_two, d_bias_up]), 2)
+    sum_g, sum_gx, d_gain_one, d_shift_one, d_bq, d_bv, d_gain_two, d_shift_two, d_bo, d_bdown = (
+        small[i] for i in range(10)
+    )
+    d_bup = small[10:].reshape(-1)
+    row_keep = (jnp.arange(band_rows, dtype=jnp.int32)[None, :] < left[:, None]).astype(f32)
+    cube = inverse * inverse * inverse
+    fix = -0.5 * inverse * sum_g / patch_total
+    slope = -0.5 * cube * sum_gx / patch_total
+    d_tokens = g_home.astype(f32) + row_keep[:, :, None] * (
+        fix + slope * (tokens.astype(f32) - batch_mean)
+    )
+    return (
+        output, d_tokens.astype(bf16), new_mean, new_var, d_gain_one, d_shift_one,
+        d_qkv[0], d_bq, d_qkv[1], d_qkv[2], d_bv, d_w_out, d_bo, d_gain_two, d_shift_two,
+        d_w_up, d_bup, d_w_down, d_bdown,
+    )
 
 
 def layer_norm(value, gain, shift):
@@ -364,8 +1170,9 @@
 
 
 def solution(mesh):
+    columns = mesh.shape["items"] == 8 and mesh.shape["band"] == 4
     return jax.shard_map(
-        local,
+        column_layer if columns else local,
         mesh=mesh,
         in_specs=(
             P("items", "band", None),

time: 1120 us -> 492 us (0.44)
  waiting for transfers between devices: 627 us -> 112 us
  matrix products: 188 us -> 0 us
  Pallas kernels: 0 us -> 159 us
  starting transfers between devices: 1.28 us -> 96.5 us
  local copies, waits for them, and re-layouts: 131 us -> 44.1 us
  blocking collectives: 83.3 us -> 0 us
  other arithmetic: 53.6 us -> 68.2 us
  between operations: 15.7 us -> 2.73 us
  loops' own time: 11.5 us -> 0 us
    reduce_scatter x14 -> x0, waiting for transfers between devices: 486 us -> none  [the longest x1 75.5 us: local(): lax.psum_scatter(jnp.stack(d_v_list).astype(jnp.bfloat16), 'band', scatte...]
    dot_general x74 -> x0, matrix products: 188 us -> none  [the longest x16 28 us: group_scores(): jnp.einsum('rhd,khd->hrk', q_part, k_part, preferred_element_type=jnp.flo...]
    pallas_call x0 -> x12, Pallas kernels: none -> 159 us  [the longest x2 45.8 us: mlp(): pl.pallas_call(mlp_kernel, name='mlp', grid_spec=pltpu.PrefetchScalarGrid...]
    all_gather x2 -> x0, waiting for transfers between devices: 142 us -> none  [the longest x1 75.7 us: local(): lax.all_gather(key_local, 'band', axis=1, tiled=True)]
    ppermute x0 -> x48, waiting for transfers between devices: none -> 112 us  [permute(): return lax.ppermute(array, ('items', 'band'), pairs)]
    ppermute x0 -> x48, starting transfers between devices: none -> 96.5 us  [permute(): return lax.ppermute(array, ('items', 'band'), pairs)]
    psum x2 -> x0, blocking collectives: 83.3 us -> none  [the longest x1 42.1 us: local(): total_one, total_two = lax.psum((part_one, part_two), ('items', 'band'))]
    dynamic_slice x64 -> x13, local copies, waits for them, and re-layouts: 49.2 us -> 11.5 us  [pick(): return lax.dynamic_index_in_dim(array, index, axis, keepdims=False)]
  transfers between devices with their start and end apart: 16 -> 48, of which waited for: 14 -> 14; matrix products, arithmetic and copies ran while one was open for 10% -> 20% of each run, Pallas kernels for 0% -> 22%
where the time goes in v1:
time: 492 us; the launch traced here: 483 us
  Pallas kernels  159 us (32%)
  waiting for transfers between devices  112 us (23%)
  starting transfers between devices  96.5 us (20%)
  other arithmetic  68.2 us (14%)
  local copies, waits for them, and re-layouts  44.1 us (9%)
    ppermute x48, waiting for transfers between devices, permute(): return lax.ppermute(array, ('items', 'band'), pairs)  112 us
    ppermute x48, starting transfers between devices, permute(): return lax.ppermute(array, ('items', 'band'), pairs)  96.5 us
    pallas_call x2, Pallas kernels, mlp(): pl.pallas_call(mlp_kernel, name='mlp', grid_spec=pltpu.PrefetchScalarGrid...  45.8 us
    pallas_call x2, Pallas kernels, all_sum(): pl.pallas_call(functools.partial(all_sum_kernel, n_items, n_band), name=f...  29.4 us
    pallas_call x1, Pallas kernels, attend_back(): pl.pallas_call(functools.partial(attend_back_kernel, qt), name='attend_ba...  24.9 us
    pallas_call x1, Pallas kernels, attend(): pl.pallas_call(functools.partial(attend_kernel, qt), name='attend', grid=...  15.3 us
    unnamed x121, local copies, waits for them, and re-layouts  13.6 us
    pallas_call x1, Pallas kernels, unproject(): pl.pallas_call(unproject_kernel, name='unproject', grid_spec=pltpu.Prefet...  12.6 us
  transfers between devices with their start and end apart: 48, of which 14 were waited for; matrix products, arithmetic and copies ran while one was open for 20% of the time, Pallas kernels for 22%

profile of v1, /device:TPU:0, one launch (start us, length us, event | category | flops | bytes accessed | tf_op | source)
XLA Modules:
  0.0 483.2 jit_solution(2060566580617158009)
XLA Ops:
  14.8 8.1 %collective-permute-done.3 = bf16[128,1024]{1,0:T(8,128)(2,1)S(1)} collective-permute-done((bf16[128,1024]{1,0:T(8,128)(2,1)S(1)}, bf16[128,1024]{1,0:T(8,128)(2,1)S(1)}, u32[]{:S(2)}, u32[]{:S(2)}) %collective-permute-start.3) | collective-permute-done | bytes 262176 | tf_op jit(solution)/shard_map/ppermute | solution.py:620
  35.1 12.0 %collective-permute-start.4 = (bf16[512,1024]{1,0:T(8,128)(2,1)}, bf16[512,1024]{1,0:T(8,128)(2,1)S(1)}, u32[]{:S(2)}, u32[]{:S(2)}) collective-permute-start(bf16[512,1024]{1,0:T(8,128)(2,1)} %pad_maximum_fusion), channel_id=1, source_target_pairs={{0,4},{1,5},{2,6},{3,7},{4,0},{5,1},{6,2},{7,3},{8,12},{9,13},{10,... | collective-permute-start | bytes 3145736 | tf_op jit(solution)/shard_map/ppermute | solution.py:620
  54.4 11.1 %all_sum_1.1 = f32[2,1024]{1,0:T(2,128)} custom-call(f32[2,1024]{1,0:T(2,128)} %stats.1.x), custom_call_target="tpu_custom_call" | custom-call | tf_op jit(solution)/shard_map/all_sum_1/pallas_call | solution.py:313
  70.0 8.1 %project.1 = (bf16[1024,1024]{1,0:T(8,128)(2,1)}, bf16[1024,512]{1,0:T(8,128)(2,1)}, bf16[1024,512]{1,0:T(8,128)(2,1)}, bf16[1024,512]{1,0:T(8,128)(2,1)}) custom-call(s32[1]{0:T(128)} %bitcast.core, bf16[1024,1024]{1,0:T(8,128)(2,1)} %copy-done.1, f32[1,1024]{1,0:T(1,128)} %bitcast.274, f32[1,1024]{1,0:T(1,128)} %bitcast.277, f32[1,1024]{1,0:T(1,128)} %bitcast.284, ...), custom_call_target="tpu_custom_call" | custom-call | flops 3221225472 | bytes 12582912 | tf_op jit(solution)/shard_map/project/pallas_call | solution.py:48
  79.0 15.3 %attend.1 = (bf16[1024,512]{1,0:T(8,128)(2,1)}, f32[4,2,1024]{2,1,0:T(2,128)}) custom-call(bf16[1024,512]{1,0:T(8,128)(2,1)} %get-tuple-element.62.q, bf16[1024,512]{1,0:T(8,128)(2,1)} %get-tuple-element.63.k, bf16[1024,512]{1,0:T(8,128)(2,1)} %get-tuple-element.64.v, bf16[1024,128]{1,0:T(8,128)(2,1)} %broadcast_in_dim.30.bias), custom_call_target="tpu_custom_call" | custom-call | flops 8589934592 | bytes 5242880 | tf_op jit(solution)/shard_map/attend/pallas_call | solution.py:107
  102.8 5.2 %join.1 = (f32[512,1024]{1,0:T(8,128)}, bf16[512,1024]{1,0:T(8,128)(2,1)}, bf16[512,1024]{1,0:T(8,128)(2,1)}) custom-call(s32[1]{0:T(128)} %bitcast.core, bf16[1024,512]{1,0:T(8,128)(2,1)} %get-tuple-element.65.attn_a, bf16[512,512]{1,0:T(8,128)(2,1)} %copy-done.19, bf16[1024,1024]{1,0:T(8,128)(2,1)} %wo_b.3, bf16[1024,1024]{1,0:T(8,128)(2,1)} %wo_b.3, ...), custom_call_target="tpu_custom_call" | custom-call | flops 1073741824 | bytes 8388608 | tf_op jit(solution)/shard_map/join/pallas_call | solution.py:384
  109.7 22.9 %mlp.2 = (f32[512,1024]{1,0:T(8,128)}, f32[512,1024]{1,0:T(8,128)}, bf16[2,1024,512]{2,1,0:T(8,128)(2,1)}, bf16[2,512,512]{2,1,0:T(8,128)(2,1)}, bf16[2,512,512]...) custom-call(s32[1]{0:T(128)} %bitcast.core, ...), custom_call_target="tpu_custom_call" | custom-call | flops 12884901888 | bytes 20971520 | tf_op jit(solution)/shard_map/mlp/pallas_call | solution.py:256
  132.5 22.9 %mlp.3 = (f32[512,1024]{1,0:T(8,128)}, f32[512,1024]{1,0:T(8,128)}, bf16[2,1024,512]{2,1,0:T(8,128)(2,1)}, bf16[2,512,512]{2,1,0:T(8,128)(2,1)}, bf16[2,512,512]...) custom-call(s32[1]{0:T(128)} %bitcast.core, ...), custom_call_target="tpu_custom_call" | custom-call | flops 12884901888 | bytes 20971520 | tf_op jit(solution)/shard_map/mlp/pallas_call | solution.py:256
  158.3 5.4 %collective-permute-start.13 = (bf16[128,1024]{1,0:T(8,128)(2,1)S(1)}, bf16[128,1024]{1,0:T(8,128)(2,1)S(1)}, u32[]{:S(2)}, u32[]{:S(2)}) collective-permute-start(bf16[128,1024]{1,0:T(8,128)(2,1)S(1)} %get-tuple-element.212), channel_id=1, source_target_pairs={{0,3},{1,1},{2,7},{3,5},{4,2},{5,0},{6,6},{7,4},{8,11},{9,9},{10,1... | collective-permute-start | bytes 786440 | tf_op jit(solution)/shard_map/ppermute | solution.py:620
  165.8 10.9 %unjoin.1 = (f32[512,1024]{1,0:T(8,128)}, bf16[512,512]{1,0:T(8,128)(2,1)}, bf16[512,512]{1,0:T(8,128)(2,1)}, bf16[512,1024]{1,0:T(8,128)(2,1)}, bf16[512,1024]{1,0:T(8,128)(2,1)}, /*index=5*/f32[4,1024]{1,0:T(4,128)}) custom-call(s32[1]{0:T(128)} %bitcast.core, f32[512,1024]{1,0:T(8,128)} %get-tuple-element.68.out_in.res, ...), custom_call_target="tpu_custom_call" | custom-call | flops 2147483648 | bytes 12582912 | tf_op jit(solution)/shard_map/unjoin/pallas_call | solution.py:476
  187.4 24.9 %attend_back.1 = (bf16[1024,512]{1,0:T(8,128)(2,1)}, bf16[1024,512]{1,0:T(8,128)(2,1)}, bf16[1024,512]{1,0:T(8,128)(2,1)}) custom-call(bf16[1024,512]{1,0:T(8,128)(2,1)} %get-tuple-element.62.q, bf16[1024,512]{1,0:T(8,128)(2,1)} %get-tuple-element.63.k, bf16[1024,512]{1,0:T(8,128)(2,1)} %get-tuple-element.64.v, bf16[1024,128]{1,0:T(8,128)(2,1)} %broadcast_in_dim.30.bias, ...), custom_call_target="tpu_custom_call" | custom-call | flops 21474836480 | bytes 8388608 | tf_op jit(solution)/shard_map/attend_back/pallas_call | solution.py:164
  212.2 12.6 %unproject.1 = (bf16[3,1024,512]{2,1,0:T(8,128)(2,1)}, bf16[1024,1024]{1,0:T(8,128)(2,1)}, f32[2,512]{1,0:T(2,128)}) custom-call(s32[1]{0:T(128)} %bitcast.core, bf16[1024,1024]{1,0:T(8,128)(2,1)} %get-tuple-element.72.h1, bf16[1024,512]{1,0:T(8,128)(2,1)} %get-tuple-element.77.dq.dq_r, bf16[1024,512]{1,0:T(8,128)(2,1)} %get-tuple-element.78.dk.dk_r, ...), custom_call_target="tpu_custom_call" | custom-call | flops 6442450944 | bytes 14680064 | tf_op jit(solution)/shard_map/unproject/pallas_call | solution.py:533
  247.5 4.9 %start_back.1 = (bf16[512,1024]{1,0:T(8,128)(2,1)}, f32[4,1024]{1,0:T(4,128)}) custom-call(bf16[1024,1024]{1,0:T(8,128)(2,1)} %copy-done.1, f32[1,1024]{1,0:T(1,128)} %bitcast.276, f32[1,1024]{1,0:T(1,128)} %bitcast.279, f32[1,1024]{1,0:T(1,128)} %bitcast.285, bf16[1024,1024]{1,0:T(8,128)(2,1)} %get-tuple-element.80.dh_a, ...), custom_call_target="tpu_custom_call" | custom-call | flops 4194304 | bytes 8388608 | tf_op jit(solution)/shard_map/start_back/pallas_call | solution.py:581
  253.8 18.3 %all_sum_2.1 = f32[14,1024]{1,0:T(8,128)} custom-call(f32[14,1024]{1,0:T(8,128)} %pad_maximum_fusion.6.x), custom_call_target="tpu_custom_call" | custom-call | tf_op jit(solution)/shard_map/all_sum_2/pallas_call | solution.py:313
  275.6 6.6 %collective-permute-start.19 = (bf16[128,1024]{1,0:T(8,128)(2,1)S(1)}, bf16[128,1024]{1,0:T(8,128)(2,1)}, u32[]{:S(2)}, u32[]{:S(2)}) collective-permute-start(bf16[128,1024]{1,0:T(8,128)(2,1)S(1)} %get-tuple-element.204), channel_id=1, source_target_pairs={{0,3},{1,1},{2,7},{3,5},{4,2},{5,0},{6,6},{7,4},{8,11},{9,9},{10,1... | collective-permute-start | bytes 786440 | tf_op jit(solution)/shard_map/ppermute | solution.py:620
  282.9 8.2 %collective-permute-start.18 = (bf16[128,1024]{1,0:T(8,128)(2,1)}, bf16[128,1024]{1,0:T(8,128)(2,1)}, u32[]{:S(2)}, u32[]{:S(2)}) collective-permute-start(bf16[128,1024]{1,0:T(8,128)(2,1)} %get-tuple-element.205), channel_id=1, source_target_pairs={{0,2},{1,0},{2,6},{3,4},{4,3},{5,1},{6,7},{7,5},{8,10},{9,8},{10,1... | collective-permute-start | bytes 786440 | tf_op jit(solution)/shard_map/ppermute | solution.py:620
  318.9 38.5 %collective-permute-done.27 = bf16[128,1024]{1,0:T(8,128)(2,1)} collective-permute-done((bf16[128,1024]{1,0:T(8,128)(2,1)}, bf16[128,1024]{1,0:T(8,128)(2,1)}, u32[]{:S(2)}, u32[]{:S(2)}) %collective-permute-start.27) | collective-permute-done | bytes 262176 | tf_op jit(solution)/shard_map/ppermute | solution.py:620
  368.0 5.6 %collective-permute-start.28 = (bf16[128,2,256]{0,2,1:T(8,128)(2,1)S(1)}, bf16[128,2,256]{0,2,1:T(8,128)(2,1)S(1)}, u32[]{:S(2)}, u32[]{:S(2)}) collective-permute-start(bf16[128,2,256]{0,2,1:T(8,128)(2,1)S(1)} %get-tuple-element.228), channel_id=1, source_target_pairs={{0,1},{1,0},{2,3},{3,2},{4,5},{5,4},{6,7},{7,6},{8,9},{9,8},{10,11... | collective-permute-start | bytes 393224 | tf_op jit(solution)/shard_map/ppermute | solution.py:620
  381.4 22.0 %collective-permute-done.33 = bf16[2,2,128,512]{3,2,0,1:T(8,128)(2,1)S(1)} collective-permute-done((bf16[2,2,128,512]{3,2,0,1:T(8,128)(2,1)S(1)}, bf16[2,2,128,512]{3,2,0,1:T(8,128)(2,1)S(1)}, u32[]{:S(2)}, u32[]{:S(2)}) %collective-permute-start.33) | collective-permute-done | bytes 524320 | tf_op jit(solution)/shard_map/ppermute | solution.py:620
  404.2 8.2 %collective-permute-start.38 = (bf16[2,128,512]{2,1,0:T(8,128)(2,1)}, bf16[2,128,512]{2,1,0:T(8,128)(2,1)}, u32[]{:S(2)}, u32[]{:S(2)}) collective-permute-start(bf16[2,128,512]{2,1,0:T(8,128)(2,1)} %get-tuple-element.196), channel_id=1, source_target_pairs={{0,1},{1,0},{2,3},{3,2},{4,5},{5,4},{6,7},{7,6},{8,9},{9,8},{10,11... | collective-permute-start | bytes 786440 | tf_op jit(solution)/shard_map/ppermute | solution.py:620
  415.5 8.2 %collective-permute-start.39 = (bf16[2,128,512]{2,1,0:T(8,128)(2,1)}, bf16[2,128,512]{2,1,0:T(8,128)(2,1)}, u32[]{:S(2)}, u32[]{:S(2)}) collective-permute-start(bf16[2,128,512]{2,1,0:T(8,128)(2,1)} %get-tuple-element.194), channel_id=1, source_target_pairs={{0,1},{1,0},{2,3},{3,2},{4,5},{5,4},{6,7},{7,6},{8,9},{9,8},{10,11... | collective-permute-start | bytes 786440 | tf_op jit(solution)/shard_map/ppermute | solution.py:620
  440.6 5.8 %collective-permute-done.40 = bf16[2,128,512]{2,1,0:T(8,128)(2,1)S(1)} collective-permute-done((bf16[2,128,512]{2,1,0:T(8,128)(2,1)S(1)}, bf16[2,128,512]{2,1,0:T(8,128)(2,1)S(1)}, u32[]{:S(2)}, u32[]{:S(2)}) %collective-permute-start.40) | collective-permute-done | bytes 262176 | tf_op jit(solution)/shard_map/ppermute | solution.py:620
  461.2 9.7 %collective-permute-done.23 = bf16[2,3,128,256]{2,3,1,0:T(8,128)(2,1)S(1)} collective-permute-done((bf16[2,3,128,256]{2,3,1,0:T(8,128)(2,1)S(1)}, bf16[2,3,128,256]{2,3,1,0:T(8,128)(2,1)S(1)}, u32[]{:S(2)}, u32[]{:S(2)}) %collective-permute-start.23) | collective-permute-done | bytes 393248 | tf_op jit(solution)/shard_map/ppermute | solution.py:620
  472.9 7.8 %collective-permute-done.24 = bf16[3,128,256]{1,2,0:T(8,128)(2,1)S(1)} collective-permute-done((bf16[3,128,256]{1,2,0:T(8,128)(2,1)S(1)}, bf16[3,128,256]{1,2,0:T(8,128)(2,1)S(1)}, u32[]{:S(2)}, u32[]{:S(2)}) %collective-permute-start.24) | collective-permute-done | bytes 196640 | tf_op jit(solution)/shard_map/ppermute | solution.py:620
  (305 shorter events, 177.4 us)
Async XLA Ops:
  3.0 98.0 %collective-permute-start.9 = (bf16[128,1024]{1,0:T(8,128)(2,1)}, bf16[128,1024]{1,0:T(8,128)(2,1)}, u32[]{:S(2)}, u32[]{:S(2)}) collective-permute-start(bf16[128,1024]{1,0:T(8,128)(2,1)} %get-tuple-element.215), channel_id=1, source_target_pairs={{0,5},{1,1},{2,4},{3,0},{4,7},{5,3},{6,6},{7,2},{8,13},{9,9},{10,1... | collective-permute-start | bytes 786440 | tf_op jit(solution)/shard_map/ppermute | solution.py:620
  22.9 77.0 %collective-permute-start.8 = (bf16[128,1024]{1,0:T(8,128)(2,1)}, bf16[128,1024]{1,0:T(8,128)(2,1)}, u32[]{:S(2)}, u32[]{:S(2)}) collective-permute-start(bf16[128,1024]{1,0:T(8,128)(2,1)} %get-tuple-element.216), channel_id=1, source_target_pairs={{0,1},{1,5},{2,0},{3,4},{4,3},{5,7},{6,2},{7,6},{8,9},{9,13},{10,8... | collective-permute-start | bytes 786440 | tf_op jit(solution)/shard_map/ppermute | solution.py:620
  27.0 72.0 %collective-permute-start.7 = (bf16[128,1024]{1,0:T(8,128)(2,1)}, bf16[128,1024]{1,0:T(8,128)(2,1)}, u32[]{:S(2)}, u32[]{:S(2)}) collective-permute-start(bf16[128,1024]{1,0:T(8,128)(2,1)} %get-tuple-element.217), channel_id=1, source_target_pairs={{0,4},{1,0},{2,5},{3,1},{4,6},{5,2},{6,7},{7,3},{8,12},{9,8},{10,1... | collective-permute-start | bytes 786440 | tf_op jit(solution)/shard_map/ppermute | solution.py:620
  30.5 67.5 %collective-permute-start.6 = (bf16[128,1024]{1,0:T(8,128)(2,1)}, bf16[128,1024]{1,0:T(8,128)(2,1)}, u32[]{:S(2)}, u32[]{:S(2)}) collective-permute-start(bf16[128,1024]{1,0:T(8,128)(2,1)} %get-tuple-element.218), channel_id=1, source_target_pairs={{0,0},{1,4},{2,1},{3,5},{4,2},{5,6},{6,3},{7,7},{8,8},{9,12},{10,9... | collective-permute-start | bytes 786440 | tf_op jit(solution)/shard_map/ppermute | solution.py:620
  35.1 33.5 %collective-permute-start.4 = (bf16[512,1024]{1,0:T(8,128)(2,1)}, bf16[512,1024]{1,0:T(8,128)(2,1)S(1)}, u32[]{:S(2)}, u32[]{:S(2)}) collective-permute-start(bf16[512,1024]{1,0:T(8,128)(2,1)} %pad_maximum_fusion), channel_id=1, source_target_pairs={{0,4},{1,5},{2,6},{3,7},{4,0},{5,1},{6,2},{7,3},{8,12},{9,13},{10,... | collective-permute-start | bytes 3145736 | tf_op jit(solution)/shard_map/ppermute | solution.py:620
  182.5 49.3 %collective-permute-start.30 = (bf16[2,512,512]{2,1,0:T(8,128)(2,1)}, bf16[2,512,512]{2,1,0:T(8,128)(2,1)}, u32[]{:S(2)}, u32[]{:S(2)}) collective-permute-start(bf16[2,512,512]{2,1,0:T(8,128)(2,1)} %get-tuple-element.95), channel_id=1, source_target_pairs={{0,4},{1,5},{2,6},{3,7},{4,0},{5,1},{6,2},{7,3},{8,12},{9,13},{10,... | collective-permute-start | bytes 3145736 | tf_op jit(solution)/shard_map/ppermute | solution.py:620
  183.0 48.9 %collective-permute-start.31 = (bf16[2,512,512]{2,1,0:T(8,128)(2,1)}, bf16[2,512,512]{2,1,0:T(8,128)(2,1)}, u32[]{:S(2)}, u32[]{:S(2)}) collective-permute-start(bf16[2,512,512]{2,1,0:T(8,128)(2,1)} %get-tuple-element.96), channel_id=1, source_target_pairs={{0,4},{1,5},{2,6},{3,7},{4,0},{5,1},{6,2},{7,3},{8,12},{9,13},{10,... | collective-permute-start | bytes 3145736 | tf_op jit(solution)/shard_map/ppermute | solution.py:620
  183.0 53.9 %collective-permute-start.25 = (bf16[2,2,128,1024]{3,2,1,0:T(8,128)(2,1)}, bf16[2,2,128,1024]{3,2,1,0:T(8,128)(2,1)}, u32[]{:S(2)}, u32[]{:S(2)}) collective-permute-start(bf16[2,2,128,1024]{3,2,1,0:T(8,128)(2,1)} %fusion.18), channel_id=1, source_target_pairs={{0,4},{1,5},{2,6},{3,7},{4,0},{5,1},{6,2},{7,3},{8,12},{9,13},{10,... | collective-permute-start | bytes 3145736 | tf_op jit(solution)/shard_map/ppermute | solution.py:620
  183.5 58.4 %collective-permute-start.34 = (bf16[2,512,512]{2,1,0:T(8,128)(2,1)}, bf16[2,512,512]{2,1,0:T(8,128)(2,1)}, u32[]{:S(2)}, u32[]{:S(2)}) collective-permute-start(bf16[2,512,512]{2,1,0:T(8,128)(2,1)} %get-tuple-element.99), channel_id=1, source_target_pairs={{0,4},{1,5},{2,6},{3,7},{4,0},{5,1},{6,2},{7,3},{8,12},{9,13},{10,... | collective-permute-start | bytes 3145736 | tf_op jit(solution)/shard_map/ppermute | solution.py:620
  185.9 56.5 %collective-permute-start.35 = (bf16[2,512,512]{2,1,0:T(8,128)(2,1)}, bf16[2,512,512]{2,1,0:T(8,128)(2,1)}, u32[]{:S(2)}, u32[]{:S(2)}) collective-permute-start(bf16[2,512,512]{2,1,0:T(8,128)(2,1)} %get-tuple-element.100), channel_id=1, source_target_pairs={{0,4},{1,5},{2,6},{3,7},{4,0},{5,1},{6,2},{7,3},{8,12},{9,13},{10,... | collective-permute-start | bytes 3145736 | tf_op jit(solution)/shard_map/ppermute | solution.py:620
  231.8 71.7 %collective-permute-start.41 = (bf16[2,1024,512]{2,1,0:T(8,128)(2,1)}, bf16[2,1024,512]{2,1,0:T(8,128)(2,1)}, u32[]{:S(2)}, u32[]{:S(2)}) collective-permute-start(bf16[2,1024,512]{2,1,0:T(8,128)(2,1)} %get-tuple-element.102), channel_id=1, source_target_pairs={{0,4},{1,5},{2,6},{3,7},{4,0},{5,1},{6,2},{7,3},{8,12},{9,13},{10,... | collective-permute-start | bytes 6291464 | tf_op jit(solution)/shard_map/ppermute | solution.py:620
  237.0 71.2 %collective-permute-start.42 = (bf16[2,1024,512]{2,1,0:T(8,128)(2,1)}, bf16[2,1024,512]{2,1,0:T(8,128)(2,1)}, u32[]{:S(2)}, u32[]{:S(2)}) collective-permute-start(bf16[2,1024,512]{2,1,0:T(8,128)(2,1)} %get-tuple-element.104), channel_id=1, source_target_pairs={{0,4},{1,5},{2,6},{3,7},{4,0},{5,1},{6,2},{7,3},{8,12},{9,13},{10,... | collective-permute-start | bytes 6291464 | tf_op jit(solution)/shard_map/ppermute | solution.py:620
  241.9 70.2 %collective-permute-start.20 = (bf16[3,2,2,128,512]{3,4,0,2,1:T(8,128)(2,1)}, bf16[3,2,2,128,512]{3,4,0,2,1:T(8,128)(2,1)S(1)}, u32[]{:S(2)}, u32[]{:S(2)}) collective-permute-start(bf16[3,2,2,128,512]{3,4,0,2,1:T(8,128)(2,1)} %bitcast.47), channel_id=1, source_target_pairs={{0,4},{1,5},{2,6},{3,7},{4,0},{5,1},{6,2},{7,3},{8,12},{9,13},{10,... | collective-permute-start | bytes 4718600 | tf_op jit(solution)/shard_map/ppermute | solution.py:620
  242.3 33.3 %collective-permute-start.26 = (bf16[2,128,1024]{2,1,0:T(8,128)(2,1)}, bf16[2,128,1024]{2,1,0:T(8,128)(2,1)}, u32[]{:S(2)}, u32[]{:S(2)}) collective-permute-start(bf16[2,128,1024]{2,1,0:T(8,128)(2,1)} %get-tuple-element.171), channel_id=1, source_target_pairs={{0,16},{1,17},{2,18},{3,19},{4,20},{5,21},{6,22},{7,23},{8,24},{9,... | collective-permute-start | bytes 1572872 | tf_op jit(solution)/shard_map/ppermute | solution.py:620
  296.5 66.3 %collective-permute-start.32 = (bf16[2,2,2,128,512]{4,3,0,1,2:T(8,128)(2,1)}, bf16[2,2,2,128,512]{4,3,0,1,2:T(8,128)(2,1)}, u32[]{:S(2)}, u32[]{:S(2)}) collective-permute-start(bf16[2,2,2,128,512]{4,3,0,1,2:T(8,128)(2,1)} %fusion.20), channel_id=1, source_target_pairs={{0,16},{1,17},{2,18},{3,19},{4,20},{5,21},{6,22},{7,23},{8,24},{9,... | collective-permute-start | bytes 3145736 | tf_op jit(solution)/shard_map/ppermute | solution.py:620
  300.9 64.2 %collective-permute-start.36 = (bf16[2,2,2,128,512]{4,3,0,1,2:T(8,128)(2,1)}, bf16[2,2,2,128,512]{4,3,0,1,2:T(8,128)(2,1)}, u32[]{:S(2)}, u32[]{:S(2)}) collective-permute-start(bf16[2,2,2,128,512]{4,3,0,1,2:T(8,128)(2,1)} %fusion.19), channel_id=1, source_target_pairs={{0,16},{1,17},{2,18},{3,19},{4,20},{5,21},{6,22},{7,23},{8,24},{9,... | collective-permute-start | bytes 3145736 | tf_op jit(solution)/shard_map/ppermute | solution.py:620
  306.8 61.2 %collective-permute-start.43 = (bf16[1024,512]{1,0:T(8,128)(2,1)}, bf16[1024,512]{1,0:T(8,128)(2,1)}, u32[]{:S(2)}, u32[]{:S(2)}) collective-permute-start(bf16[1024,512]{1,0:T(8,128)(2,1)} %get-tuple-element.169), channel_id=1, source_target_pairs={{0,8},{1,9},{2,10},{3,11},{4,12},{5,13},{6,14},{7,15},{8,0},{9,1},... | collective-permute-start | bytes 3145736 | tf_op jit(solution)/shard_map/ppermute | solution.py:620
  311.4 62.2 %collective-permute-start.44 = (bf16[1024,512]{1,0:T(8,128)(2,1)}, bf16[1024,512]{1,0:T(8,128)(2,1)}, u32[]{:S(2)}, u32[]{:S(2)}) collective-permute-start(bf16[1024,512]{1,0:T(8,128)(2,1)} %get-tuple-element.167), channel_id=1, source_target_pairs={{0,8},{1,9},{2,10},{3,11},{4,12},{5,13},{6,14},{7,15},{8,0},{9,1},... | collective-permute-start | bytes 3145736 | tf_op jit(solution)/shard_map/ppermute | solution.py:620
  312.1 45.3 %collective-permute-start.27 = (bf16[128,1024]{1,0:T(8,128)(2,1)}, bf16[128,1024]{1,0:T(8,128)(2,1)}, u32[]{:S(2)}, u32[]{:S(2)}) collective-permute-start(bf16[128,1024]{1,0:T(8,128)(2,1)} %get-tuple-element.198), channel_id=1, source_target_pairs={{0,8},{1,9},{2,10},{3,11},{4,12},{5,13},{6,14},{7,15},{8,0},{9,1},... | collective-permute-start | bytes 786440 | tf_op jit(solution)/shard_map/ppermute | solution.py:620
  357.4 75.0 %collective-permute-start.21 = (bf16[2,3,2,128,512]{4,3,2,1,0:T(8,128)(2,1)}, bf16[2,3,2,128,512]{4,3,2,1,0:T(8,128)(2,1)}, u32[]{:S(2)}, u32[]{:S(2)}) collective-permute-start(bf16[2,3,2,128,512]{4,3,2,1,0:T(8,128)(2,1)} %bitcast.257), channel_id=1, source_target_pairs={{0,8},{1,9},{2,10},{3,11},{4,12},{5,13},{6,14},{7,15},{8,0},{9,1},... | collective-permute-start | bytes 4718600 | tf_op jit(solution)/shard_map/ppermute | solution.py:620
  364.5 39.0 %collective-permute-start.33 = (bf16[2,2,128,512]{3,2,0,1:T(8,128)(2,1)S(1)}, bf16[2,2,128,512]{3,2,0,1:T(8,128)(2,1)S(1)}, u32[]{:S(2)}, u32[]{:S(2)}) collective-permute-start(bf16[2,2,128,512]{3,2,0,1:T(8,128)(2,1)S(1)} %get-tuple-element.183), channel_id=1, source_target_pairs={{0,8},{1,9},{2,10},{3,11},{4,12},{5,13},{6,14},{7,15},{8,0},{9,1},... | collective-permute-start | bytes 1572872 | tf_op jit(solution)/shard_map/ppermute | solution.py:620
  366.5 48.2 %collective-permute-start.37 = (bf16[2,2,128,512]{3,2,0,1:T(8,128)(2,1)S(1)}, bf16[2,2,128,512]{3,2,0,1:T(8,128)(2,1)S(1)}, u32[]{:S(2)}, u32[]{:S(2)}) collective-permute-start(bf16[2,2,128,512]{3,2,0,1:T(8,128)(2,1)S(1)} %get-tuple-element.177), channel_id=1, source_target_pairs={{0,8},{1,9},{2,10},{3,11},{4,12},{5,13},{6,14},{7,15},{8,0},{9,1},... | collective-permute-start | bytes 1572872 | tf_op jit(solution)/shard_map/ppermute | solution.py:620
  378.1 57.5 %collective-permute-start.45 = (bf16[1024,512]{1,0:T(8,128)(2,1)}, bf16[1024,512]{1,0:T(8,128)(2,1)}, u32[]{:S(2)}, u32[]{:S(2)}) collective-permute-start(bf16[1024,512]{1,0:T(8,128)(2,1)} %get-tuple-element.165), channel_id=1, source_target_pairs={{0,16},{1,17},{2,18},{3,19},{4,20},{5,21},{6,22},{7,23},{8,24},{9,... | collective-permute-start | bytes 3145736 | tf_op jit(solution)/shard_map/ppermute | solution.py:620
  380.1 43.6 %collective-permute-start.29 = (bf16[128,256]{0,1:T(8,128)(2,1)S(1)}, bf16[128,256]{0,1:T(8,128)(2,1)S(1)}, u32[]{:S(2)}, u32[]{:S(2)}) collective-permute-start(bf16[128,256]{0,1:T(8,128)(2,1)S(1)} %fusion.46), channel_id=1, source_target_pairs={{0,2},{1,3},{2,0},{3,1},{4,6},{5,7},{6,4},{7,5},{8,10},{9,11},{10,... | collective-permute-start | bytes 196616 | tf_op jit(solution)/shard_map/ppermute | solution.py:620
  (76 other events, 1306.6 us)

commit v2 on v1

--- a/solution.py
+++ b/solution.py
@@ -23,6 +23,172 @@
 
 def params(**kw):
     return pltpu.CompilerParams(vmem_limit_bytes=VMEM_LIMIT, **kw)
+
+
+def place():
+    it, bd = lax.axis_index("items"), lax.axis_index("band")
+    return it, bd, lax.rem(it, 2), it // 2
+
+
+def remote(src, dst, send, recv, to):
+    return pltpu.make_async_remote_copy(
+        src_ref=src,
+        dst_ref=dst,
+        send_sem=send,
+        recv_sem=recv,
+        device_id=to,
+        device_id_type=pl.DeviceIdType.MESH,
+    )
+
+
+def greet(peers):
+    barrier = pltpu.get_barrier_semaphore()
+    for peer in peers:
+        pl.semaphore_signal(barrier, inc=1, device_id=peer, device_id_type=pl.DeviceIdType.MESH)
+    pl.semaphore_wait(barrier, len(peers))
+
+
+def column_peers():
+    it, bd, c, yx = place()
+    peers = [(it, lax.rem(bd + o, 4)) for o in range(1, 4)]
+    return peers + [(it + 1 - 2 * c, lax.rem(bd + o, 4)) for o in range(4)]
+
+
+def rows_out(src, dst, send, recv):
+    it, bd, c, yx = place()
+    cut = src.shape[1] // 2
+    for q in range(4):
+        s, h = q // 2, q % 2
+        block = src.at[s, pl.ds(h * cut, cut)]
+        target = dst.at[bd]
+        own = (c == h) & (bd == 2 * c + s)
+
+        @pl.when(own)
+        def _():
+            pltpu.make_async_copy(block, target, recv.at[bd]).start()
+
+        @pl.when(jnp.logical_not(own))
+        def _():
+            remote(block, target, send.at[q], recv.at[bd], (yx * 2 + h, 2 * c + s)).start()
+
+
+def rows_out_sent(src, dst, send, recv):
+    it, bd, c, yx = place()
+    cut = src.shape[1] // 2
+    for q in range(4):
+        s, h = q // 2, q % 2
+        own = (c == h) & (bd == 2 * c + s)
+
+        @pl.when(jnp.logical_not(own))
+        def _():
+            block = src.at[s, pl.ds(h * cut, cut)]
+            remote(block, dst.at[bd], send.at[q], recv.at[bd], (yx * 2 + h, 2 * c + s)).wait_send()
+
+
+def rows_out_got(src, dst, send, recv, band):
+    it, bd, c, yx = place()
+    cut = src.shape[1] // 2
+    pltpu.make_async_copy(src.at[0, pl.ds(0, cut)], dst.at[band], recv.at[band]).wait()
+
+
+def rows_back(src, dst, send, recv):
+    it, bd, c, yx = place()
+    cut = src.shape[1]
+    home = bd // 2
+    s = lax.rem(bd, 2)
+    target = dst.at[s, pl.ds(pl.multiple_of(c * cut, cut), cut)]
+    got = recv.at[2 * s + c]
+    for r in range(4):
+        own = (home == c) & (bd == r)
+
+        @pl.when(own)
+        def _():
+            pltpu.make_async_copy(src.at[r], target, got).start()
+
+        @pl.when(jnp.logical_not(own))
+        def _():
+            remote(src.at[r], target, send.at[r], got, (yx * 2 + home, r)).start()
+
+
+def rows_back_sent(src, dst, send, recv):
+    it, bd, c, yx = place()
+    cut = src.shape[1]
+    home = bd // 2
+    for r in range(4):
+        own = (home == c) & (bd == r)
+
+        @pl.when(jnp.logical_not(own))
+        def _():
+            target = dst.at[0, pl.ds(0, cut)]
+            remote(src.at[r], target, send.at[r], recv.at[0], (yx * 2 + home, r)).wait_send()
+
+
+def rows_back_got(src, dst, send, recv, q):
+    cut = src.shape[1]
+    s, h = q // 2, q % 2
+    pltpu.make_async_copy(src.at[0], dst.at[s, pl.ds(h * cut, cut)], recv.at[q]).wait()
+
+
+def gather_kernel(n_items, n_band, table, counts, tok, rows, sums, one, buf_i, part, buf_b, *sems):
+    (send_t, recv_t, send_s, recv_s, send_i, recv_i, send_b, recv_b) = sems
+    it, bd, c, yx = place()
+    sibling = (it + 1 - 2 * c, bd)
+    others = []
+    for o in range(1, n_items // 2):
+        for k in range(2):
+            others.append((lax.rem(yx + o, n_items // 2) * 2 + k, bd))
+    greet(column_peers() + others)
+    rows_out(tok, rows, send_t, recv_t)
+    slots, band_rows, width = tok.shape
+    at = lax.broadcasted_iota(jnp.int32, (band_rows, width), 0) + bd * band_rows
+    first = jnp.zeros((1, width), f32)
+    second = jnp.zeros((1, width), f32)
+    for s in range(slots):
+        x = jnp.where(at < counts[table[it * slots + s]], tok[s].astype(f32), 0.0)
+        first = first + jnp.sum(x, 0, keepdims=True)
+        second = second + jnp.sum(x * x, 0, keepdims=True)
+    one[0:1, :] = first
+    one[1:2, :] = second
+    part[...] = share(n_items, it, lambda p: (p, bd), one, buf_i, send_i, recv_i)
+    sums[...] = share(n_band, bd, lambda p: (it, p), part, buf_b, send_b, recv_b)
+    hand = []
+    for o in range(4):
+        band = lax.rem(bd + o, 4)
+        rows_out_got(tok, rows, send_t, recv_t, band)
+        copy = remote(rows.at[band], rows.at[4 + band], send_s.at[o], recv_s.at[o], sibling)
+        copy.start()
+        hand.append(copy)
+    for copy in hand:
+        copy.wait()
+    rows_out_sent(tok, rows, send_t, recv_t)
+
+
+def gather(table, counts, tok):
+    n_items, n_band = lax.axis_size("items"), lax.axis_size("band")
+    slots, band_rows, width = tok.shape
+    vmem = pl.BlockSpec(memory_space=pltpu.VMEM)
+    smem = pl.BlockSpec(memory_space=pltpu.SMEM)
+    dma = pltpu.SemaphoreType.DMA
+    return pl.pallas_call(
+        functools.partial(gather_kernel, n_items, n_band),
+        name="gather",
+        in_specs=[smem, smem, vmem],
+        out_specs=[pl.BlockSpec(memory_space=pltpu.HBM), vmem],
+        out_shape=[
+            jax.ShapeDtypeStruct((8, band_rows // 2, width), bf16),
+            jax.ShapeDtypeStruct((2, width), f32),
+        ],
+        scratch_shapes=[
+            pltpu.VMEM((2, width), f32),
+            pltpu.VMEM((n_items, 2, width), f32),
+            pltpu.VMEM((2, width), f32),
+            pltpu.VMEM((n_band, 2, width), f32),
+        ]
+        + [dma((4,))] * 4
+        + [dma((n_items,))] * 2
+        + [dma((n_band,))] * 2,
+        compiler_params=params(collective_id=1, has_side_effects=True),
+    )(table, counts, tok)
 
 
 def project_kernel(core, tok, mean, inv, gain, shift, wq, wk, wv, bq, bv, h1, q, k, v):
@@ -78,7 +244,14 @@
     return jnp.where(lane == spare, jnp.ones_like(q_pair), head_lanes(q_pair, head, lane))
 
 
-def attend_kernel(qt, q, k, v, bias, out, log_total):
+def attend_kernel(qt, q, k, v, bias, cot, out, log_total, cot_rows, send, recv):
+    step = pl.program_id(0)
+
+    @pl.when(step == 0)
+    def _():
+        greet(column_peers())
+        rows_out(cot, cot_rows, send, recv)
+
     rows, lanes = q.shape
     lane_k = lax.broadcasted_iota(jnp.int32, (rows, lanes), 1)
     lane_q = lax.broadcasted_iota(jnp.int32, (qt, lanes), 1)
@@ -99,29 +272,47 @@
             parts.append(part * (1.0 / total))
         out[at, :] = jnp.where(row_out < HEAD_DIM, parts[0], parts[1]).T.astype(bf16)
 
-
-def attend(q, k, v, bias, qt=512):
+    @pl.when(step == pl.num_programs(0) - 1)
+    def _():
+        for band in range(4):
+            rows_out_got(cot, cot_rows, send, recv, band)
+        rows_out_sent(cot, cot_rows, send, recv)
+
+
+def attend(q, k, v, bias, cot, qt=512):
     rows, width = q.shape
     pairs = width // 128
     blk = pl.BlockSpec((rows, 128), lambda i: (0, i))
+    hbm = pl.BlockSpec(memory_space=pltpu.HBM)
     return pl.pallas_call(
         functools.partial(attend_kernel, qt),
         name="attend",
         grid=(pairs,),
-        in_specs=[blk, blk, blk, pl.BlockSpec((rows, 128), lambda i: (0, 0))],
-        out_specs=[blk, pl.BlockSpec((1, 2, rows), lambda i: (i, 0, 0))],
+        in_specs=[blk, blk, blk, pl.BlockSpec((rows, 128), lambda i: (0, 0)), hbm],
+        out_specs=[blk, pl.BlockSpec((1, 2, rows), lambda i: (i, 0, 0)), hbm],
         out_shape=[
             jax.ShapeDtypeStruct((rows, width), bf16),
             jax.ShapeDtypeStruct((pairs, 2, rows), f32),
+            jax.ShapeDtypeStruct((4, cot.shape[1] // 2, cot.shape[2]), bf16),
         ],
-        compiler_params=params(),
+        scratch_shapes=[pltpu.SemaphoreType.DMA((4,))] * 2,
+        compiler_params=params(collective_id=3, has_side_effects=True),
         cost_estimate=pl.CostEstimate(
             flops=16 * rows * rows * width, bytes_accessed=5 * 2**20, transcendentals=0
         ),
-    )(q, k, v, bias)
-
-
-def attend_back_kernel(qt, q, k, v, bias, d_attn, log_total, dq, dk, dv, dk_acc, dv_acc):
+    )(q, k, v, bias, cot)
+
+
+def attend_back_kernel(
+    qt, q, k, v, bias, d_attn, log_total, out_rows, dq, dk, dv, out_home, dk_acc, dv_acc, send, recv
+):
+    step = pl.program_id(0)
+
+    @pl.when(step == 0)
+    def _():
+        greet(column_peers())
+        rows_back(out_rows, out_home, send, recv)
+
     rows, lanes = q.shape
     lane_k = lax.broadcasted_iota(jnp.int32, (rows, lanes), 1)
     lane_q = lax.broadcasted_iota(jnp.int32, (qt, lanes), 1)
@@ -156,11 +347,18 @@
     dk[...] = dk_acc[...].astype(bf16)
     dv[...] = dv_acc[...].astype(bf16)
 
-
-def attend_back(q, k, v, bias, d_attn, log_total, qt=512):
+    @pl.when(step == pl.num_programs(0) - 1)
+    def _():
+        for i in range(4):
+            rows_back_got(out_rows, out_home, send, recv, i)
+        rows_back_sent(out_rows, out_home, send, recv)
+
+
+def attend_back(q, k, v, bias, d_attn, log_total, out_rows, qt=512):
     rows, width = q.shape
     pairs = width // 128
     blk = pl.BlockSpec((rows, 128), lambda i: (0, i))
+    hbm = pl.BlockSpec(memory_space=pltpu.HBM)
     return pl.pallas_call(
         functools.partial(attend_back_kernel, qt),
         name="attend_back",
@@ -172,15 +370,17 @@
             pl.BlockSpec((rows, 128), lambda i: (0, 0)),
             blk,
             pl.BlockSpec((1, 2, rows), lambda i: (i, 0, 0)),
+            hbm,
         ],
-        out_specs=[blk] * 3,
-        out_shape=[jax.ShapeDtypeStruct((rows, width), bf16)] * 3,
-        scratch_shapes=[pltpu.VMEM((rows, 128), f32)] * 2,
-        compiler_params=params(),
+        out_specs=[blk] * 3 + [hbm],
+        out_shape=[jax.ShapeDtypeStruct((rows, width), bf16)] * 3
+        + [jax.ShapeDtypeStruct((2, 2 * out_rows.shape[1], out_rows.shape[2]), bf16)],
+        scratch_shapes=[pltpu.VMEM((rows, 128), f32)] * 2 + [pltpu.SemaphoreType.DMA((4,))] * 2,
+        compiler_params=params(collective_id=5, has_side_effects=True),
         cost_estimate=pl.CostEstimate(
             flops=40 * rows * rows * width, bytes_accessed=8 * 2**20, transcendentals=0
         ),
-    )(q, k, v, bias, d_attn, log_total)
+    )(q, k, v, bias, d_attn, log_total, out_rows)
 
 
 def gelu_and_slope(u):
@@ -193,21 +393,32 @@
     return u * half, slope
 
 
-def mlp_kernel(core, h2, h2p, cot, out_in, dh_in, *refs):
+def mlp_kernel(h2, h2p, cot, res, *refs):
     (wu_a, bu_a, wd_a, wu_b, bu_b, wd_b) = refs[:6]
-    (out, dh, dwd_a, dwu_ak, dwu_as, dbu_a, dwd_b, dwu_bk, dwu_bs, dbu_b) = refs[6:]
+    (out, dh, dwd, dwu_a, dwu_b, dbu_a, dbu_b) = refs[6:13]
+    (send_wd, send_wua, send_wub, got_wd, got_wua, got_wub, keep_a, keep_d, keep_b, send, recv) = refs[13:]
     step = pl.program_id(0)
+    steps = pl.num_programs(0) - 1
     half = h2.shape[1] // 2
+    it, bd, c, yx = place()
+    sibling = (it + 1 - 2 * c, bd)
+    slot = lax.rem(step, 2)
+    before = 1 - slot
+
+    def copies(at):
+        pairs = ((send_wd, got_wd), (send_wua, got_wua), (send_wub, got_wub))
+        return [
+            remote(src.at[at], dst.at[at], send.at[i, at], recv.at[i, at], sibling)
+            for i, (src, dst) in enumerate(pairs)
+        ]
 
     @pl.when(step == 0)
     def _():
-        out[...] = out_in[...]
-        dh[...] = dh_in[...]
-
-    for wu, bu, wd, dwd, dwu_k, dwu_s, dbu in (
-        (wu_a, bu_a, wd_a, dwd_a, dwu_ak, dwu_as, dbu_a),
-        (wu_b, bu_b, wd_b, dwd_b, dwu_bk, dwu_bs, dbu_b),
-    ):
+        greet([sibling])
+        out[...] = res[...]
+        dh[...] = jnp.zeros_like(dh)
+
+    def tile(wu, bu, wd, dbu):
         up = dot(h2[...], wu[...]) + bu[...]
         d_act = dot(cot[...], wd[...], 1, 1)
         act, slope = gelu_and_slope(up)
@@ -215,144 +426,180 @@
         d_up32 = d_act * slope
         d_up = d_up32.astype(bf16)
         dbu[0] = jnp.sum(d_up32, 0, keepdims=True)
-        dwd[0] = dot(cot[...], act, 0, 0).astype(bf16)
+        d_wd = dot(cot[...], act, 0, 0).astype(bf16)
         d_wu = dot(h2p[...], d_up, 0, 0).astype(bf16)
-        dwu_k[0] = d_wu[:half]
-        dwu_s[0] = d_wu[half:]
         out[...] += dot(act, wd[...])
         dh[...] += dot(d_up, wu[...], 1, 1)
-
-
-def mlp(core, h2, h2p, cot, out_in, dh_in, w_up, b_up, w_down, first, steps):
+        return d_wd, d_wu
+
+    @pl.when(step >= 2)
+    def _():
+        for copy in copies(slot):
+            copy.wait_send()
+
+    @pl.when(step < steps)
+    def _():
+        d_wd, d_wu = tile(wu_a, bu_a, wd_a, dbu_a)
+        send_wd[slot] = d_wd
+        send_wua[slot] = d_wu[half:]
+        keep_a[slot] = d_wu[:half]
+
+    @pl.when(step > 0)
+    def _():
+        for copy in copies(before):
+            copy.wait_recv()
+        dwd[0] = keep_d[...] + got_wd[before]
+        dwu_b[0] = keep_b[...] + got_wua[before]
+        dwu_a[0] = keep_a[before] + got_wub[before]
+
+    @pl.when(step < steps)
+    def _():
+        for copy in copies(slot)[:2]:
+            copy.start()
+        d_wd, d_wu = tile(wu_b, bu_b, wd_b, dbu_b)
+        send_wub[slot] = d_wu[half:]
+        copies(slot)[2].start()
+        keep_b[...] = d_wu[:half]
+        keep_d[...] = d_wd
+
+    @pl.when(step == steps)
+    def _():
+        for copy in copies(before):
+            copy.wait_send()
+
+
+def mlp(core, h2, h2p, cot, res, w_up, b_up, w_down):
     rows, width = h2.shape
     ff = w_up.shape[1]
     tile = ff // 8
     half = width // 2
-    whole = pl.BlockSpec((rows, width), lambda i, c: (0, 0))
-    at_a = lambda i, c: 2 * (first + i) + 1 - c[0]
-    at_b = lambda i, c: 2 * (first + i) + c[0]
+    steps = 4
+    vmem = pl.BlockSpec(memory_space=pltpu.VMEM)
+    now = lambda i: jnp.minimum(i, steps - 1)
+    last = lambda i: jnp.maximum(i - 1, 0)
+    at_a = lambda i: 2 * now(i) + 1 - lax.rem(lax.axis_index("items"), 2)
+    at_b = lambda i: 2 * now(i) + lax.rem(lax.axis_index("items"), 2)
     w_specs = []
     for at in (at_a, at_b):
         w_specs += [
-            pl.BlockSpec((width, tile), lambda i, c, at=at: (0, at(i, c))),
-            pl.BlockSpec((1, tile), lambda i, c, at=at: (0, at(i, c))),
-            pl.BlockSpec((tile, width), lambda i, c, at=at: (at(i, c), 0)),
+            pl.BlockSpec((width, tile), lambda i, at=at: (0, at(i))),
+            pl.BlockSpec((1, tile), lambda i, at=at: (0, at(i))),
+            pl.BlockSpec((tile, width), lambda i, at=at: (at(i), 0)),
         ]
-    out_specs = [whole, whole]
-    out_shape = [jax.ShapeDtypeStruct((rows, width), f32)] * 2
-    for _ in range(2):
-        out_specs += [
-            pl.BlockSpec((1, width, tile), lambda i, c: (i, 0, 0)),
-            pl.BlockSpec((1, half, tile), lambda i, c: (i, 0, 0)),
-            pl.BlockSpec((1, half, tile), lambda i, c: (i, 0, 0)),
-            pl.BlockSpec((1, 1, tile), lambda i, c: (i, 0, 0)),
-        ]
-        out_shape += [
-            jax.ShapeDtypeStruct((steps, width, tile), bf16),
-            jax.ShapeDtypeStruct((steps, half, tile), bf16),
-            jax.ShapeDtypeStruct((steps, half, tile), bf16),
-            jax.ShapeDtypeStruct((steps, 1, tile), f32),
-        ]
+    bias = pl.BlockSpec((1, 1, tile), lambda i: (now(i), 0, 0))
+    up_grad = pl.BlockSpec((1, half, tile), lambda i: (last(i), 0, 0))
+    dma = pltpu.SemaphoreType.DMA
     return pl.pallas_call(
         mlp_kernel,
         name="mlp",
-        grid_spec=pltpu.PrefetchScalarGridSpec(
-            num_scalar_prefetch=1,
-            grid=(steps,),
-            in_specs=[whole] * 5 + w_specs,
-            out_specs=out_specs,
+        grid=(steps + 1,),
+        in_specs=[vmem] * 4 + w_specs,
+        out_specs=[
+            vmem,
+            vmem,
+            pl.BlockSpec((1, width, tile), lambda i: (last(i), 0, 0)),
+            up_grad,
+            up_grad,
+            bias,
+            bias,
+        ],
+        out_shape=[jax.ShapeDtypeStruct((rows, width), f32)] * 2
+        + [jax.ShapeDtypeStruct((steps, width, tile), bf16)]
+        + [jax.ShapeDtypeStruct((steps, half, tile), bf16)] * 2
+        + [jax.ShapeDtypeStruct((steps, 1, tile), f32)] * 2,
+        scratch_shapes=(
+            [pltpu.VMEM((2, width, tile), bf16)]
+            + [pltpu.VMEM((2, half, tile), bf16)] * 2
+        )
+        * 2
+        + [
+            pltpu.VMEM((2, half, tile), bf16),
+            pltpu.VMEM((width, tile), bf16),
+            pltpu.VMEM((half, tile), bf16),
+            dma((3, 2)),
+            dma((3, 2)),
+        ],
+        compiler_params=params(collective_id=4, has_side_effects=True),
+        cost_estimate=pl.CostEstimate(
+            flops=2 * 6 * rows * width * ff, bytes_accessed=40 * 2**20, transcendentals=0
         ),
-        out_shape=out_shape,
-        compiler_params=params(),
-        cost_estimate=pl.CostEstimate(
-            flops=2 * 6 * rows * width * 2 * tile * steps, bytes_accessed=20 * 2**20, transcendentals=0
-        ),
-    )(core, h2, h2p, cot, out_in, dh_in, w_up, b_up, w_down, w_up, b_up, w_down)
-
-
-def all_sum_kernel(n_items, n_band, x, total, buf_i, buf_b, part, send_i, recv_i, send_b, recv_b):
-    it = lax.axis_index("items")
-    bd = lax.axis_index("band")
-    barrier = pltpu.get_barrier_semaphore()
-    for o in range(1, n_items):
-        peer = (lax.rem(it + o, n_items), bd)
-        pl.semaphore_signal(barrier, inc=1, device_id=peer, device_id_type=pl.DeviceIdType.MESH)
-    for o in range(1, n_band):
-        peer = (it, lax.rem(bd + o, n_band))
-        pl.semaphore_signal(barrier, inc=1, device_id=peer, device_id_type=pl.DeviceIdType.MESH)
-    pl.semaphore_wait(barrier, n_items + n_band - 2)
-
-    def share(n, rank, peer_of, src, buf, send, recv):
-        copies = []
-        for o in range(1, n):
-            copy = pltpu.make_async_remote_copy(
-                src_ref=src,
-                dst_ref=buf.at[rank],
-                send_sem=send.at[o],
-                recv_sem=recv.at[o],
-                device_id=peer_of(lax.rem(rank + o, n)),
-                device_id_type=pl.DeviceIdType.MESH,
-            )
-            copy.start()
-            copies.append(copy)
-        buf[rank] = src[...]
-        for copy in copies:
-            copy.wait()
-        added = buf[0]
-        for i in range(1, n):
-            added = added + buf[i]
-        return added
-
-    part[...] = share(n_items, it, lambda p: (p, bd), x, buf_i, send_i, recv_i)
+    )(h2, h2p, cot, res, w_up, b_up, w_down, w_up, b_up, w_down)
+
+
+def share(n, rank, peer_of, src, buf, send, recv):
+    copies = []
+    for o in range(1, n):
+        copy = pltpu.make_async_remote_copy(
+            src_ref=src,
+            dst_ref=buf.at[rank],
+            send_sem=send.at[o],
+            recv_sem=recv.at[o],
+            device_id=peer_of(lax.rem(rank + o, n)),
+            device_id_type=pl.DeviceIdType.MESH,
+        )
+        copy.start()
+        copies.append(copy)
+    buf[rank] = src[...]
+    for copy in copies:
+        copy.wait()
+    added = buf[0]
+    for i in range(1, n):
+        added = added + buf[i]
+    return added
+
+
+def finish_kernel(n_items, n_band, patches, table, counts, g_rows, small, tok, batch, inv, d_tok, total, *refs):
+    (got, buf_i, part, buf_b, send_g, recv_g, send_i, recv_i, send_b, recv_b) = refs
+    it, bd, c, yx = place()
+    others = []
+    for o in range(1, n_items // 2):
+        for k in range(2):
+            others.append((lax.rem(yx + o, n_items // 2) * 2 + k, bd))
+    greet(column_peers() + others)
+    rows_back(g_rows, got, send_g, recv_g)
+    part[...] = share(n_items, it, lambda p: (p, bd), small, buf_i, send_i, recv_i)
     total[...] = share(n_band, bd, lambda p: (it, p), part, buf_b, send_b, recv_b)
-
-
-def all_sum(x, collective_id):
+    slots, band_rows, width = tok.shape
+    cut = band_rows // 2
+    scale = inv[...] * patches[0]
+    fix = -0.5 * scale * total[0:1, :]
+    slope = -0.5 * scale * inv[...] * inv[...] * total[1:2, :]
+    at = lax.broadcasted_iota(jnp.int32, (cut, width), 0) + bd * band_rows
+    for q in range(4):
+        s, h = q // 2, q % 2
+        rows_back_got(g_rows, got, send_g, recv_g, q)
+        now = pl.ds(h * cut, cut)
+        valid = at + h * cut < counts[table[it * slots + s]]
+        term = fix + slope * (tok[s, now].astype(f32) - batch[...])
+        d_tok[s, now] = (got[s, now].astype(f32) + jnp.where(valid, term, 0.0)).astype(bf16)
+    rows_back_sent(g_rows, got, send_g, recv_g)
+
+
+def finish(patches, table, counts, g_rows, small, tok, batch, inv):
     n_items, n_band = lax.axis_size("items"), lax.axis_size("band")
     vmem = pl.BlockSpec(memory_space=pltpu.VMEM)
+    smem = pl.BlockSpec(memory_space=pltpu.SMEM)
+    dma = pltpu.SemaphoreType.DMA
     return pl.pallas_call(
-        functools.partial(all_sum_kernel, n_items, n_band),
-        name=f"all_sum_{collective_id}",
-        out_shape=jax.ShapeDtypeStruct(x.shape, f32),
-        in_specs=[vmem],
-        out_specs=vmem,
+        functools.partial(finish_kernel, n_items, n_band),
+        name="finish",
+        in_specs=[smem, smem, smem, pl.BlockSpec(memory_space=pltpu.HBM), vmem, vmem, vmem, vmem],
+        out_specs=[vmem, vmem],
+        out_shape=[
+            jax.ShapeDtypeStruct(tok.shape, bf16),
+            jax.ShapeDtypeStruct(small.shape, f32),
+        ],
         scratch_shapes=[
-            pltpu.VMEM((n_items,) + x.shape, f32),
-            pltpu.VMEM((n_band,) + x.shape, f32),
-            pltpu.VMEM(x.shape, f32),
-            pltpu.SemaphoreType.DMA((n_items,)),
-            pltpu.SemaphoreType.DMA((n_items,)),
-            pltpu.SemaphoreType.DMA((n_band,)),
-            pltpu.SemaphoreType.DMA((n_band,)),
-        ],
-        compiler_params=params(collective_id=collective_id, has_side_effects=True),
-    )(x)
-
-
-def stats_kernel(left, tok, sums):
-    slots, rows, width = tok.shape
-    row = lax.broadcasted_iota(jnp.int32, (rows, width), 0)
-    one = jnp.zeros((1, width), f32)
-    two = jnp.zeros((1, width), f32)
-    for s in range(slots):
-        x = jnp.where(row < left[s], tok[s].astype(f32), 0.0)
-        one = one + jnp.sum(x, 0, keepdims=True)
-        two = two + jnp.sum(x * x, 0, keepdims=True)
-    sums[0:1, :] = one
-    sums[1:2, :] = two
-
-
-def stats(left, tok):
-    width = tok.shape[2]
-    vmem = pl.BlockSpec(memory_space=pltpu.VMEM)
-    return pl.pallas_call(
-        stats_kernel,
-        name="stats",
-        in_specs=[pl.BlockSpec(memory_space=pltpu.SMEM), vmem],
-        out_specs=vmem,
-        out_shape=jax.ShapeDtypeStruct((2, width), f32),
-        compiler_params=params(),
-    )(left, tok)
+            pltpu.VMEM(tok.shape, bf16),
+            pltpu.VMEM((n_items,) + small.shape, f32),
+            pltpu.VMEM(small.shape, f32),
+            pltpu.VMEM((n_band,) + small.shape, f32),
+        ]
+        + [dma((4,))] * 2
+        + [dma((n_items,))] * 2
+        + [dma((n_band,))] * 2,
+        compiler_params=params(collective_id=2, has_side_effects=True),
+    )(patches, table, counts, g_rows, small, tok, batch, inv)
 
 
 def join_kernel(core, attn_a, attn_b, wo_a, wo_b, tok, mean, inv, bo, gain, shift, res, h2, h2p):
@@ -625,35 +872,9 @@
     to_z1 = lambda i, b: (i, b ^ 1)
     to_z2 = lambda i, b: (i, b ^ 2)
 
-    def out_round(r):
-        def to(i, b):
-            q = b ^ r
-            return ((i // 2) * 2 + (q & 1), 2 * (i % 2) + (q >> 1))
-
-        return to
-
-    def back_round(r):
-        there = {out_round(r)(i, b): (i, b) for i, b in devices}
-        return lambda i, b: there[(i, b)]
-
-    def gather_rows(array):
-        blocks = array.reshape(slots * 2, cut, width)
-        return [permute(pick(blocks, bd ^ r), out_round(r)) for r in range(4)]
-
-    def return_rows(rows):
-        blocks = rows.reshape(4, cut, width)
-        got = jnp.stack([permute(blocks[r], back_round(r)) for r in range(4)])
-        return jnp.stack([pick(got, bd ^ q) for q in range(4)]).reshape(slots, band_rows, width)
-
-    counts = patch_counts[slot_table]
-    my_counts = lax.dynamic_slice_in_dim(counts, it * slots, slots)
-    left = my_counts - bd * band_rows
-    item_count = pick(counts, yx * 4 + bd)
-
-    tok_rows = jnp.concatenate(gather_rows(tokens))
-    sums = all_sum(stats(left, tokens), 1)
-    tok_sib = permute(tok_rows, to_core)
-    cot_rows = jnp.concatenate(gather_rows(cotangent))
+    item_count = pick(patch_counts, pick(slot_table, yx * 4 + bd))
+    gathered, sums = gather(slot_table, patch_counts, tokens)
+    tok = gathered.reshape(8 * cut, width)
 
     patch_total = jnp.sum(patch_counts).astype(f32)
     batch_mean = sums[0] / patch_total
@@ -664,44 +885,33 @@
     mean_row, inv_row = new_mean.reshape(1, -1), inverse.reshape(1, -1)
     as_row = lambda a: a.astype(f32).reshape(1, -1)
 
-    round_of = jnp.arange(4 * cut, dtype=jnp.int32) // cut
-    at = jnp.arange(4 * cut, dtype=jnp.int32) % cut
-    base = 2 * lax.rem(bd, 2)
-    own = ((base + c) ^ round_of) * band_rows + c * cut + at
-    sib = ((base + 1 - c) ^ round_of) * band_rows + (1 - c) * cut + at
-    bias = jnp.where(jnp.concatenate([own, sib]) < item_count, 0.0, masked_score).astype(bf16)
+    at = jnp.arange(4 * cut, dtype=jnp.int32)
+    at = (at // cut) * band_rows + at % cut
+    at = jnp.concatenate([at + c * cut, at + (1 - c) * cut])
+    bias = jnp.where(at < item_count, 0.0, masked_score).astype(bf16)
     bias = jnp.broadcast_to(bias[:, None], (8 * cut, 128))
 
-    tok = jnp.concatenate([tok_rows, tok_sib])
     h1, q, k, v = project(
         core, tok, mean_row, inv_row, as_row(ln1_gain), as_row(ln1_bias),
         w_query, w_key, w_value, as_row(b_query), as_row(b_value),
     )
-    attn, log_total = attend(q, k, v, bias)
+    attn, log_total, cot_rows = attend(q, k, v, bias, cotangent)
     rows = 4 * cut
+    cot_rows = cot_rows.reshape(rows, width)
     attn_recv = permute(attn[rows:], to_core)
     res, h2, h2p = join(
         core, attn, attn_recv, w_out, tok, mean_row, inv_row, as_row(b_out), as_row(ln2_gain), as_row(ln2_bias)
     )
-    up_bias = as_row(b_up)
-    zero = jnp.zeros_like(res)
-    d_down_part, d_up_part, d_bias_up = [], [], []
-    total, d_h2 = res, zero
+    total, d_h2, d_down, d_up_a, d_up_b, dbu_a, dbu_b = mlp(
+        core, h2, h2p, cot_rows, res, w_up, as_row(b_up), w_down
+    )
+    d_down_part, d_up_part = [], []
+    down = d_down.reshape(2, 2, width, -1)
+    up = jnp.stack([d_up_a, d_up_b]).reshape(2, 2, 2, 2, 2, -1, d_up_a.shape[-1])
     for j in range(2):
-        (total, d_h2, dwd_a, dwu_ak, dwu_as, dbu_a, dwd_b, dwu_bk, dwu_bs, dbu_b) = mlp(
-            core, h2, h2p, cot_rows, total, d_h2, w_up, up_bias, w_down, 2 * j, 2
-        )
-        d_down = (dwd_b, permute(dwd_a, to_core))
-        got_a, got_b = permute(dwu_as, to_core), permute(dwu_bs, to_core)
-        d_up = (jnp.stack([dwu_ak, dwu_bk]), jnp.stack([got_b, got_a]))
-        d_bias_up.append(jnp.stack([dbu_a, dbu_b]))
-        send = pick(d_down[0], 1 - x) + pick(d_down[1], 1 - x)
-        keep = pick(d_down[0], x) + pick(d_down[1], x)
-        d_down_part.append((keep, permute(send, to_x)))
-        d_up = [a.reshape(2, 2, 2, 2, -1, a.shape[-1]) for a in d_up]
-        send = pick(d_up[0], 1 - y, 2) + pick(d_up[1], 1 - y, 2)
-        keep = pick(d_up[0], y, 2) + pick(d_up[1], y, 2)
-        got = permute(send, to_y)
+        d_down_part.append((pick(down[j], x), permute(pick(down[j], 1 - x), to_x)))
+        got = permute(pick(up[:, j], 1 - y, 2), to_y)
+        keep = pick(up[:, j], y, 2)
         send = pick(keep, 1 - x, 2) + pick(got, 1 - x, 2)
         keep = pick(keep, x, 2) + pick(got, x, 2)
         got = permute(send, to_x)
@@ -740,17 +950,20 @@
         jnp.concatenate([d_w_up[1], d_w_up[0]], 1),
         jnp.concatenate([d_w_up[0], d_w_up[1]], 1),
     )
-    d_bias_up = jnp.stack(d_bias_up)[:, :, :, 0]
-    d_bias_up = jnp.where(c == 0, d_bias_up[:, ::-1], d_bias_up)
-    d_bias_up = d_bias_up.transpose(0, 2, 1, 3).reshape(-1, width)
-
-    output = return_rows((total + as_row(b_down)).astype(bf16))
+    d_bias_up = jnp.where(
+        c == 0,
+        jnp.concatenate([dbu_b[:, 0], dbu_a[:, 0]], 1),
+        jnp.concatenate([dbu_a[:, 0], dbu_b[:, 0]], 1),
+    )
+    out_rows = (total + as_row(b_down)).astype(bf16).reshape(4, cut, width)
 
     d_res, da_own, da_send, dwo_a, dwo_b, sums_two = unjoin(
         core, res, d_h2, cot_rows, as_row(ln2_gain), attn, attn_recv, w_out
     )
     da_recv = permute(da_send, to_core)
-    dq, dk, dv = attend_back(q, k, v, bias, jnp.concatenate([da_own, da_recv]), log_total)
+    dq, dk, dv, output = attend_back(
+        q, k, v, bias, jnp.concatenate([da_own, da_recv]), log_total, out_rows
+    )
     dw, dh1, sums_qv = unproject(core, h1, dq, dk, dv, w_query, w_key, w_value)
 
     dwo = jnp.stack([dwo_a, dwo_b]).reshape(2, 2, 2, -1, width)
@@ -793,27 +1006,23 @@
 
     dh_recv = permute(dh1[rows:], to_core)
     g_rows, sums_one = start_back(tok, mean_row, inv_row, as_row(ln1_gain), dh1, dh_recv, d_res)
-    g_home = return_rows(g_rows)
     empty = jnp.zeros_like(sums_qv)
     halves = jnp.where(
         c == 0,
         jnp.concatenate([sums_qv, empty], 1),
         jnp.concatenate([empty, sums_qv], 1),
     )
-    small = all_sum(jnp.concatenate([sums_one, halves, sums_two, d_bias_up]), 2)
-    sum_g, sum_gx, d_gain_one, d_shift_one, d_bq, d_bv, d_gain_two, d_shift_two, d_bo, d_bdown = (
-        small[i] for i in range(10)
+    d_tokens, small = finish(
+        (1.0 / patch_total).reshape(1), slot_table, patch_counts, g_rows.reshape(4, cut, width),
+        jnp.concatenate([sums_one, halves, sums_two, d_bias_up]), tokens,
+        batch_mean.reshape(1, -1), inv_row,
+    )
+    d_gain_one, d_shift_one, d_bq, d_bv, d_gain_two, d_shift_two, d_bo, d_bdown = (
+        small[i] for i in range(2, 10)
     )
     d_bup = small[10:].reshape(-1)
-    row_keep = (jnp.arange(band_rows, dtype=jnp.int32)[None, :] < left[:, None]).astype(f32)
-    cube = inverse * inverse * inverse
-    fix = -0.5 * inverse * sum_g / patch_total
-    slope = -0.5 * cube * sum_gx / patch_total
-    d_tokens = g_home.astype(f32) + row_keep[:, :, None] * (
-        fix + slope * (tokens.astype(f32) - batch_mean)
-    )
     return (
-        output, d_tokens.astype(bf16), new_mean, new_var, d_gain_one, d_shift_one,
+        output, d_tokens, new_mean, new_var, d_gain_one, d_shift_one,
         d_qkv[0], d_bq, d_qkv[1], d_qkv[2], d_bv, d_w_out, d_bo, d_gain_two, d_shift_two,
         d_w_up, d_bup, d_w_down, d_bdown,
     )

time: 492 us -> 395 us (0.80)
  waiting for transfers between devices: 112 us -> 40.2 us
  starting transfers between devices: 96.5 us -> 26.3 us
  Pallas kernels: 159 us -> 213 us
  other arithmetic: 68.2 us -> 56.5 us
    ppermute x48 -> x25, waiting for transfers between devices: 112 us -> 40.2 us  [permute(): return lax.ppermute(array, ('items', 'band'), pairs)]
    ppermute x48 -> x25, starting transfers between devices: 96.5 us -> 26.3 us  [permute(): return lax.ppermute(array, ('items', 'band'), pairs)]
    pallas_call x5 -> x3, Pallas kernels: 77.5 us -> 119 us  [the longest x1 41.7 us: finish(): pl.pallas_call(functools.partial(finish_kernel, n_items, n_band), name='f...]
    another operation x11 -> x1, other arithmetic: 11.3 us -> 1.88 us  [column_layer(): jnp.stack([d_up_a, d_up_b]).reshape(2, 2, 2, 2, 2, -1, d_up_a.shape[-1])]
    add x7 -> x3, other arithmetic: 10.9 us -> 2.3 us  [the longest x2 2.3 us: column_layer(): send = pick(keep, 1 - x, 2) + pick(got, 1 - x, 2)]
    pallas_call x1, Pallas kernels: 24.9 us -> 32.8 us  [attend_back(): pl.pallas_call(functools.partial(attend_back_kernel, qt), name='attend_ba...]
    dynamic_slice x13 -> x14, local copies, waits for them, and re-layouts: 11.5 us -> 19.1 us  [pick(): return lax.dynamic_index_in_dim(array, index, axis, keepdims=False)]
    pallas_call x1, Pallas kernels: 15.3 us -> 20.2 us  [attend(): pl.pallas_call(functools.partial(attend_kernel, qt), name='attend', grid=...]
  transfers between devices with their start and end apart: 48 -> 25, of which waited for: 14 -> 8; matrix products, arithmetic and copies ran while one was open for 20% -> 20% of each run, Pallas kernels for 22% -> 26%
where the time goes in v2:
time: 395 us; the launch traced here: 388 us
  Pallas kernels  213 us (54%)
  other arithmetic  56.5 us (14%)
  local copies, waits for them, and re-layouts  47.7 us (12%)
  waiting for transfers between devices  40.2 us (10%)
  starting transfers between devices  26.3 us (7%)
  between operations  4.27 us (1%)
    pallas_call x1, Pallas kernels, finish(): pl.pallas_call(functools.partial(finish_kernel, n_items, n_band), name='f...  41.7 us
    pallas_call x1, Pallas kernels, mlp(): pl.pallas_call(mlp_kernel, name='mlp', grid=(steps + 1,), in_specs=[vmem]...  40.8 us
    ppermute x25, waiting for transfers between devices, permute(): return lax.ppermute(array, ('items', 'band'), pairs)  40.2 us
    pallas_call x1, Pallas kernels, gather(): pl.pallas_call(functools.partial(gather_kernel, n_items, n_band), name='g...  36.1 us
    pallas_call x1, Pallas kernels, attend_back(): pl.pallas_call(functools.partial(attend_back_kernel, qt), name='attend_ba...  32.8 us
    ppermute x25, starting transfers between devices, permute(): return lax.ppermute(array, ('items', 'band'), pairs)  26.3 us
    pallas_call x1, Pallas kernels, attend(): pl.pallas_call(functools.partial(attend_kernel, qt), name='attend', grid=...  20.2 us
    dynamic_slice x14, local copies, waits for them, and re-layouts, pick(): return lax.dynamic_index_in_dim(array, index, axis, keepdims=False)  19.1 us
  transfers between devices with their start and end apart: 25, of which 8 were waited for; matrix products, arithmetic and copies ran while one was open for 20% of the time, Pallas kernels for 26%

profile of v2, /device:TPU:0, one launch (start us, length us, event | category | flops | bytes accessed | tf_op | source)
XLA Modules:
  0.0 387.8 jit_solution(14683885132105397657)
XLA Ops:
  6.4 36.1 %gather.1 = (bf16[8,128,1024]{2,1,0:T(8,128)(2,1)}, f32[2,1024]{1,0:T(2,128)}) custom-call(s32[16]{0:T(128)} %table.3, s32[16]{0:T(128)} %counts.3, bf16[2,256,1024]{2,1,0:T(8,128)(2,1)} %tok.3), custom_call_target="tpu_custom_call" | custom-call | tf_op jit(solution)/shard_map/gather/pallas_call | solution.py:172
  51.0 8.1 %project.1 = (bf16[1024,1024]{1,0:T(8,128)(2,1)}, bf16[1024,512]{1,0:T(8,128)(2,1)}, bf16[1024,512]{1,0:T(8,128)(2,1)}, bf16[1024,512]{1,0:T(8,128)(2,1)}) custom-call(s32[1]{0:T(128)} %bitcast.core, bf16[1024,1024]{1,0:T(8,128)(2,1)} %bitcast.213, f32[1,1024]{1,0:T(1,128)} %bitcast.240, f32[1,1024]{1,0:T(1,128)} %bitcast.234, f32[1,1024]{1,0:T(1,128)} %bitcast.248, ...), custom_call_target="tpu_custom_call" | custom-call | flops 3221225472 | bytes 12582912 | tf_op jit(solution)/shard_map/project/pallas_call | solution.py:214
  60.0 20.2 %attend.1 = (bf16[1024,512]{1,0:T(8,128)(2,1)}, f32[4,2,1024]{2,1,0:T(2,128)}, bf16[4,128,1024]{2,1,0:T(8,128)(2,1)}) custom-call(bf16[1024,512]{1,0:T(8,128)(2,1)} %get-tuple-element.57.q, bf16[1024,512]{1,0:T(8,128)(2,1)} %get-tuple-element.58.k, bf16[1024,512]{1,0:T(8,128)(2,1)} %get-tuple-element.59.v, bf16[1024,128]{1,0:T(8,128)(2,1)} %broadcast_in_dim.17.bias, ...), custom_call_target="tpu_custom_call" | custom-call | flops 8589934592 | bytes 5242880 | tf_op jit(solution)/shard_map/attend/pallas_call | solution.py:287
  81.3 2.7 collective-permute-start
  87.3 5.2 %join.1 = (f32[512,1024]{1,0:T(8,128)}, bf16[512,1024]{1,0:T(8,128)(2,1)}, bf16[512,1024]{1,0:T(8,128)(2,1)}) custom-call(s32[1]{0:T(128)} %bitcast.core, bf16[1024,512]{1,0:T(8,128)(2,1)} %get-tuple-element.60.attn_a, bf16[512,512]{1,0:T(8,128)(2,1)} %copy-done.13, bf16[1024,1024]{1,0:T(8,128)(2,1)} %wo_b.3, bf16[1024,1024]{1,0:T(8,128)(2,1)} %wo_b.3, ...), custom_call_target="tpu_custom_call" | custom-call | flops 1073741824 | bytes 8388608 | tf_op jit(solution)/shard_map/join/pallas_call | solution.py:631
  92.5 40.8 %mlp.1 = (f32[512,1024]{1,0:T(8,128)}, f32[512,1024]{1,0:T(8,128)}, bf16[4,1024,512]{2,1,0:T(8,128)(2,1)}, bf16[4,512,512]{2,1,0:T(8,128)(2,1)}, bf16[4,512,512]...) custom-call(bf16[512,1024]{1,0:T(8,128)(2,1)} %get-tuple-element.62.h2, ...), custom_call_target="tpu_custom_call" | custom-call | flops 25769803776 | bytes 41943040 | tf_op jit(solution)/shard_map/mlp/pallas_call | solution.py:492
  147.8 10.5 %unjoin.1 = (f32[512,1024]{1,0:T(8,128)}, bf16[512,512]{1,0:T(8,128)(2,1)}, bf16[512,512]{1,0:T(8,128)(2,1)}, bf16[512,1024]{1,0:T(8,128)(2,1)}, bf16[512,1024]{1,0:T(8,128)(2,1)}, /*index=5*/f32[4,1024]{1,0:T(4,128)}) custom-call(s32[1]{0:T(128)} %bitcast.core, f32[512,1024]{1,0:T(8,128)} %get-tuple-element.61.res, f32[512,1024]{1,0:T(8,128)} %get-tuple-element.65.dh, ...), custom_call_target="tpu_custom_call" | custom-call | flops 2147483648 | bytes 12582912 | tf_op jit(solution)/shard_map/unjoin/pallas_call | solution.py:723
  158.5 2.3 fusion.18
  165.5 32.8 %attend_back.1 = (bf16[1024,512]{1,0:T(8,128)(2,1)}, bf16[1024,512]{1,0:T(8,128)(2,1)}, bf16[1024,512]{1,0:T(8,128)(2,1)}, bf16[2,256,1024]{2,1,0:T(8,128)(2,1)}) custom-call(bf16[1024,512]{1,0:T(8,128)(2,1)} %get-tuple-element.57.q, bf16[1024,512]{1,0:T(8,128)(2,1)} %get-tuple-element.58.k, bf16[1024,512]{1,0:T(8,128)(2,1)} %get-tuple-element.59.v, ...), custom_call_target="tpu_custom_call" | custom-call | flops 21474836480 | bytes 8388608 | tf_op jit(solution)/shard_map/attend_back/pallas_call | solution.py:362
  198.3 12.5 %unproject.1 = (bf16[3,1024,512]{2,1,0:T(8,128)(2,1)}, bf16[1024,1024]{1,0:T(8,128)(2,1)}, f32[2,512]{1,0:T(2,128)}) custom-call(s32[1]{0:T(128)} %bitcast.core, bf16[1024,1024]{1,0:T(8,128)(2,1)} %get-tuple-element.71.h1, bf16[1024,512]{1,0:T(8,128)(2,1)} %get-tuple-element.72.dq.dq_r, bf16[1024,512]{1,0:T(8,128)(2,1)} %get-tuple-element.73.dk.dk_r, ...), custom_call_target="tpu_custom_call" | custom-call | flops 6442450944 | bytes 14680064 | tf_op jit(solution)/shard_map/unproject/pallas_call | solution.py:780
  210.8 3.3 constant_dynamic-slice_fusion.7
  218.8 2.3 slice.77
  221.1 2.3 rev.3
  225.7 2.9 fusion.24
  232.8 4.5 %fusion.8 = (bf16[1,1024,512]{2,1,0:T(8,128)(2,1)}, bf16[1024,512]{1,0:T(8,128)(2,1)}) fusion(s32[]{:T(128)S(6)} %select_n.219, bf16[1,1024,512]{2,1,0:T(8,128)(2,1)} %bitcast.84, bf16[1,1024,512]{2,1,0:T(8,128)(2,1)} %bitcast.86, bf16[1,1024,512]{2,1,0:T(8,128)(2,1)S(1)} %copy-done.4, bf16[1,1024,512]{2,1,0:T(8,128)(2,1)S(1)} %copy-done.5, s32[]{:T(128)S(6)} %select_n.225), kind=kLoop, calls=%fused_computation.37 | loop fusion | flops 3145728 | bytes 6291464 | tf_op jit(solution)/shard_map/add | solution.py:930
  239.4 14.9 %collective-permute-done.16 = bf16[2,2,128,512]{3,2,0,1:T(8,128)(2,1)S(1)} collective-permute-done((bf16[2,2,128,512]{3,2,0,1:T(8,128)(2,1)S(1)}, bf16[2,2,128,512]{3,2,0,1:T(8,128)(2,1)S(1)}, u32[]{:S(2)}, u32[]{:S(2)}) %collective-permute-start.16) | collective-permute-done | bytes 524320 | tf_op jit(solution)/shard_map/ppermute | solution.py:867
  255.8 2.3 collective-permute-start.18
  259.4 2.6 copy.94
  267.8 4.9 %start_back.1 = (bf16[512,1024]{1,0:T(8,128)(2,1)}, f32[4,1024]{1,0:T(4,128)}) custom-call(bf16[1024,1024]{1,0:T(8,128)(2,1)} %bitcast.215, f32[1,1024]{1,0:T(1,128)} %bitcast.242, f32[1,1024]{1,0:T(1,128)} %bitcast.236, f32[1,1024]{1,0:T(1,128)} %bitcast.249, bf16[1024,1024]{1,0:T(8,128)(2,1)} %get-tuple-element.75.dh_a, ...), custom_call_target="tpu_custom_call" | custom-call | flops 4194304 | bytes 8388608 | tf_op jit(solution)/shard_map/start_back/pallas_call | solution.py:828
  275.9 41.7 %finish.1 = (bf16[2,256,1024]{2,1,0:T(8,128)(2,1)}, f32[14,1024]{1,0:T(8,128)}) custom-call(f32[1]{0:T(128)} %bitcast.18.patches, s32[16]{0:T(128)} %table.3, s32[16]{0:T(128)} %counts.3, bf16[4,128,1024]{2,1,0:T(8,128)(2,1)} %bitcast.231, f32[14,1024]{1,0:T(8,128)} %pad_maximum_fusion.1.small, bf16[2,256,1024]{2,1,0:T(8,128)(2,1)} %tok.3, ...), custom_call_target="tpu_custom_call" | custom-call | tf_op jit(solution)/shard_map/finish/pallas_call | solution.py:583
  350.4 7.0 %collective-permute-done.5 = bf16[2,3,128,512]{3,2,1,0:T(8,128)(2,1)} collective-permute-done((bf16[2,3,128,512]{3,2,1,0:T(8,128)(2,1)}, bf16[2,3,128,512]{3,2,1,0:T(8,128)(2,1)}, u32[]{:S(2)}, u32[]{:S(2)}) %collective-permute-start.5) | collective-permute-done | bytes 786464 | tf_op jit(solution)/shard_map/ppermute | solution.py:867
  364.7 8.7 %collective-permute-done.6 = bf16[2,3,128,256]{2,3,1,0:T(8,128)(2,1)S(1)} collective-permute-done((bf16[2,3,128,256]{2,3,1,0:T(8,128)(2,1)}, bf16[2,3,128,256]{2,3,1,0:T(8,128)(2,1)S(1)}, u32[]{:S(2)}, u32[]{:S(2)}) %collective-permute-start.6) | collective-permute-done | bytes 393248 | tf_op jit(solution)/shard_map/ppermute | solution.py:867
  374.0 3.2 collective-permute-done.24
  379.1 4.0 %collective-permute-done.7 = bf16[3,128,256]{1,2,0:T(8,128)(2,1)S(1)} collective-permute-done((bf16[3,128,256]{1,2,0:T(8,128)(2,1)S(1)}, bf16[3,128,256]{1,2,0:T(8,128)(2,1)S(1)}, u32[]{:S(2)}, u32[]{:S(2)}) %collective-permute-start.7) | collective-permute-done | bytes 196640 | tf_op jit(solution)/shard_map/ppermute | solution.py:867
  (191 shorter events, 107.8 us)
Async XLA Ops:
  141.2 89.4 %collective-permute-start.20 = (bf16[1024,512]{1,0:T(8,128)(2,1)}, bf16[1024,512]{1,0:T(8,128)(2,1)}, u32[]{:S(2)}, u32[]{:S(2)}) collective-permute-start(bf16[1024,512]{1,0:T(8,128)(2,1)} %get-tuple-element.165), channel_id=1, source_target_pairs={{0,8},{1,9},{2,10},{3,11},{4,12},{5,13},{6,14},{7,15},{8,0},{9,1},... | collective-permute-start | bytes 3145736 | tf_op jit(solution)/shard_map/ppermute | solution.py:867
  143.3 88.7 %collective-permute-start.21 = (bf16[1024,512]{1,0:T(8,128)(2,1)}, bf16[1024,512]{1,0:T(8,128)(2,1)}, u32[]{:S(2)}, u32[]{:S(2)}) collective-permute-start(bf16[1024,512]{1,0:T(8,128)(2,1)} %get-tuple-element.163), channel_id=1, source_target_pairs={{0,8},{1,9},{2,10},{3,11},{4,12},{5,13},{6,14},{7,15},{8,0},{9,1},... | collective-permute-start | bytes 3145736 | tf_op jit(solution)/shard_map/ppermute | solution.py:867
  145.8 77.6 %collective-permute-start.13 = (bf16[2,2,2,128,512]{4,3,2,1,0:T(8,128)(2,1)}, bf16[2,2,2,128,512]{4,3,2,1,0:T(8,128)(2,1)}, u32[]{:S(2)}, u32[]{:S(2)}) collective-permute-start(bf16[2,2,2,128,512]{4,3,2,1,0:T(8,128)(2,1)} %dynamic-slice_bitcast_fusion.2), channel_id=1, source_target_pairs={{0,16},{1,17},{2,18},{3,19},{4,20},{5,21},{6,22},{7,23},{8,24},{9,... | collective-permute-start | bytes 3145736 | tf_op jit(solution)/shard_map/ppermute | solution.py:867
  146.5 82.1 %collective-permute-start.15 = (bf16[2,2,2,128,512]{4,3,2,1,0:T(8,128)(2,1)}, bf16[2,2,2,128,512]{4,3,2,1,0:T(8,128)(2,1)}, u32[]{:S(2)}, u32[]{:S(2)}) collective-permute-start(bf16[2,2,2,128,512]{4,3,2,1,0:T(8,128)(2,1)} %fusion.3), channel_id=1, source_target_pairs={{0,16},{1,17},{2,18},{3,19},{4,20},{5,21},{6,22},{7,23},{8,24},{9,... | collective-permute-start | bytes 3145736 | tf_op jit(solution)/shard_map/ppermute | solution.py:867
  158.4 5.6 %collective-permute-start.1 = (bf16[512,512]{1,0:T(8,128)(2,1)}, bf16[512,512]{1,0:T(8,128)(2,1)S(1)}, u32[]{:S(2)}, u32[]{:S(2)}) collective-permute-start(bf16[512,512]{1,0:T(8,128)(2,1)} %get-tuple-element.67), channel_id=1, source_target_pairs={{0,4},{1,5},{2,6},{3,7},{4,0},{5,1},{6,2},{7,3},{8,12},{9,13},{10,... | collective-permute-start | bytes 1572872 | tf_op jit(solution)/shard_map/ppermute | solution.py:867
  164.0 51.7 %collective-permute-start.8 = (bf16[2,2,128,1024]{3,2,1,0:T(8,128)(2,1)}, bf16[2,2,128,1024]{3,2,1,0:T(8,128)(2,1)S(1)}, u32[]{:S(2)}, u32[]{:S(2)}) collective-permute-start(bf16[2,2,128,1024]{3,2,1,0:T(8,128)(2,1)} %fusion.12), channel_id=1, source_target_pairs={{0,4},{1,5},{2,6},{3,7},{4,0},{5,1},{6,2},{7,3},{8,12},{9,13},{10,... | collective-permute-start | bytes 3145736 | tf_op jit(solution)/shard_map/ppermute | solution.py:867
  215.7 40.1 %collective-permute-start.3 = (bf16[3,2,2,128,512]{3,4,0,2,1:T(8,128)(2,1)}, bf16[3,2,2,128,512]{3,4,0,2,1:T(8,128)(2,1)S(1)}, u32[]{:S(2)}, u32[]{:S(2)}) collective-permute-start(bf16[3,2,2,128,512]{3,4,0,2,1:T(8,128)(2,1)} %bitcast.24), channel_id=1, source_target_pairs={{0,4},{1,5},{2,6},{3,7},{4,0},{5,1},{6,2},{7,3},{8,12},{9,13},{10,... | collective-permute-start | bytes 4718600 | tf_op jit(solution)/shard_map/ppermute | solution.py:867
  223.4 43.8 %collective-permute-start.2 = (bf16[512,1024]{1,0:T(8,128)(2,1)}, bf16[512,1024]{1,0:T(8,128)(2,1)}, u32[]{:S(2)}, u32[]{:S(2)}) collective-permute-start(bf16[512,1024]{1,0:T(8,128)(2,1)} %slice.77), channel_id=1, source_target_pairs={{0,4},{1,5},{2,6},{3,7},{4,0},{5,1},{6,2},{7,3},{8,12},{9,13},{10,... | collective-permute-start | bytes 3145736 | tf_op jit(solution)/shard_map/ppermute | solution.py:867
  228.5 33.4 %collective-permute-start.14 = (bf16[2,2,128,512]{3,2,0,1:T(8,128)(2,1)}, bf16[2,2,128,512]{3,2,0,1:T(8,128)(2,1)}, u32[]{:S(2)}, u32[]{:S(2)}) collective-permute-start(bf16[2,2,128,512]{3,2,0,1:T(8,128)(2,1)} %copy_add_fusion.2), channel_id=1, source_target_pairs={{0,8},{1,9},{2,10},{3,11},{4,12},{5,13},{6,14},{7,15},{8,0},{9,1},... | collective-permute-start | bytes 1572872 | tf_op jit(solution)/shard_map/ppermute | solution.py:867
  230.6 23.7 %collective-permute-start.16 = (bf16[2,2,128,512]{3,2,0,1:T(8,128)(2,1)S(1)}, bf16[2,2,128,512]{3,2,0,1:T(8,128)(2,1)S(1)}, u32[]{:S(2)}, u32[]{:S(2)}) collective-permute-start(bf16[2,2,128,512]{3,2,0,1:T(8,128)(2,1)S(1)} %copy_add_fusion), channel_id=1, source_target_pairs={{0,8},{1,9},{2,10},{3,11},{4,12},{5,13},{6,14},{7,15},{8,0},{9,1},... | collective-permute-start | bytes 1572872 | tf_op jit(solution)/shard_map/ppermute | solution.py:867
  232.1 33.1 %collective-permute-start.9 = (bf16[2,128,1024]{2,1,0:T(8,128)(2,1)}, bf16[2,128,1024]{2,1,0:T(8,128)(2,1)}, u32[]{:S(2)}, u32[]{:S(2)}) collective-permute-start(bf16[2,128,1024]{2,1,0:T(8,128)(2,1)} %get-tuple-element.157), channel_id=1, source_target_pairs={{0,16},{1,17},{2,18},{3,19},{4,20},{5,21},{6,22},{7,23},{8,24},{9,... | collective-permute-start | bytes 1572872 | tf_op jit(solution)/shard_map/ppermute | solution.py:867
  254.3 86.3 %collective-permute-start.22 = (bf16[1024,512]{1,0:T(8,128)(2,1)}, bf16[1024,512]{1,0:T(8,128)(2,1)}, u32[]{:S(2)}, u32[]{:S(2)}) collective-permute-start(bf16[1024,512]{1,0:T(8,128)(2,1)} %get-tuple-element.151), channel_id=1, source_target_pairs={{0,16},{1,17},{2,18},{3,19},{4,20},{5,21},{6,22},{7,23},{8,24},{9,... | collective-permute-start | bytes 3145736 | tf_op jit(solution)/shard_map/ppermute | solution.py:867
  255.8 73.1 %collective-permute-start.18 = (bf16[2,128,512]{2,1,0:T(8,128)(2,1)}, bf16[2,128,512]{2,1,0:T(8,128)(2,1)}, u32[]{:S(2)}, u32[]{:S(2)}) collective-permute-start(bf16[2,128,512]{2,1,0:T(8,128)(2,1)} %get-tuple-element.172), channel_id=1, source_target_pairs={{0,1},{1,0},{2,3},{3,2},{4,5},{5,4},{6,7},{7,6},{8,9},{9,8},{10,11... | collective-permute-start | bytes 786440 | tf_op jit(solution)/shard_map/ppermute | solution.py:867
  261.9 75.2 %collective-permute-start.4 = (bf16[2,3,2,128,512]{4,3,2,1,0:T(8,128)(2,1)}, bf16[2,3,2,128,512]{4,3,2,1,0:T(8,128)(2,1)}, u32[]{:S(2)}, u32[]{:S(2)}) collective-permute-start(bf16[2,3,2,128,512]{4,3,2,1,0:T(8,128)(2,1)} %bitcast.227), channel_id=1, source_target_pairs={{0,8},{1,9},{2,10},{3,11},{4,12},{5,13},{6,14},{7,15},{8,0},{9,1},... | collective-permute-start | bytes 4718600 | tf_op jit(solution)/shard_map/ppermute | solution.py:867
  265.2 63.6 %collective-permute-start.17 = (bf16[2,128,512]{2,1,0:T(8,128)(2,1)}, bf16[2,128,512]{2,1,0:T(8,128)(2,1)}, u32[]{:S(2)}, u32[]{:S(2)}) collective-permute-start(bf16[2,128,512]{2,1,0:T(8,128)(2,1)} %fusion.36), channel_id=1, source_target_pairs={{0,1},{1,0},{2,3},{3,2},{4,5},{5,4},{6,7},{7,6},{8,9},{9,8},{10,11... | collective-permute-start | bytes 786440 | tf_op jit(solution)/shard_map/ppermute | solution.py:867
  267.2 52.1 %collective-permute-start.10 = (bf16[128,1024]{1,0:T(8,128)(2,1)}, bf16[128,1024]{1,0:T(8,128)(2,1)}, u32[]{:S(2)}, u32[]{:S(2)}) collective-permute-start(bf16[128,1024]{1,0:T(8,128)(2,1)} %get-tuple-element.176), channel_id=1, source_target_pairs={{0,8},{1,9},{2,10},{3,11},{4,12},{5,13},{6,14},{7,15},{8,0},{9,1},... | collective-permute-start | bytes 786440 | tf_op jit(solution)/shard_map/ppermute | solution.py:867
  322.2 5.8 %collective-permute-start.11 = (bf16[128,2,256]{0,2,1:T(8,128)(2,1)S(1)}, bf16[128,2,256]{0,2,1:T(8,128)(2,1)S(1)}, u32[]{:S(2)}, u32[]{:S(2)}) collective-permute-start(bf16[128,2,256]{0,2,1:T(8,128)(2,1)S(1)} %get-tuple-element.182), channel_id=1, source_target_pairs={{0,1},{1,0},{2,3},{3,2},{4,5},{5,4},{6,7},{7,6},{8,9},{9,8},{10,11... | collective-permute-start | bytes 393224 | tf_op jit(solution)/shard_map/ppermute | solution.py:867
  328.0 5.5 %collective-permute-start.12 = (bf16[128,256]{0,1:T(8,128)(2,1)S(1)}, bf16[128,256]{0,1:T(8,128)(2,1)S(1)}, u32[]{:S(2)}, u32[]{:S(2)}) collective-permute-start(bf16[128,256]{0,1:T(8,128)(2,1)S(1)} %fusion.38), channel_id=1, source_target_pairs={{0,2},{1,3},{2,0},{3,1},{4,6},{5,7},{6,4},{7,5},{8,10},{9,11},{10,... | collective-permute-start | bytes 196616 | tf_op jit(solution)/shard_map/ppermute | solution.py:867
  330.7 14.9 %collective-permute-start.19 = (bf16[2,128,512]{2,1,0:T(8,128)(2,1)}, bf16[2,128,512]{2,1,0:T(8,128)(2,1)}, u32[]{:S(2)}, u32[]{:S(2)}) collective-permute-start(bf16[2,128,512]{2,1,0:T(8,128)(2,1)} %fusion.28), channel_id=1, source_target_pairs={{0,2},{1,3},{2,0},{3,1},{4,6},{5,7},{6,4},{7,5},{8,10},{9,11},{10,... | collective-permute-start | bytes 786440 | tf_op jit(solution)/shard_map/ppermute | solution.py:867
  339.3 18.1 %collective-permute-start.5 = (bf16[2,3,128,512]{3,2,1,0:T(8,128)(2,1)}, bf16[2,3,128,512]{3,2,1,0:T(8,128)(2,1)}, u32[]{:S(2)}, u32[]{:S(2)}) collective-permute-start(bf16[2,3,128,512]{3,2,1,0:T(8,128)(2,1)} %bitcast_add_fusion), channel_id=1, source_target_pairs={{0,16},{1,17},{2,18},{3,19},{4,20},{5,21},{6,22},{7,23},{8,24},{9,... | collective-permute-start | bytes 2359304 | tf_op jit(solution)/shard_map/ppermute | solution.py:867
  343.2 18.0 %collective-permute-start.23 = (bf16[2,256,512]{1,2,0:T(8,128)(2,1)}, bf16[2,256,512]{1,2,0:T(8,128)(2,1)}, u32[]{:S(2)}, u32[]{:S(2)}) collective-permute-start(bf16[2,256,512]{1,2,0:T(8,128)(2,1)} %add_bitcast_fusion), channel_id=1, source_target_pairs={{0,1},{1,0},{2,3},{3,2},{4,5},{5,4},{6,7},{7,6},{8,9},{9,8},{10,11... | collective-permute-start | bytes 1572872 | tf_op jit(solution)/shard_map/ppermute | solution.py:867
  359.7 13.7 %collective-permute-start.6 = (bf16[2,3,128,256]{2,3,1,0:T(8,128)(2,1)}, bf16[2,3,128,256]{2,3,1,0:T(8,128)(2,1)S(1)}, u32[]{:S(2)}, u32[]{:S(2)}) collective-permute-start(bf16[2,3,128,256]{2,3,1,0:T(8,128)(2,1)} %get-tuple-element.167), channel_id=1, source_target_pairs={{0,1},{1,0},{2,3},{3,2},{4,5},{5,4},{6,7},{7,6},{8,9},{9,8},{10,11... | collective-permute-start | bytes 1179656 | tf_op jit(solution)/shard_map/ppermute | solution.py:867
  362.9 14.3 %collective-permute-start.24 = (bf16[256,512]{0,1:T(8,128)(2,1)}, bf16[256,512]{0,1:T(8,128)(2,1)S(1)}, u32[]{:S(2)}, u32[]{:S(2)}) collective-permute-start(bf16[256,512]{0,1:T(8,128)(2,1)} %fusion.35), channel_id=1, source_target_pairs={{0,2},{1,3},{2,0},{3,1},{4,6},{5,7},{6,4},{7,5},{8,10},{9,11},{10,... | collective-permute-start | bytes 786440 | tf_op jit(solution)/shard_map/ppermute | solution.py:867
  373.4 9.6 %collective-permute-start.7 = (bf16[3,128,256]{1,2,0:T(8,128)(2,1)S(1)}, bf16[3,128,256]{1,2,0:T(8,128)(2,1)S(1)}, u32[]{:S(2)}, u32[]{:S(2)}) collective-permute-start(bf16[3,128,256]{1,2,0:T(8,128)(2,1)S(1)} %fusion.37), channel_id=1, source_target_pairs={{0,2},{1,3},{2,0},{3,1},{4,6},{5,7},{6,4},{7,5},{8,10},{9,11},{10,... | collective-permute-start | bytes 589832 | tf_op jit(solution)/shard_map/ppermute | solution.py:867
  (34 other events, 272.6 us)

commit v3 on v0

--- a/solution.py
+++ b/solution.py
@@ -1,16 +1,1044 @@
+import functools
 import jax
 import jax.numpy as jnp
 from jax import lax
+from jax.experimental import pallas as pl
+from jax.experimental.pallas import tpu as pltpu
 from jax.sharding import PartitionSpec as P
 
 HEADS = 16
 HEAD_DIM = 64
-
-
 epsilon = 1e-05
 score_scale = 0.125
 masked_score = -1e30
 momentum = 0.5
+f32 = jnp.float32
+bf16 = jnp.bfloat16
+VMEM_LIMIT = 60 * 2**20
+R_MEAN, R_VAR, R_G1, R_S1, R_BQ, R_BV, R_BO, R_G2, R_S2, R_BD, R_BU = range(11)
+S_MEAN, S_VAR, S_BATCH, S_INV = range(4)
+
+
+def dot(a, b, ca=1, cb=0):
+    return lax.dot_general(a, b, (((ca,), (cb,)), ((), ())), preferred_element_type=f32)
+
+
+def params(**kw):
+    return pltpu.CompilerParams(vmem_limit_bytes=VMEM_LIMIT, **kw)
+
+
+def place():
+    it, bd = lax.axis_index("items"), lax.axis_index("band")
+    return it, bd, lax.rem(it, 2), it // 2
+
+
+def remote(src, dst, send, recv, to):
+    return pltpu.make_async_remote_copy(
+        src_ref=src,
+        dst_ref=dst,
+        send_sem=send,
+        recv_sem=recv,
+        device_id=to,
+        device_id_type=pl.DeviceIdType.MESH,
+    )
+
+
+def greet(peers):
+    barrier = pltpu.get_barrier_semaphore()
+    for peer in peers:
+        pl.semaphore_signal(barrier, inc=1, device_id=peer, device_id_type=pl.DeviceIdType.MESH)
+    pl.semaphore_wait(barrier, len(peers))
+
+
+def column_peers():
+    it, bd, c, yx = place()
+    peers = [(it, lax.rem(bd + o, 4)) for o in range(1, 4)]
+    return peers + [(it + 1 - 2 * c, lax.rem(bd + o, 4)) for o in range(4)]
+
+
+def rows_out(src, dst, send, recv):
+    it, bd, c, yx = place()
+    cut = src.shape[1] // 2
+    for q in range(4):
+        s, h = q // 2, q % 2
+        block = src.at[s, pl.ds(h * cut, cut)]
+        target = dst.at[bd]
+        own = (c == h) & (bd == 2 * c + s)
+
+        @pl.when(own)
+        def _():
+            pltpu.make_async_copy(block, target, recv.at[bd]).start()
+
+        @pl.when(jnp.logical_not(own))
+        def _():
+            remote(block, target, send.at[q], recv.at[bd], (yx * 2 + h, 2 * c + s)).start()
+
+
+def rows_out_sent(src, dst, send, recv):
+    it, bd, c, yx = place()
+    cut = src.shape[1] // 2
+    for q in range(4):
+        s, h = q // 2, q % 2
+        own = (c == h) & (bd == 2 * c + s)
+
+        @pl.when(jnp.logical_not(own))
+        def _():
+            block = src.at[s, pl.ds(h * cut, cut)]
+            remote(block, dst.at[bd], send.at[q], recv.at[bd], (yx * 2 + h, 2 * c + s)).wait_send()
+
+
+def rows_out_got(src, dst, send, recv, band):
+    it, bd, c, yx = place()
+    cut = src.shape[1] // 2
+    pltpu.make_async_copy(src.at[0, pl.ds(0, cut)], dst.at[band], recv.at[band]).wait()
+
+
+def rows_back(src, dst, send, recv):
+    it, bd, c, yx = place()
+    cut = src.shape[1]
+    home = bd // 2
+    s = lax.rem(bd, 2)
+    target = dst.at[s, pl.ds(pl.multiple_of(c * cut, cut), cut)]
+    got = recv.at[2 * s + c]
+    for r in range(4):
+        own = (home == c) & (bd == r)
+
+        @pl.when(own)
+        def _():
+            pltpu.make_async_copy(src.at[r], target, got).start()
+
+        @pl.when(jnp.logical_not(own))
+        def _():
+            remote(src.at[r], target, send.at[r], got, (yx * 2 + home, r)).start()
+
+
+def rows_back_sent(src, dst, send, recv):
+    it, bd, c, yx = place()
+    cut = src.shape[1]
+    home = bd // 2
+    for r in range(4):
+        own = (home == c) & (bd == r)
+
+        @pl.when(jnp.logical_not(own))
+        def _():
+            target = dst.at[0, pl.ds(0, cut)]
+            remote(src.at[r], target, send.at[r], recv.at[0], (yx * 2 + home, r)).wait_send()
+
+
+def rows_back_got(src, dst, send, recv, q):
+    cut = src.shape[1]
+    s, h = q // 2, q % 2
+    pltpu.make_async_copy(src.at[0], dst.at[s, pl.ds(h * cut, cut)], recv.at[q]).wait()
+
+
+def share_start(n, rank, peer_of, src, buf, send, recv):
+    copies = []
+    for o in range(1, n):
+        to = peer_of(lax.rem(rank + o, n))
+        copies.append(remote(src, buf.at[rank], send.at[o], recv.at[o], to))
+        copies[-1].start()
+    buf[rank] = src[...]
+    return copies
+
+
+def share_end(n, copies, buf):
+    for copy in copies:
+        copy.wait()
+    added = buf[0]
+    for i in range(1, n):
+        added = added + buf[i]
+    return added
+
+
+def all_peers(n_items):
+    it, bd, c, yx = place()
+    others = []
+    for o in range(1, n_items // 2):
+        for k in range(2):
+            others.append((lax.rem(yx + o, n_items // 2) * 2 + k, bd))
+    return column_peers() + others
+
+
+def gather_kernel(n_items, n_band, table, counts, vecs, tok, rows, stat, one, buf_i, part, buf_b, *sems):
+    (send_t, recv_t, send_s, recv_s, send_i, recv_i, send_b, recv_b) = sems
+    it, bd, c, yx = place()
+    sibling = (it + 1 - 2 * c, bd)
+    greet(all_peers(n_items))
+    rows_out(tok, rows, send_t, recv_t)
+    slots, band_rows, width = tok.shape
+    at = lax.broadcasted_iota(jnp.int32, (band_rows, width), 0) + bd * band_rows
+    first = jnp.zeros((1, width), f32)
+    second = jnp.zeros((1, width), f32)
+    for s in range(slots):
+        x = jnp.where(at < counts[table[it * slots + s]], tok[s].astype(f32), 0.0)
+        first = first + jnp.sum(x, 0, keepdims=True)
+        second = second + jnp.sum(x * x, 0, keepdims=True)
+    one[0:1, :] = first
+    one[1:2, :] = second
+    copies = share_start(n_items, it, lambda p: (p, bd), one, buf_i, send_i, recv_i)
+    part[...] = share_end(n_items, copies, buf_i)
+    copies = share_start(n_band, bd, lambda p: (it, p), part, buf_b, send_b, recv_b)
+    sums = share_end(n_band, copies, buf_b) / patch_total(counts, (1, width))
+    mean = sums[0:1]
+    var = sums[1:2] - mean * mean
+    new_var = momentum * vecs[R_VAR : R_VAR + 1, :] + momentum * var
+    stat[S_MEAN : S_MEAN + 1, :] = momentum * vecs[R_MEAN : R_MEAN + 1, :] + momentum * mean
+    stat[S_VAR : S_VAR + 1, :] = new_var
+    stat[S_BATCH : S_BATCH + 1, :] = mean
+    stat[S_INV : S_INV + 1, :] = lax.rsqrt(new_var + epsilon)
+    hand = []
+    for o in range(4):
+        band = lax.rem(bd + o, 4)
+        rows_out_got(tok, rows, send_t, recv_t, band)
+        copy = remote(rows.at[band], rows.at[4 + band], send_s.at[o], recv_s.at[o], sibling)
+        copy.start()
+        hand.append(copy)
+    for copy in hand:
+        copy.wait()
+    rows_out_sent(tok, rows, send_t, recv_t)
+
+
+def patch_total(counts, shape):
+    total = counts[0]
+    for i in range(1, counts.shape[0]):
+        total = total + counts[i]
+    return jnp.full(shape, total, jnp.int32).astype(f32)
+
+
+VMEM = pl.BlockSpec(memory_space=pltpu.VMEM)
+SMEM = pl.BlockSpec(memory_space=pltpu.SMEM)
+HBM = pl.BlockSpec(memory_space=pltpu.HBM)
+DMA = pltpu.SemaphoreType.DMA
+
+
+def gather(table, counts, vecs, tok):
+    n_items, n_band = lax.axis_size("items"), lax.axis_size("band")
+    slots, band_rows, width = tok.shape
+    return pl.pallas_call(
+        functools.partial(gather_kernel, n_items, n_band),
+        name="gather",
+        in_specs=[SMEM, SMEM, VMEM, VMEM],
+        out_specs=[HBM, VMEM],
+        out_shape=[
+            jax.ShapeDtypeStruct((8, band_rows // 2, width), bf16),
+            jax.ShapeDtypeStruct((4, width), f32),
+        ],
+        scratch_shapes=[
+            pltpu.VMEM((2, width), f32),
+            pltpu.VMEM((n_items, 2, width), f32),
+            pltpu.VMEM((2, width), f32),
+            pltpu.VMEM((n_band, 2, width), f32),
+        ]
+        + [DMA((4,))] * 4
+        + [DMA((n_items,))] * 2
+        + [DMA((n_band,))] * 2,
+        compiler_params=params(collective_id=1, has_side_effects=True),
+    )(table, counts, vecs, tok)
+
+
+def half_lanes(ref, row, half):
+    at = pl.multiple_of(lax.rem(lax.axis_index("items"), 2) * half, 128)
+    return ref[row : row + 1, pl.ds(at, half)]
+
+
+def project_kernel(stat, vecs, tok, wq, wk, wv, h1, q, k, v):
+    half = q.shape[1]
+    start = (tok[...].astype(f32) - stat[S_MEAN : S_MEAN + 1, :]) * stat[S_INV : S_INV + 1, :]
+    centre = start - jnp.mean(start, -1, keepdims=True)
+    spread = jnp.mean(centre * centre, -1, keepdims=True)
+    h = centre * lax.rsqrt(spread + epsilon) * vecs[R_G1 : R_G1 + 1, :] + vecs[R_S1 : R_S1 + 1, :]
+    h = h.astype(bf16)
+    h1[...] = h
+    q[...] = ((dot(h, wq[...]) + half_lanes(vecs, R_BQ, half)).astype(bf16) * score_scale).astype(bf16)
+    k[...] = dot(h, wk[...]).astype(bf16)
+    v[...] = (dot(h, wv[...]) + half_lanes(vecs, R_BV, half)).astype(bf16)
+
+
+def project(stat, vecs, tok, wq, wk, wv, block=256):
+    rows, width = tok.shape
+    half = width // 2
+    w = pl.BlockSpec((width, half), lambda i: (0, lax.rem(lax.axis_index("items"), 2)))
+    full = pl.BlockSpec((block, width), lambda i: (i, 0))
+    part = pl.BlockSpec((block, half), lambda i: (i, 0))
+    return pl.pallas_call(
+        project_kernel,
+        name="project",
+        grid=(rows // block,),
+        in_specs=[VMEM, VMEM, full, w, w, w],
+        out_specs=[full] + [part] * 3,
+        out_shape=[jax.ShapeDtypeStruct((rows, width), bf16)]
+        + [jax.ShapeDtypeStruct((rows, half), bf16)] * 3,
+        compiler_params=params(),
+        cost_estimate=pl.CostEstimate(
+            flops=6 * rows * width * half, bytes_accessed=12 * 2**20, transcendentals=0
+        ),
+    )(stat, vecs, tok, wq, wk, wv)
+
+
+def head_lanes(array, head, lane):
+    keep = (lane >= head * HEAD_DIM) & (lane < (head + 1) * HEAD_DIM)
+    return jnp.where(keep, array, jnp.zeros_like(array))
+
+
+def with_spare(array, spare_value, head, lane):
+    spare = (1 - head) * HEAD_DIM
+    return jnp.where(lane == spare, spare_value, head_lanes(array, head, lane))
+
+
+def ones_beside(array, head, lane):
+    return with_spare(array, jnp.ones_like(array), head, lane)
+
+
+def key_bias(table, counts, shape):
+    it, bd, c, yx = place()
+    cut = shape[0] // 8
+    row = lax.broadcasted_iota(jnp.int32, shape, 0)
+    there = row >= 4 * cut
+    row = jnp.where(there, row - 4 * cut, row)
+    band = row // cut
+    half = jnp.where(there, 1 - c, c)
+    position = band * (2 * cut) + half * cut + (row - band * cut)
+    return jnp.where(position < counts[table[yx * 4 + bd]], 0.0, masked_score).astype(bf16)
+
+
+def attend_kernel(qt, table, counts, q, k, v, cot, out, log_total, cot_rows, out_sib, part_sib, *sems):
+    (send, recv, send_s, recv_s) = sems
+    step = pl.program_id(0)
+    rows, lanes = q.shape
+    own = rows // 2
+    it, bd, c, yx = place()
+    sibling = (it + 1 - 2 * c, bd)
+
+    @pl.when(step == 0)
+    def _():
+        greet(column_peers())
+        rows_out(cot, cot_rows, send, recv)
+
+    lane_k = lax.broadcasted_iota(jnp.int32, (rows, lanes), 1)
+    lane_q = lax.broadcasted_iota(jnp.int32, (qt, lanes), 1)
+    row_out = lax.broadcasted_iota(jnp.int32, (lanes, qt), 0)
+    bias = key_bias(table, counts, (rows, lanes))
+    keys = [with_spare(k[...], bias, hd, lane_k) for hd in range(2)]
+    values = [ones_beside(v[...], hd, lane_k).T for hd in range(2)]
+    for t in range(rows // qt):
+        at = slice(t * qt, (t + 1) * qt)
+        scores = [dot(keys[hd], ones_beside(q[at, :], hd, lane_q), 1, 1) for hd in range(2)]
+        tops = [jnp.max(s, 0, keepdims=True) for s in scores]
+        weights = [jnp.exp(s - top).astype(bf16) for s, top in zip(scores, tops)]
+        parts = []
+        for hd in range(2):
+            part = dot(values[hd], weights[hd])
+            spare = (1 - hd) * HEAD_DIM
+            total = part[spare : spare + 1, :]
+            log_total[0, hd : hd + 1, at] = tops[hd] + jnp.log(total)
+            parts.append(part * (1.0 / total))
+        both = jnp.where(row_out < HEAD_DIM, parts[0], parts[1]).T.astype(bf16)
+        if t * qt < own:
+            out[at, :] = both
+        else:
+            part_sib[step, t * qt - own : (t + 1) * qt - own, :] = both
+
+    def hand(i):
+        return remote(
+            part_sib.at[i],
+            out_sib.at[:, pl.ds(pl.multiple_of(i * lanes, lanes), lanes)],
+            send_s.at[i],
+            recv_s.at[i],
+            sibling,
+        )
+
+    hand(step).start()
+
+    @pl.when(step == pl.num_programs(0) - 1)
+    def _():
+        for i in range(part_sib.shape[0]):
+            hand(i).wait()
+        for band in range(4):
+            rows_out_got(cot, cot_rows, send, recv, band)
+        rows_out_sent(cot, cot_rows, send, recv)
+
+
+def attend(table, counts, q, k, v, cot, qt=512):
+    rows, width = q.shape
+    pairs = width // 128
+    blk = pl.BlockSpec((rows, 128), lambda i: (0, i))
+    return pl.pallas_call(
+        functools.partial(attend_kernel, qt),
+        name="attend",
+        grid=(pairs,),
+        in_specs=[SMEM, SMEM, blk, blk, blk, HBM],
+        out_specs=[
+            pl.BlockSpec((rows // 2, 128), lambda i: (0, i)),
+            pl.BlockSpec((1, 2, rows), lambda i: (i, 0, 0)),
+            HBM,
+            HBM,
+        ],
+        out_shape=[
+            jax.ShapeDtypeStruct((rows // 2, width), bf16),
+            jax.ShapeDtypeStruct((pairs, 2, rows), f32),
+            jax.ShapeDtypeStruct((4, cot.shape[1] // 2, cot.shape[2]), bf16),
+            jax.ShapeDtypeStruct((rows // 2, width), bf16),
+        ],
+        scratch_shapes=[pltpu.VMEM((pairs, rows // 2, 128), bf16)]
+        + [DMA((4,))] * 2
+        + [DMA((pairs,))] * 2,
+        compiler_params=params(collective_id=3, has_side_effects=True),
+        cost_estimate=pl.CostEstimate(
+            flops=16 * rows * rows * width, bytes_accessed=5 * 2**20, transcendentals=0
+        ),
+    )(table, counts, q, k, v, cot)
+
+
+def half_rows(ref, which, half):
+    return ref[pl.ds(pl.multiple_of(which * half, 128), half), :]
+
+
+def join_kernel(stat, vecs, attn_a, attn_b, wo, tok, res, h2, h2p):
+    it, bd, c, yx = place()
+    half = attn_a.shape[1]
+    start = (tok[...].astype(f32) - stat[S_MEAN : S_MEAN + 1, :]) * stat[S_INV : S_INV + 1, :]
+    r = dot(attn_a[...], half_rows(wo, c, half)) + dot(attn_b[...], half_rows(wo, 1 - c, half))
+    r = start + r + vecs[R_BO : R_BO + 1, :]
+    res[...] = r
+    centre = r - jnp.mean(r, -1, keepdims=True)
+    spread = jnp.mean(centre * centre, -1, keepdims=True)
+    h = centre * lax.rsqrt(spread + epsilon) * vecs[R_G2 : R_G2 + 1, :] + vecs[R_S2 : R_S2 + 1, :]
+    h = h.astype(bf16)
+    h2[...] = h
+    width = h.shape[1] // 8
+    for x in range(4):
+        first = h[:, 2 * x * width : (2 * x + 1) * width]
+        second = h[:, (2 * x + 1) * width : (2 * x + 2) * width]
+        h2p[:, x * width : (x + 1) * width] = jnp.where(c == 0, first, second)
+        h2p[:, half + x * width : half + (x + 1) * width] = jnp.where(c == 0, second, first)
+
+
+def join(stat, vecs, attn, attn_sib, w_out, tok, block=256):
+    rows, half = attn.shape
+    width = 2 * half
+    act = pl.BlockSpec((block, half), lambda i: (i, 0))
+    full = pl.BlockSpec((block, width), lambda i: (i, 0))
+    return pl.pallas_call(
+        join_kernel,
+        name="join",
+        grid=(rows // block,),
+        in_specs=[VMEM, VMEM, act, act, VMEM, full],
+        out_specs=[full] * 3,
+        out_shape=[
+            jax.ShapeDtypeStruct((rows, width), f32),
+            jax.ShapeDtypeStruct((rows, width), bf16),
+            jax.ShapeDtypeStruct((rows, width), bf16),
+        ],
+        compiler_params=params(),
+        cost_estimate=pl.CostEstimate(
+            flops=2 * rows * width * width, bytes_accessed=8 * 2**20, transcendentals=0
+        ),
+    )(stat, vecs, attn, attn_sib, w_out, tok)
+
+
+def gelu_and_slope(u):
+    u2 = u * u
+    t = jnp.tanh(u * (0.7978845608028654 + (0.7978845608028654 * 0.044715) * u2))
+    half = 0.5 + 0.5 * t
+    slope = half * (
+        1.0 + u * (1.0 - t) * (0.7978845608028654 + (3 * 0.7978845608028654 * 0.044715) * u2)
+    )
+    return u * half, slope
+
+
+def mlp_kernel(vecs, h2, h2p, cot, res, *refs):
+    (wu_a, wd_a, wu_b, wd_b) = refs[:4]
+    (out_low, dh, dwd, dwu_a, dwu_b, dbu_a, dbu_b) = refs[4:11]
+    (send_wd, send_wua, send_wub, got_wd, got_wua, got_wub, keep_a, keep_d, keep_b, out) = refs[11:21]
+    (send, recv) = refs[21:]
+    step = pl.program_id(0)
+    steps = pl.num_programs(0) - 1
+    half = h2.shape[1] // 2
+    it, bd, c, yx = place()
+    sibling = (it + 1 - 2 * c, bd)
+    slot = lax.rem(step, 2)
+    before = 1 - slot
+
+    def copies(at, which=(0, 1, 2)):
+        pairs = ((send_wd, got_wd), (send_wua, got_wua), (send_wub, got_wub))
+        return [
+            remote(pairs[i][0].at[at], pairs[i][1].at[at], send.at[i, at], recv.at[i, at], sibling)
+            for i in which
+        ]
+
+    @pl.when(step == 0)
+    def _():
+        greet([sibling])
+        out[...] = res[...]
+        dh[...] = jnp.zeros_like(dh)
+
+    def tile(wu, wd, dbu, which):
+        lanes = pl.ds(pl.multiple_of(which * wu.shape[1], 128), wu.shape[1])
+        up = dot(h2[...], wu[...]) + vecs[pl.ds(R_BU + step, 1), lanes]
+        d_act = dot(cot[...], wd[...], 1, 1)
+        act, slope = gelu_and_slope(up)
+        act = act.astype(bf16)
+        d_up32 = d_act * slope
+        d_up = d_up32.astype(bf16)
+        dbu[0] = jnp.sum(d_up32, 0, keepdims=True)
+        d_wd = dot(cot[...], act, 0, 0).astype(bf16)
+        d_wu = dot(h2p[...], d_up, 0, 0).astype(bf16)
+        out[...] += dot(act, wd[...])
+        dh[...] += dot(d_up, wu[...], 1, 1)
+        return d_wd, d_wu
+
+    @pl.when(step >= 2)
+    def _():
+        for copy in copies(slot):
+            copy.wait_send()
+
+    @pl.when(step < steps)
+    def _():
+        d_wd, d_wu = tile(wu_a, wd_a, dbu_a, 1 - c)
+        send_wd[slot] = d_wd
+        send_wua[slot] = d_wu[half:]
+        keep_a[slot] = d_wu[:half]
+
+    @pl.when(step > 0)
+    def _():
+        for copy in copies(before):
+            copy.wait_recv()
+        dwd[0] = keep_d[...] + got_wd[before]
+        dwu_b[0] = keep_b[...] + got_wua[before]
+        dwu_a[0] = keep_a[before] + got_wub[before]
+
+    @pl.when(step < steps)
+    def _():
+        for copy in copies(slot, (0, 1)):
+            copy.start()
+        d_wd, d_wu = tile(wu_b, wd_b, dbu_b, c)
+        send_wub[slot] = d_wu[half:]
+        copies(slot, (2,))[0].start()
+        keep_b[...] = d_wu[:half]
+        keep_d[...] = d_wd
+
+    @pl.when(step == steps)
+    def _():
+        out_low[...] = (out[...] + vecs[R_BD : R_BD + 1, :]).astype(bf16)
+        for copy in copies(before):
+            copy.wait_send()
+
+
+def mlp(vecs, h2, h2p, cot, res, w_up, w_down):
+    rows, width = h2.shape
+    ff = w_up.shape[1]
+    tile = ff // 8
+    half = width // 2
+    steps = 4
+    now = lambda i: jnp.minimum(i, steps - 1)
+    last = lambda i: jnp.maximum(i - 1, 0)
+    at_a = lambda i: 2 * now(i) + 1 - lax.rem(lax.axis_index("items"), 2)
+    at_b = lambda i: 2 * now(i) + lax.rem(lax.axis_index("items"), 2)
+    w_specs = []
+    for at in (at_a, at_b):
+        w_specs += [
+            pl.BlockSpec((width, tile), lambda i, at=at: (0, at(i))),
+            pl.BlockSpec((tile, width), lambda i, at=at: (at(i), 0)),
+        ]
+    bias = pl.BlockSpec((1, 1, tile), lambda i: (now(i), 0, 0))
+    up_grad = pl.BlockSpec((1, half, tile), lambda i: (last(i), 0, 0))
+    return pl.pallas_call(
+        mlp_kernel,
+        name="mlp",
+        grid=(steps + 1,),
+        in_specs=[VMEM] * 5 + w_specs,
+        out_specs=[
+            VMEM,
+            VMEM,
+            pl.BlockSpec((1, width, tile), lambda i: (last(i), 0, 0)),
+            up_grad,
+            up_grad,
+            bias,
+            bias,
+        ],
+        out_shape=[jax.ShapeDtypeStruct((rows, width), bf16)]
+        + [jax.ShapeDtypeStruct((rows, width), f32)]
+        + [jax.ShapeDtypeStruct((steps, width, tile), bf16)]
+        + [jax.ShapeDtypeStruct((steps, half, tile), bf16)] * 2
+        + [jax.ShapeDtypeStruct((steps, 1, tile), f32)] * 2,
+        scratch_shapes=(
+            [pltpu.VMEM((2, width, tile), bf16)]
+            + [pltpu.VMEM((2, half, tile), bf16)] * 2
+        )
+        * 2
+        + [
+            pltpu.VMEM((2, half, tile), bf16),
+            pltpu.VMEM((width, tile), bf16),
+            pltpu.VMEM((half, tile), bf16),
+            pltpu.VMEM((rows, width), f32),
+            DMA((3, 2)),
+            DMA((3, 2)),
+        ],
+        compiler_params=params(collective_id=4, has_side_effects=True),
+        cost_estimate=pl.CostEstimate(
+            flops=2 * 6 * rows * width * ff, bytes_accessed=40 * 2**20, transcendentals=0
+        ),
+    )(vecs, h2, h2p, cot, res, w_up, w_down, w_up, w_down)
+
+
+def norm_back(z, scale, dz):
+    return scale * (dz - jnp.mean(dz, -1, keepdims=True) - z * jnp.mean(dz * z, -1, keepdims=True))
+
+
+def normalize(value):
+    centre = value - jnp.mean(value, -1, keepdims=True)
+    scale = lax.rsqrt(jnp.mean(centre * centre, -1, keepdims=True) + epsilon)
+    return centre * scale, scale
+
+
+def tail_kernel(n_items, n_band, qt, *refs):
+    (table, counts, stat, vecs, dbu_a, dbu_b, log_total) = refs[:7]
+    (res_h, dh_h, cot_h, out_rows, attn_h, attn_sib_h, wo_h, q_h, k_h, v_h, h1_h) = refs[7:18]
+    (wq_h, wk_h, wv_h, tok_h, down_h, up_a_h, up_b_h, tokens_h) = refs[18:26]
+    (out_home, d_tok, total, o_down, o_up, o_wo, o_wq, o_wk, o_wv) = refs[26:35]
+    (res, dh, cot, low, wo, attn, attn_sib, kd, rd1, rd2, rd3, rd4) = refs[35:47]
+    (ku, ru1, ru2, ru3, ru4, q, k, v, da, da_send, dk_acc, dv_acc) = refs[47:59]
+    (h1, wq, wk, wv, tok, gw, gw_core, gw1, gw2, gw3, gw4) = refs[59:70]
+    (gp, gp_core, gqk1, gv1, gqk2, gv2, gp3, gp4, home) = refs[70:79]
+    (small, buf_i, part, buf_b, buf_i2, part2, buf_b2) = refs[79:86]
+    (send, recv, lsem, send_r, recv_r, send_g, recv_g, send_i, recv_i, send_b, recv_b) = refs[86:97]
+
+    it, bd, c, yx = place()
+    x, y = lax.rem(yx, 2), yx // 2
+    bl, bh = lax.rem(bd, 2), bd // 2
+    sibling = (it + 1 - 2 * c, bd)
+    to_x, to_y = (it + 2 - 4 * x, bd), (it + 4 - 8 * y, bd)
+    to_z1, to_z2 = (it, bd + 1 - 2 * bl), (it, lax.rem(bd + 2, 4))
+    rows, width = res.shape
+    half = width // 2
+    fourth = width // 4
+    tile = kd.shape[-1]
+    sent = []
+
+    def load(src, dst):
+        copy = pltpu.make_async_copy(src, dst, lsem.at[len(loads)])
+        copy.start()
+        loads.append(copy)
+        return copy
+
+    def push(src, dst, to):
+        i = len(sent)
+        copy = remote(src, dst, send.at[i], recv.at[i], to)
+        copy.start()
+        sent.append(copy)
+        return copy
+
+    loads = []
+    greet(all_peers(n_items))
+
+    def down_first(yy):
+        return push(down_h.at[2 * yy + 1 - x], rd1.at[yy], to_x)
+
+    def up_first(high):
+        got = []
+        for low_bit in range(2):
+            for i, up in enumerate((up_a_h, up_b_h)):
+                src = up.at[2 * high + low_bit, pl.ds(pl.multiple_of((1 - y) * tile // 2, 128), tile // 2)]
+                got.append(push(src, ru1.at[high, low_bit, i], to_y))
+        return got
+
+    d1 = [down_first(1 - y)]
+    u1 = up_first(0)
+    rows_back(out_rows, out_home, send_r, recv_r)
+
+    get_res, get_dh, get_cot = load(res_h, res), load(dh_h, dh), load(cot_h, cot)
+    get_wo, get_attn, get_sib = load(wo_h, wo), load(attn_h, attn), load(attn_sib_h, attn_sib)
+    get_qkv = [load(src, dst) for src, dst in ((q_h, q), (k_h, k), (v_h, v))]
+    get_kd = [load(down_h.at[2 * yy + x], kd.at[yy]) for yy in range(2)]
+    get_ku = []
+    for high in range(2):
+        for low_bit in range(2):
+            for i, up in enumerate((up_a_h, up_b_h)):
+                src = up.at[2 * high + low_bit, pl.ds(pl.multiple_of(y * tile // 2, 128), tile // 2)]
+                get_ku.append(load(src, ku.at[high, low_bit, i]))
+    lanes = pl.ds(pl.multiple_of(c * half, 128), half)
+    get_h1 = load(h1_h, h1)
+    get_w = [load(src.at[:, lanes], dst) for src, dst in ((wq_h, wq), (wk_h, wk), (wv_h, wv))]
+    get_tok = load(tok_h.at[pl.ds(0, rows)], tok)
+
+    small[...] = jnp.zeros_like(small)
+    for i in range(4):
+        for src, h in ((dbu_a, 1 - c), (dbu_b, c)):
+            small[4 + i : 5 + i, pl.ds(pl.multiple_of(h * half, 128), half)] = src[i]
+    for copy in (get_res, get_dh, get_cot, get_wo):
+        copy.wait()
+    block = 256
+
+    @pl.loop(0, rows // block)
+    def _(i):
+        at = pl.ds(pl.multiple_of(i * block, block), block)
+        z, scale = normalize(res[at, :])
+        d_h = dh[at, :]
+        c32 = cot[at, :].astype(f32)
+        full = c32 + norm_back(z, scale, d_h * vecs[R_G2 : R_G2 + 1, :])
+        res[at, :] = full
+        d_low = full.astype(bf16)
+        low[at, :] = d_low
+        for j, term in enumerate((d_h * z, d_h, d_low.astype(f32), c32)):
+            small[j : j + 1, :] += jnp.sum(term, 0, keepdims=True)
+        da[at, :] = dot(d_low, half_rows(wo, c, half), 1, 1).astype(bf16)
+        da_send[at, :] = dot(d_low, half_rows(wo, 1 - c, half), 1, 1).astype(bf16)
+
+    da_copy = push(da_send, da.at[pl.ds(rows, rows)], sibling)
+    d1.append(down_first(y))
+    u1 += up_first(1)
+
+    get_attn.wait()
+    get_sib.wait()
+    for i, heads in enumerate((attn, attn_sib)):
+        for xx in range(2):
+            part_wo = dot(heads[:, xx * fourth : (xx + 1) * fourth], low[...], 0, 0).astype(bf16)
+            for cc in range(2):
+                gw[i, xx, cc] = part_wo[cc * fourth // 2 : (cc + 1) * fourth // 2]
+    core_w = [push(gw.at[i, :, 1 - c], gw_core.at[1 - i], sibling) for i in range(2)]
+    early = share_start(
+        n_items, it, lambda p: (p, bd), small.at[pl.ds(0, 8)], buf_i, send_i.at[0], recv_i.at[0]
+    )
+
+    for copy in get_qkv:
+        copy.wait()
+    da_copy.wait_recv()
+    lane_k = lax.broadcasted_iota(jnp.int32, (2 * rows, 128), 1)
+    lane_q = lax.broadcasted_iota(jnp.int32, (qt, 128), 1)
+
+    def pair(i):
+        at_lanes = pl.ds(pl.multiple_of(i * 128, 128), 128)
+        k_pair, v_pair = k[:, at_lanes], v[:, at_lanes]
+        bias = key_bias(table, counts, k_pair.shape)
+        keys = [with_spare(k_pair, bias, hd, lane_k) for hd in range(2)]
+        keys_only = [head_lanes(k_pair, hd, lane_k) for hd in range(2)]
+        values = [head_lanes(v_pair, hd, lane_k) for hd in range(2)]
+        for t in range(2 * rows // qt):
+            at = slice(t * qt, (t + 1) * qt)
+            q_tile, d_tile = q[at, at_lanes], da[at, at_lanes]
+            dq_both = None
+            for hd in range(2):
+                q_head = head_lanes(q_tile, hd, lane_q)
+                d_head = head_lanes(d_tile, hd, lane_q)
+                s = dot(keys[hd], ones_beside(q_tile, hd, lane_q), 1, 1)
+                p = jnp.exp(s - log_total[i, hd : hd + 1, at])
+                d_p = dot(values[hd], d_tile, 1, 1)
+                weighted = p * d_p
+                delta = jnp.sum(weighted, 0, keepdims=True)
+                ds = (weighted - p * delta).astype(bf16)
+                dv_part = dot(p.astype(bf16), d_head)
+                dk_part = dot(ds, q_head)
+                if t == 0 and hd == 0:
+                    dv_acc[...] = dv_part
+                    dk_acc[...] = dk_part
+                else:
+                    dv_acc[...] += dv_part
+                    dk_acc[...] += dk_part
+                term = dot(keys_only[hd], ds, 0, 0)
+                dq_both = term if dq_both is None else dq_both + term
+            q[at, at_lanes] = (dq_both.T * score_scale).astype(bf16)
+        k[:, at_lanes] = dk_acc[...].astype(bf16)
+        v[:, at_lanes] = dv_acc[...].astype(bf16)
+
+    @pl.loop(0, 2)
+    def _(i):
+        pair(i)
+
+    part[...] = share_end(n_items, early, buf_i)
+    early = share_start(
+        n_band, bd, lambda p: (it, p), part, buf_b, send_b.at[0], recv_b.at[0]
+    )
+    for copy in get_kd:
+        copy.wait()
+    d1[0].wait_recv()
+    kd[1 - y] += rd1[1 - y]
+    d2 = push(kd.at[1 - y], rd2, to_y)
+    for copy in get_ku:
+        copy.wait()
+
+    def up_second(high):
+        for copy in u1[4 * high : 4 * high + 4]:
+            copy.wait_recv()
+        ku[high] += ru1[high]
+        return push(ku.at[high, :, :, pl.ds(pl.multiple_of((1 - x) * tile // 4, 128), tile // 4)], ru2.at[high], to_x)
+
+    u2 = [up_second(0)]
+    for i in range(2):
+        core_w[i].wait_recv()
+    for i in range(2):
+        gw[i, :, c] += gw_core[i]
+    rel_y = lax.rem(y + c, 2)
+    w1 = push(gw.at[1 - rel_y, :, c], gw1, to_y)
+
+    @pl.loop(2, q.shape[1] // 128)
+    def _(i):
+        pair(i)
+
+    total[0:8, :] = share_end(n_band, early, buf_b)
+
+    get_h1.wait()
+    core_p = []
+    for j in range(4):
+        for i, d in enumerate((q, k, v)):
+            part_p = dot(h1[:, j * fourth : (j + 1) * fourth], d[...], 0, 0).astype(bf16)
+            for cc in range(2):
+                gp[i, j, cc] = part_p[cc * fourth // 2 : (cc + 1) * fourth // 2]
+        core_p.append(push(gp.at[:, j, 1 - c], gp_core.at[:, j], sibling))
+    for i, d in ((0, q), (1, v)):
+        row = jnp.sum(d[...].astype(f32), 0, keepdims=True)
+        small[12 + i : 13 + i, pl.ds(pl.multiple_of(c * half, 128), half)] = row
+
+    for copy in get_w:
+        copy.wait()
+    dh1, dh1_sib = wo, low
+
+    @pl.loop(0, 2 * rows // block)
+    def _(i):
+        at = pl.ds(pl.multiple_of(lax.rem(i + rows // block, 2 * rows // block) * block, block), block)
+        term = dot(q[at, :], wq[...], 1, 1) + dot(k[at, :], wk[...], 1, 1)
+        dh1[at, :] = (term + dot(v[at, :], wv[...], 1, 1)).astype(bf16)
+
+    dh_copy = push(dh1.at[pl.ds(rows, rows)], dh1_sib, sibling)
+    for copy in core_p:
+        copy.wait_recv()
+    qk1, v1 = [], []
+    for j in range(2):
+        yx_x = 2 * j + 1 - x
+        qk1.append(push(gp.at[pl.ds(0, 2), yx_x, c], gqk1.at[0, j], to_x))
+        qk1.append(push(gp_core.at[pl.ds(0, 2), yx_x], gqk1.at[1, j], to_x))
+        yx_y = 2 * (1 - y) + j
+        v1.append(push(gp.at[2, yx_y, c], gv1.at[0, j], to_y))
+        v1.append(push(gp_core.at[2, yx_y], gv1.at[1, j], to_y))
+
+    get_tok.wait()
+    dh_copy.wait_recv()
+    g_rows = cot
+
+    @pl.loop(0, rows // block)
+    def _(i):
+        at = pl.ds(pl.multiple_of(i * block, block), block)
+        inv = stat[S_INV : S_INV + 1, :]
+        centred = tok[at, :].astype(f32) - stat[S_MEAN : S_MEAN + 1, :]
+        z, scale = normalize(centred * inv)
+        d_h = dh1[at, :].astype(f32) + dh1_sib[at, :].astype(f32)
+        d_start = res[at, :] + norm_back(z, scale, d_h * vecs[R_G1 : R_G1 + 1, :])
+        g_rows[at, :] = (d_start * inv).astype(bf16)
+        for j, term in enumerate((d_start, d_start * centred, d_h * z, d_h)):
+            small[8 + j : 9 + j, :] += jnp.sum(term, 0, keepdims=True)
+
+    late = share_start(
+        n_items, it, lambda p: (p, bd), small.at[pl.ds(8, 8)], buf_i2, send_i.at[1], recv_i.at[1]
+    )
+    g_blocks = g_rows.reshape(4, rows // 4, width)
+    rows_back(g_blocks, home, send_g, recv_g)
+    part2[...] = share_end(n_items, late, buf_i2)
+    late = share_start(
+        n_band, bd, lambda p: (it, p), part2, buf_b2, send_b.at[1], recv_b.at[1]
+    )
+
+    d1[1].wait_recv()
+    kd[y] += rd1[y]
+    u2.append(up_second(1))
+    sums = share_end(n_band, late, buf_b2)
+    total[8:16, :] = sums
+
+    count = patch_total(counts, (1, width))
+    inv = stat[S_INV : S_INV + 1, :]
+    fix = -0.5 * inv * sums[0:1, :] / count
+    slope = -0.5 * inv * inv * inv * sums[1:2, :] / count
+    cut = rows // 4
+    position = lax.broadcasted_iota(jnp.int32, (cut, width), 0) + bd * (2 * cut)
+    for i in range(4):
+        s, h = i // 2, i % 2
+        rows_back_got(g_blocks, home, send_g, recv_g, i)
+        now = pl.ds(h * cut, cut)
+        valid = position + h * cut < counts[table[it * 2 + s]]
+        term = fix + slope * (tokens_h[s, now, :].astype(f32) - stat[S_BATCH : S_BATCH + 1, :])
+        d_tok[s, now, :] = (home[s, now, :].astype(f32) + jnp.where(valid, term, 0.0)).astype(bf16)
+
+    d2.wait_recv()
+    kd[y] += rd2[...]
+    blocks = kd.reshape(2, 2, 2, width // 4, tile)
+    d3 = push(blocks.at[y, :, 1 - bl], rd3, to_z1)
+    w1.wait_recv()
+    gw[rel_y, :, c] += gw1[...]
+    w2 = push(gw.at[rel_y, 1 - x, c], gw2, to_x)
+    for copy in v1:
+        copy.wait_recv()
+    for j in range(2):
+        gp[2, 2 * y + j, c] += gv1[0, j]
+        gp_core[2, 2 * y + j] += gv1[1, j]
+    v2 = [
+        push(gp.at[2, 2 * y + 1 - x, c], gv2.at[0], to_x),
+        push(gp_core.at[2, 2 * y + 1 - x], gv2.at[1], to_x),
+    ]
+    for copy in qk1:
+        copy.wait_recv()
+    for i in range(2):
+        for j in range(2):
+            gp[i, 2 * j + x, c] += gqk1[0, j, i]
+            gp_core[i, 2 * j + x] += gqk1[1, j, i]
+    qk2 = [
+        push(gp.at[pl.ds(0, 2), 2 * (1 - y) + x, c], gqk2.at[0], to_y),
+        push(gp_core.at[pl.ds(0, 2), 2 * (1 - y) + x], gqk2.at[1], to_y),
+    ]
+    for copy in u2:
+        copy.wait_recv()
+    mine = pl.ds(pl.multiple_of(x * tile // 4, 128), tile // 4)
+    for high in range(2):
+        ku[high, :, :, mine] += ru2[high]
+    u3 = push(ku.at[:, 1 - bl, :, mine], ru3, to_z1)
+    d3.wait_recv()
+    for high in range(2):
+        blocks[y, high, bl] += rd3[high]
+    d4 = push(blocks.at[y, 1 - bh, bl], rd4, to_z2)
+    w2.wait_recv()
+    gw[rel_y, x, c] += gw2[...]
+
+    def z_lanes(which):
+        return pl.ds(pl.multiple_of(which * fourth, 128), fourth)
+
+    w3 = [
+        push(gw.at[rel_y, x, c, :, z_lanes(2 * high + 1 - bl)], gw3.at[high], to_z1) for high in range(2)
+    ]
+    for copy in v2:
+        copy.wait_recv()
+    here = 2 * y + x
+    gp[2, here, c] += gv2[0]
+    gp_core[2, here] += gv2[1]
+    for copy in qk2:
+        copy.wait_recv()
+    for i in range(2):
+        gp[i, here, c] += gqk2[0, i]
+        gp_core[i, here] += gqk2[1, i]
+    p3 = [
+        push(gp.at[:, here, c, :, z_lanes(1 - bl)], gp3.at[0], to_z1),
+        push(gp_core.at[:, here, :, z_lanes(1 - bl)], gp3.at[1], to_z1),
+    ]
+    u3.wait_recv()
+    for high in range(2):
+        ku[high, bl, :, mine] += ru3[high]
+    u4 = push(ku.at[1 - bh, bl, :, mine], ru4, to_z2)
+    for high in range(2):
+        w3[high].wait_recv()
+    w_mine = [gw[rel_y, x, c, :, z_lanes(2 * high + bl)] + gw3[high] for high in range(2)]
+    gw3[0] = w_mine[0]
+    gw3[1] = w_mine[1]
+    w4 = push(gw3.at[1 - bh], gw4, to_z2)
+    for copy in p3:
+        copy.wait_recv()
+    gp3[0] = gp[:, here, c, :, z_lanes(bl)] + gp3[0]
+    gp3[1] = gp_core[:, here, :, z_lanes(bl)] + gp3[1]
+    rel_b = lax.rem(bh + c, 2)
+    p4 = push(gp3.at[1 - rel_b], gp4, to_z2)
+    d4.wait_recv()
+    o_down[...] = (blocks[y, bh, bl].astype(f32) + rd4[...].astype(f32)).T
+    u4.wait_recv()
+    up = ku[bh, bl, :, mine].astype(f32) + ru4[...].astype(f32)
+    for i, h in ((0, 1 - c), (1, c)):
+        o_up[:, pl.ds(pl.multiple_of(h * tile, 128), tile)] = up[i]
+    w4.wait_recv()
+    o_wo[...] = gw3[bh].astype(f32) + gw4[...].astype(f32)
+    p4.wait_recv()
+    for i, ref in enumerate((o_wq, o_wk, o_wv)):
+        ref[...] = gp3[rel_b, i].astype(f32) + gp4[i].astype(f32)
+
+    for i in range(4):
+        rows_back_got(out_rows, out_home, send_r, recv_r, i)
+    rows_back_sent(out_rows, out_home, send_r, recv_r)
+    rows_back_sent(g_blocks, home, send_g, recv_g)
+    for copy in sent:
+        copy.wait_send()
+
+
+def tail(table, counts, stat, vecs, dbu_a, dbu_b, log_total, res, dh, cot, out_rows, attn, attn_sib, wo, *rest, qt=512):
+    (q, k, v, h1, wq, wk, wv, tok, down, up_a, up_b, tokens) = rest
+    n_items, n_band = lax.axis_size("items"), lax.axis_size("band")
+    rows, width = res.shape
+    half, fourth, cut = width // 2, width // 4, rows // 4
+    tile = down.shape[2]
+    buf = lambda *shape: pltpu.VMEM(shape, bf16)
+    buf32 = lambda *shape: pltpu.VMEM(shape, f32)
+    out = lambda *shape: jax.ShapeDtypeStruct(shape, f32)
+    e, s = fourth // 2, fourth
+    return pl.pallas_call(
+        functools.partial(tail_kernel, n_items, n_band, qt),
+        name="tail",
+        in_specs=[SMEM, SMEM] + [VMEM] * 5 + [HBM] * 18 + [VMEM],
+        out_specs=[HBM] + [VMEM] * 8,
+        out_shape=[
+            jax.ShapeDtypeStruct(tokens.shape, bf16),
+            jax.ShapeDtypeStruct(tokens.shape, bf16),
+            out(16, width),
+            out(tile, s),
+            out(e, 2 * tile),
+            out(e, s),
+            out(e, s),
+            out(e, s),
+            out(e, s),
+        ],
+        scratch_shapes=[
+            buf32(rows, width), buf32(rows, width), buf(rows, width), buf(rows, width),
+            buf(width, width), buf(rows, half), buf(rows, half),
+            buf(2, width, tile), buf(2, width, tile), buf(width, tile), buf(2, s, tile), buf(s, tile),
+            buf(2, 2, 2, tile // 2, tile), buf(2, 2, 2, tile // 2, tile), buf(2, 2, 2, tile // 4, tile),
+            buf(2, 2, tile // 4, tile), buf(2, tile // 4, tile),
+            buf(2 * rows, half), buf(2 * rows, half), buf(2 * rows, half),
+            buf(2 * rows, half), buf(rows, half), buf32(2 * rows, 128), buf32(2 * rows, 128),
+            buf(2 * rows, width), buf(width, half), buf(width, half), buf(width, half), buf(rows, width),
+            buf(2, 2, 2, e, width), buf(2, 2, e, width), buf(2, e, width), buf(e, width),
+            buf(2, e, s), buf(e, s),
+            buf(3, 4, 2, e, half), buf(3, 4, e, half), buf(2, 2, 2, e, half), buf(2, 2, e, half),
+            buf(2, 2, e, half), buf(2, e, half), buf(2, 3, e, s), buf(3, e, s),
+            buf(2, 2 * cut, width),
+            buf32(16, width), buf32(n_items, 8, width), buf32(8, width), buf32(n_band, 8, width),
+            buf32(n_items, 8, width), buf32(8, width), buf32(n_band, 8, width),
+            DMA((48,)), DMA((48,)), DMA((32,)),
+            DMA((4,)), DMA((4,)), DMA((4,)), DMA((4,)),
+            DMA((2, n_items)), DMA((2, n_items)), DMA((2, n_band)), DMA((2, n_band)),
+        ],
+        compiler_params=params(collective_id=5, has_side_effects=True),
+        cost_estimate=pl.CostEstimate(
+            flops=60 * rows * width * width, bytes_accessed=40 * 2**20, transcendentals=0
+        ),
+    )(
+        table, counts, stat, vecs, dbu_a, dbu_b, log_total, res, dh, cot,
+        out_rows.reshape(4, cut, width), attn, attn_sib, wo, q, k, v, h1, wq, wk, wv, tok,
+        down, up_a, up_b, tokens,
+    )
+
+
+def column_layer(
+    tokens, cotangent, running_mean, running_var, slot_table, patch_counts,
+    ln1_gain, ln1_bias, w_query, b_query, w_key, w_value, b_value, w_out, b_out,
+    ln2_gain, ln2_bias, w_up, b_up, w_down, b_down,
+):
+    slots, band_rows, width = tokens.shape
+    rows = slots * band_rows
+    parts = (running_mean, running_var, ln1_gain, ln1_bias, b_query, b_value, b_out)
+    parts += (ln2_gain, ln2_bias, b_down, b_up)
+    vecs = jnp.concatenate([part.astype(f32) for part in parts]).reshape(-1, width)
+    gathered, stat = gather(slot_table, patch_counts, vecs, tokens)
+    tok = gathered.reshape(2 * rows, width)
+    h1, q, k, v = project(stat, vecs, tok, w_query, w_key, w_value)
+    attn, log_total, cot_rows, attn_sib = attend(slot_table, patch_counts, q, k, v, cotangent)
+    cot_rows = cot_rows.reshape(rows, width)
+    res, h2, h2p = join(stat, vecs, attn, attn_sib, w_out, tok)
+    out_rows, d_h2, d_down, d_up_a, d_up_b, dbu_a, dbu_b = mlp(
+        vecs, h2, h2p, cot_rows, res, w_up, w_down
+    )
+    output, d_tokens, small, d_w_down, d_w_up, d_w_out, d_wq, d_wk, d_wv = tail(
+        slot_table, patch_counts, stat, vecs, dbu_a, dbu_b, log_total, res, d_h2, cot_rows,
+        out_rows, attn, attn_sib, w_out, q, k, v, h1, w_query, w_key, w_value, tok,
+        d_down, d_up_a, d_up_b, tokens,
+    )
+    d_gain_two, d_shift_two, d_bo, d_bdown = (small[i] for i in range(4))
+    d_gain_one, d_shift_one, d_bq, d_bv = (small[i] for i in range(10, 14))
+    return (
+        output, d_tokens, stat[S_MEAN], stat[S_VAR], d_gain_one, d_shift_one,
+        d_wq, d_bq, d_wk, d_wv, d_bv, d_w_out, d_bo, d_gain_two, d_shift_two,
+        d_w_up, small[4:8].reshape(-1), d_w_down, d_bdown,
+    )
 
 
 def layer_norm(value, gain, shift):
@@ -364,8 +1392,9 @@
 
 
 def solution(mesh):
+    columns = mesh.shape["items"] == 8 and mesh.shape["band"] == 4
     return jax.shard_map(
-        local,
+        column_layer if columns else local,
         mesh=mesh,
         in_specs=(
             P("items", "band", None),

time: 1120 us -> 312 us (0.28)
  waiting for transfers between devices: 627 us -> 0 us
  Pallas kernels: 0 us -> 286 us
  matrix products: 188 us -> 0 us
  local copies, waits for them, and re-layouts: 131 us -> 13.1 us
  blocking collectives: 83.3 us -> 0 us
  other arithmetic: 53.6 us -> 6.16 us
  between operations: 15.7 us -> 1.17 us
  loops' own time: 11.5 us -> 0 us
    reduce_scatter x14 -> x0, waiting for transfers between devices: 486 us -> none  [the longest x1 75.5 us: local(): lax.psum_scatter(jnp.stack(d_v_list).astype(jnp.bfloat16), 'band', scatte...]
    pallas_call x0 -> x6, Pallas kernels: none -> 286 us  [the longest x1 173 us: tail(): pl.pallas_call(functools.partial(tail_kernel, n_items, n_band, qt), name=...]
    dot_general x74 -> x0, matrix products: 188 us -> none  [the longest x16 28 us: group_scores(): jnp.einsum('rhd,khd->hrk', q_part, k_part, preferred_element_type=jnp.flo...]
    all_gather x2 -> x0, waiting for transfers between devices: 142 us -> none  [the longest x1 75.7 us: local(): lax.all_gather(key_local, 'band', axis=1, tiled=True)]
    psum x2 -> x0, blocking collectives: 83.3 us -> none  [the longest x1 42.1 us: local(): total_one, total_two = lax.psum((part_one, part_two), ('items', 'band'))]
    dynamic_slice x64 -> x0, local copies, waits for them, and re-layouts: 49.2 us -> none  [the longest x16 14.7 us: head_block(): lax.dynamic_slice_in_dim(q_slot, begin, group_width, 1)]
    reduce_sum x23 -> x0, other arithmetic: 27.7 us -> none  [the longest x8 8.15 us: head_block(): jnp.sum(jnp.exp(scores - top_score), -1, keepdims=True)]
    dynamic_update_slice x32 -> x0, local copies, waits for them, and re-layouts: 22.1 us -> none  [the longest x16 13.6 us: attend_backward(): lax.map(head_block, (jnp.arange(groups, dtype=jnp.int32), log_totals, del...]
  transfers between devices with their start and end apart: 16 -> 0, of which waited for: 14 -> 0; matrix products, arithmetic and copies ran while one was open for 10% -> 0% of each run, Pallas kernels for 0% -> 0%
where the time goes in v3:
time: 312 us; the launch traced here: 306 us
  Pallas kernels  286 us (92%)
  local copies, waits for them, and re-layouts  13.1 us (4%)
  other arithmetic  6.16 us (2%)
    pallas_call x1, Pallas kernels, tail(): pl.pallas_call(functools.partial(tail_kernel, n_items, n_band, qt), name=...  173 us
    pallas_call x1, Pallas kernels, mlp(): pl.pallas_call(mlp_kernel, name='mlp', grid=(steps + 1,), in_specs=[VMEM]...  42.6 us
    pallas_call x1, Pallas kernels, gather(): pl.pallas_call(functools.partial(gather_kernel, n_items, n_band), name='g...  36.1 us
    pallas_call x1, Pallas kernels, attend(): pl.pallas_call(functools.partial(attend_kernel, qt), name='attend', grid=...  19.9 us
    unnamed x28, local copies, waits for them, and re-layouts  10.3 us
    pallas_call x1, Pallas kernels, project(): pl.pallas_call(project_kernel, name='project', grid=(rows // block,), in_...  8.1 us

profile of v3, /device:TPU:0, one launch (start us, length us, event | category | flops | bytes accessed | tf_op | source)
XLA Modules:
  0.0 306.0 jit_solution(1916296678943330879)
XLA Ops:
  0.7 0.7 constant_dynamic-update-slice_fusion.9
  1.3 0.7 constant_dynamic-update-slice_fusion.8
  2.0 0.7 constant_dynamic-update-slice_fusion.7
  2.7 0.7 constant_dynamic-update-slice_fusion.6
  3.4 0.7 constant_dynamic-update-slice_fusion.5
  4.1 0.7 constant_dynamic-update-slice_fusion.4
  4.8 0.7 constant_dynamic-update-slice_fusion.3
  5.5 0.7 constant_dynamic-update-slice_fusion.2
  6.1 0.7 constant_dynamic-update-slice_fusion.1
  6.8 0.7 constant_dynamic-update-slice_fusion
  7.5 0.7 convert_dynamic-update-slice_fusion
  8.8 36.1 %gather.1 = (bf16[8,128,1024]{2,1,0:T(8,128)(2,1)}, f32[4,1024]{1,0:T(4,128)}) custom-call(s32[16]{0:T(128)} %refs_0_.3, s32[16]{0:T(128)} %refs_1_.3, f32[14,1024]{1,0:T(8,128)} %reshape.53.vecs.refs_3_, bf16[2,256,1024]{2,1,0:T(8,128)(2,1)} %refs_25_.1), custom_call_target="tpu_custom_call" | custom-call | tf_op jit(solution)/shard_map/gather/pallas_call | solution.py:217
  45.0 8.1 %project.1 = (bf16[1024,1024]{1,0:T(8,128)(2,1)}, bf16[1024,512]{1,0:T(8,128)(2,1)}, bf16[1024,512]{1,0:T(8,128)(2,1)}, bf16[1024,512]{1,0:T(8,128)(2,1)}) custom-call(f32[4,1024]{1,0:T(4,128)} %get-tuple-element.48.stat.refs_2_, f32[14,1024]{1,0:T(8,128)} %reshape.53.vecs.refs_3_, bf16[1024,1024]{1,0:T(8,128)(2,1)} %bitcast.18, ...), custom_call_target="tpu_custom_call" | custom-call | flops 3221225472 | bytes 12582912 | tf_op jit(solution)/shard_map/project/pallas_call | solution.py:263
  53.1 19.9 %attend.1 = (bf16[512,512]{1,0:T(8,128)(2,1)}, f32[4,2,1024]{2,1,0:T(2,128)}, bf16[4,128,1024]{2,1,0:T(8,128)(2,1)}, bf16[512,512]{1,0:T(8,128)(2,1)}) custom-call(s32[16]{0:T(128)} %refs_0_.3, s32[16]{0:T(128)} %refs_1_.3, bf16[1024,512]{1,0:T(8,128)(2,1)} %get-tuple-element.50.q.refs_14_, bf16[1024,512]{1,0:T(8,128)(2,1)} %get-tuple-element.51.k.refs_15_, ...), custom_call_target="tpu_custom_call" | custom-call | flops 8589934592 | bytes 5242880 | tf_op jit(solution)/shard_map/attend/pallas_call | solution.py:365
  73.0 5.3 %join.1 = (f32[512,1024]{1,0:T(8,128)}, bf16[512,1024]{1,0:T(8,128)(2,1)}, bf16[512,1024]{1,0:T(8,128)(2,1)}) custom-call(f32[4,1024]{1,0:T(4,128)} %get-tuple-element.48.stat.refs_2_, f32[14,1024]{1,0:T(8,128)} %reshape.53.vecs.refs_3_, bf16[512,512]{1,0:T(8,128)(2,1)} %get-tuple-element.53.attn_a.refs_11_, ...), custom_call_target="tpu_custom_call" | custom-call | flops 1073741824 | bytes 8388608 | tf_op jit(solution)/shard_map/join/pallas_call | solution.py:421
  78.4 42.6 %mlp.1 = (bf16[512,1024]{1,0:T(8,128)(2,1)}, f32[512,1024]{1,0:T(8,128)}, bf16[4,1024,512]{2,1,0:T(8,128)(2,1)}, bf16[4,512,512]{2,1,0:T(8,128)(2,1)}, bf16[4,51...) custom-call(f32[14,1024]{1,0:T(8,128)} %reshape.53.vecs.refs_3_, ...), custom_call_target="tpu_custom_call" | custom-call | flops 25769803776 | bytes 41943040 | tf_op jit(solution)/shard_map/mlp/pallas_call | solution.py:545
  121.0 173.4 %tail.1 = (bf16[2,256,1024]{2,1,0:T(8,128)(2,1)}, bf16[2,256,1024]{2,1,0:T(8,128)(2,1)}, f32[16,1024]{1,0:T(8,128)}, f32[512,256]{1,0:T(8,128)}, f32[128,1024]{1...) custom-call(s32[16]{0:T(128)} %refs_0_.3, s32[16]{0:T(128)} %refs_1_.3, ...), custom_call_target="tpu_custom_call" | custom-call | flops 32212254720 | bytes 41943040 | tf_op jit(solution)/shard_map/tail/pallas_call | solution.py:964
  294.4 1.6 fusion
  296.0 0.8 slice_bitcast_fusion
  298.0 2.3 copy.61
  300.4 1.0 copy.62
  301.3 0.7 copy.63
  304.0 0.8 copy.67
  304.8 0.8 copy.68
  (22 shorter events, 3.9 us)
Async XLA Ops:
  121.0 176.4 %copy-start.7 = (f32[4,1024]{1,0:T(4,128)S(1)}, f32[4,1024]{1,0:T(4,128)}, u32[]{:S(2)}) copy-start(f32[4,1024]{1,0:T(4,128)} %get-tuple-element.48.stat.refs_2_) | copy-start | bytes 49156
  294.4 6.0 %copy-start = (bf16[2,256,1024]{2,1,0:T(8,128)(2,1)S(1)}, bf16[2,256,1024]{2,1,0:T(8,128)(2,1)}, u32[]{:S(2)}) copy-start(bf16[2,256,1024]{2,1,0:T(8,128)(2,1)} %get-tuple-element.107) | copy-start | bytes 3145732
  298.0 3.3 %copy-start.6 = (f32[128,256]{1,0:T(8,128)S(1)}, f32[128,256]{1,0:T(8,128)}, u32[]{:S(2)}) copy-start(f32[128,256]{1,0:T(8,128)} %get-tuple-element.112) | copy-start | bytes 393220
  298.0 4.0 %copy-start.5 = (f32[128,256]{1,0:T(8,128)S(1)}, f32[128,256]{1,0:T(8,128)}, u32[]{:S(2)}) copy-start(f32[128,256]{1,0:T(8,128)} %get-tuple-element.114) | copy-start | bytes 393220
  298.0 4.7 %copy-start.4 = (f32[128,256]{1,0:T(8,128)S(1)}, f32[128,256]{1,0:T(8,128)}, u32[]{:S(2)}) copy-start(f32[128,256]{1,0:T(8,128)} %get-tuple-element.115) | copy-start | bytes 393220
  298.0 5.3 %copy-start.3 = (f32[128,256]{1,0:T(8,128)S(1)}, f32[128,256]{1,0:T(8,128)}, u32[]{:S(2)}) copy-start(f32[128,256]{1,0:T(8,128)} %get-tuple-element.117) | copy-start | bytes 393220
  298.0 6.0 %copy-start.2 = (f32[128,1024]{1,0:T(8,128)S(1)}, f32[128,1024]{1,0:T(8,128)}, u32[]{:S(2)}) copy-start(f32[128,1024]{1,0:T(8,128)} %get-tuple-element.121) | copy-start | bytes 1572868
  300.4 4.4 %copy-start.1 = (f32[512,256]{1,0:T(8,128)S(1)}, f32[512,256]{1,0:T(8,128)}, u32[]{:S(2)}) copy-start(f32[512,256]{1,0:T(8,128)} %get-tuple-element.123) | copy-start | bytes 1572868

commit v4 on v3

--- a/solution.py
+++ b/solution.py
@@ -446,18 +446,28 @@
     return u * half, slope
 
 
+def block_order(step):
+    it, bd, c, yx = place()
+    x = lax.rem(yx, 2)
+    return 2 * lax.rem(step, 2) + jnp.where(step < 2, 1 - x, x)
+
+
 def mlp_kernel(vecs, h2, h2p, cot, res, *refs):
     (wu_a, wd_a, wu_b, wd_b) = refs[:4]
-    (out_low, dh, dwd, dwu_a, dwu_b, dbu_a, dbu_b) = refs[4:11]
-    (send_wd, send_wua, send_wub, got_wd, got_wua, got_wub, keep_a, keep_d, keep_b, out) = refs[11:21]
-    (send, recv) = refs[21:]
+    (out_low, dh, kd, rd, rest_d, ku, ru, rest_u, dbu_a, dbu_b) = refs[4:14]
+    (send_wd, send_wua, send_wub, got_wd, got_wua, got_wub, keep_a, out, gd, gu) = refs[14:24]
+    (send, recv, send_d, recv_d, send_u, recv_u, keep_d, sem_u, rest_sem) = refs[24:]
     step = pl.program_id(0)
     steps = pl.num_programs(0) - 1
     half = h2.shape[1] // 2
     it, bd, c, yx = place()
+    x, y = lax.rem(yx, 2), yx // 2
     sibling = (it + 1 - 2 * c, bd)
+    to_x, to_y = (it + 2 - 4 * x, bd), (it + 4 - 8 * y, bd)
     slot = lax.rem(step, 2)
     before = 1 - slot
+    some = gd.shape[1] // 2
+    part = gu.shape[2] // 2
 
     def copies(at, which=(0, 1, 2)):
         pairs = ((send_wd, got_wd), (send_wua, got_wua), (send_wub, got_wub))
@@ -466,15 +476,50 @@
             for i in which
         ]
 
+    def down_copy(at):
+        if at == 0:
+            return [remote(gd.at[0], rd.at[0], send_d.at[0], recv_d.at[0], to_x)]
+        if at == 1:
+            first, second = pl.ds(0, some), pl.ds(some, some)
+            return [
+                remote(gd.at[1, first], rd.at[1, first], send_d.at[1], recv_d.at[1], to_x),
+                pltpu.make_async_copy(gd.at[1, second], rest_d, rest_sem.at[2]),
+            ]
+        return [pltpu.make_async_copy(gd.at[at], kd.at[at - 2], keep_d.at[at - 2])]
+
+    def up_rows(which):
+        return pl.ds(pl.multiple_of(which * part, 128), part)
+
+    def up_keep(at, i):
+        return pltpu.make_async_copy(gu.at[at, i, up_rows(y)], ku.at[block_order(at), i], sem_u.at[at, i])
+
+    def up_send(at, i):
+        src, dst = gu.at[at, i, up_rows(1 - y)], ru.at[block_order(at), i]
+        return remote(src, dst, send_u.at[at, i], recv_u.at[at, i], to_y)
+
+    def up_rest(at, i):
+        return pltpu.make_async_copy(gu.at[at, i, up_rows(1 - y)], rest_u.at[i], rest_sem.at[i])
+
+    def up_ready(at, i):
+        up_keep(at, i).start()
+
+        @pl.when(at < steps - 1)
+        def _():
+            up_send(at, i).start()
+
+        @pl.when(at == steps - 1)
+        def _():
+            up_rest(at, i).start()
+
     @pl.when(step == 0)
     def _():
-        greet([sibling])
+        greet([sibling, to_x, to_y])
         out[...] = res[...]
         dh[...] = jnp.zeros_like(dh)
 
     def tile(wu, wd, dbu, which):
         lanes = pl.ds(pl.multiple_of(which * wu.shape[1], 128), wu.shape[1])
-        up = dot(h2[...], wu[...]) + vecs[pl.ds(R_BU + step, 1), lanes]
+        up = dot(h2[...], wu[...]) + vecs[pl.ds(R_BU + block_order(step), 1), lanes]
         d_act = dot(cot[...], wd[...], 1, 1)
         act, slope = gelu_and_slope(up)
         act = act.astype(bf16)
@@ -501,11 +546,9 @@
 
     @pl.when(step > 0)
     def _():
-        for copy in copies(before):
-            copy.wait_recv()
-        dwd[0] = keep_d[...] + got_wd[before]
-        dwu_b[0] = keep_b[...] + got_wua[before]
-        dwu_a[0] = keep_a[before] + got_wub[before]
+        copies(before, (2,))[0].wait_recv()
+        gu[step - 1, 0] = keep_a[before] + got_wub[before]
+        up_ready(step - 1, 0)
 
     @pl.when(step < steps)
     def _():
@@ -514,14 +557,30 @@
         d_wd, d_wu = tile(wu_b, wd_b, dbu_b, c)
         send_wub[slot] = d_wu[half:]
         copies(slot, (2,))[0].start()
-        keep_b[...] = d_wu[:half]
-        keep_d[...] = d_wd
+        for copy in copies(slot, (0, 1)):
+            copy.wait_recv()
+        gd[step] = d_wd + got_wd[slot]
+        gu[step, 1] = d_wu[:half] + got_wua[slot]
+        up_ready(step, 1)
+
+    for at in range(4):
+
+        @pl.when(step == at)
+        def _():
+            for copy in down_copy(at):
+                copy.start()
 
     @pl.when(step == steps)
     def _():
         out_low[...] = (out[...] + vecs[R_BD : R_BD + 1, :]).astype(bf16)
         for copy in copies(before):
             copy.wait_send()
+        for at in range(4):
+            for copy in down_copy(at):
+                copy.wait()
+            for i in range(2):
+                up_keep(at, i).wait()
+                (up_send(at, i) if at < 3 else up_rest(at, i)).wait()
 
 
 def mlp(vecs, h2, h2p, cot, res, w_up, w_down):
@@ -530,8 +589,7 @@
     tile = ff // 8
     half = width // 2
     steps = 4
-    now = lambda i: jnp.minimum(i, steps - 1)
-    last = lambda i: jnp.maximum(i - 1, 0)
+    now = lambda i: block_order(jnp.minimum(i, steps - 1))
     at_a = lambda i: 2 * now(i) + 1 - lax.rem(lax.axis_index("items"), 2)
     at_b = lambda i: 2 * now(i) + lax.rem(lax.axis_index("items"), 2)
     w_specs = []
@@ -541,38 +599,42 @@
             pl.BlockSpec((tile, width), lambda i, at=at: (at(i), 0)),
         ]
     bias = pl.BlockSpec((1, 1, tile), lambda i: (now(i), 0, 0))
-    up_grad = pl.BlockSpec((1, half, tile), lambda i: (last(i), 0, 0))
+    low = lambda *shape: jax.ShapeDtypeStruct(shape, bf16)
     return pl.pallas_call(
         mlp_kernel,
         name="mlp",
         grid=(steps + 1,),
         in_specs=[VMEM] * 5 + w_specs,
-        out_specs=[
-            VMEM,
-            VMEM,
-            pl.BlockSpec((1, width, tile), lambda i: (last(i), 0, 0)),
-            up_grad,
-            up_grad,
-            bias,
-            bias,
-        ],
-        out_shape=[jax.ShapeDtypeStruct((rows, width), bf16)]
-        + [jax.ShapeDtypeStruct((rows, width), f32)]
-        + [jax.ShapeDtypeStruct((steps, width, tile), bf16)]
-        + [jax.ShapeDtypeStruct((steps, half, tile), bf16)] * 2
+        out_specs=[VMEM, VMEM] + [HBM] * 6 + [bias, bias],
+        out_shape=[
+            low(rows, width),
+            jax.ShapeDtypeStruct((rows, width), f32),
+            low(2, width, tile),
+            low(2, width, tile),
+            low(width // 2, tile),
+            low(4, 2, half // 2, tile),
+            low(4, 2, half // 2, tile),
+            low(2, half // 2, tile),
+        ]
         + [jax.ShapeDtypeStruct((steps, 1, tile), f32)] * 2,
         scratch_shapes=(
-            [pltpu.VMEM((2, width, tile), bf16)]
-            + [pltpu.VMEM((2, half, tile), bf16)] * 2
+            [pltpu.VMEM((2, width, tile), bf16)] + [pltpu.VMEM((2, half, tile), bf16)] * 2
         )
         * 2
         + [
             pltpu.VMEM((2, half, tile), bf16),
-            pltpu.VMEM((width, tile), bf16),
-            pltpu.VMEM((half, tile), bf16),
             pltpu.VMEM((rows, width), f32),
+            pltpu.VMEM((steps, width, tile), bf16),
+            pltpu.VMEM((steps, 2, half, tile), bf16),
             DMA((3, 2)),
             DMA((3, 2)),
+            DMA((2,)),
+            DMA((2,)),
+            DMA((3, 2)),
+            DMA((3, 2)),
+            DMA((2,)),
+            DMA((4, 2)),
+            DMA((3,)),
         ],
         compiler_params=params(collective_id=4, has_side_effects=True),
         cost_estimate=pl.CostEstimate(
@@ -594,14 +656,14 @@
 def tail_kernel(n_items, n_band, qt, *refs):
     (table, counts, stat, vecs, dbu_a, dbu_b, log_total) = refs[:7]
     (res_h, dh_h, cot_h, out_rows, attn_h, attn_sib_h, wo_h, q_h, k_h, v_h, h1_h) = refs[7:18]
-    (wq_h, wk_h, wv_h, tok_h, down_h, up_a_h, up_b_h, tokens_h) = refs[18:26]
-    (out_home, d_tok, total, o_down, o_up, o_wo, o_wq, o_wk, o_wv) = refs[26:35]
-    (res, dh, cot, low, wo, attn, attn_sib, kd, rd1, rd2, rd3, rd4) = refs[35:47]
-    (ku, ru1, ru2, ru3, ru4, q, k, v, da, da_send, dk_acc, dv_acc) = refs[47:59]
-    (h1, wq, wk, wv, tok, gw, gw_core, gw1, gw2, gw3, gw4) = refs[59:70]
-    (gp, gp_core, gqk1, gv1, gqk2, gv2, gp3, gp4, home) = refs[70:79]
-    (small, buf_i, part, buf_b, buf_i2, part2, buf_b2) = refs[79:86]
-    (send, recv, lsem, send_r, recv_r, send_g, recv_g, send_i, recv_i, send_b, recv_b) = refs[86:97]
+    (wq_h, wk_h, wv_h, tok_h, kd_h, rd_h, rest_d, ku_h, ru_h, rest_u, tokens) = refs[18:29]
+    (out_home, d_tok, total, o_down, o_up, o_wo, o_wq, o_wk, o_wv) = refs[29:38]
+    (res, dh, cot, low, wo, attn, attn_sib, kd, rd1, rdr, rd2, rd3, rd4) = refs[38:51]
+    (ku, ru1, rur, ru2, ru3, ru4, q, k, v, da, da_send, dk_acc, dv_acc) = refs[51:64]
+    (h1, wq, wk, wv, tok, gw, gw_core, gw1, gw2, gw3, gw4) = refs[64:75]
+    (d_pair, gp, gp_core, gp1, gp2, gp3, gp4, home) = refs[75:83]
+    (small, buf_i, part, buf_b, buf_i2, part2, buf_b2) = refs[83:90]
+    (send, recv, lsem, send_r, recv_r, send_g, recv_g, send_i, recv_i, send_b, recv_b) = refs[90:101]
 
     it, bd, c, yx = place()
     x, y = lax.rem(yx, 2), yx // 2
@@ -612,8 +674,10 @@
     rows, width = res.shape
     half = width // 2
     fourth = width // 4
+    eighth = width // 8
     tile = kd.shape[-1]
     sent = []
+    loads = []
 
     def load(src, dst):
         copy = pltpu.make_async_copy(src, dst, lsem.at[len(loads)])
@@ -628,50 +692,35 @@
         sent.append(copy)
         return copy
 
-    loads = []
+    def some(which, size):
+        return pl.ds(pl.multiple_of(which * size, 128), size)
+
     greet(all_peers(n_items))
-
-    def down_first(yy):
-        return push(down_h.at[2 * yy + 1 - x], rd1.at[yy], to_x)
-
-    def up_first(high):
-        got = []
-        for low_bit in range(2):
-            for i, up in enumerate((up_a_h, up_b_h)):
-                src = up.at[2 * high + low_bit, pl.ds(pl.multiple_of((1 - y) * tile // 2, 128), tile // 2)]
-                got.append(push(src, ru1.at[high, low_bit, i], to_y))
-        return got
-
-    d1 = [down_first(1 - y)]
-    u1 = up_first(0)
+    d1 = push(rest_d, rdr, to_x)
+    u1 = push(rest_u, rur, to_y)
     rows_back(out_rows, out_home, send_r, recv_r)
 
     get_res, get_dh, get_cot = load(res_h, res), load(dh_h, dh), load(cot_h, cot)
     get_wo, get_attn, get_sib = load(wo_h, wo), load(attn_h, attn), load(attn_sib_h, attn_sib)
+    get_down = [load(kd_h, kd), load(rd_h, rd1)]
+    get_up = [load(ku_h, ku), load(ru_h, ru1)]
     get_qkv = [load(src, dst) for src, dst in ((q_h, q), (k_h, k), (v_h, v))]
-    get_kd = [load(down_h.at[2 * yy + x], kd.at[yy]) for yy in range(2)]
-    get_ku = []
-    for high in range(2):
-        for low_bit in range(2):
-            for i, up in enumerate((up_a_h, up_b_h)):
-                src = up.at[2 * high + low_bit, pl.ds(pl.multiple_of(y * tile // 2, 128), tile // 2)]
-                get_ku.append(load(src, ku.at[high, low_bit, i]))
-    lanes = pl.ds(pl.multiple_of(c * half, 128), half)
     get_h1 = load(h1_h, h1)
+    lanes = some(c, half)
     get_w = [load(src.at[:, lanes], dst) for src, dst in ((wq_h, wq), (wk_h, wk), (wv_h, wv))]
     get_tok = load(tok_h.at[pl.ds(0, rows)], tok)
 
     small[...] = jnp.zeros_like(small)
     for i in range(4):
         for src, h in ((dbu_a, 1 - c), (dbu_b, c)):
-            small[4 + i : 5 + i, pl.ds(pl.multiple_of(h * half, 128), half)] = src[i]
+            small[4 + i : 5 + i, some(h, half)] = src[i]
     for copy in (get_res, get_dh, get_cot, get_wo):
         copy.wait()
     block = 256
 
     @pl.loop(0, rows // block)
     def _(i):
-        at = pl.ds(pl.multiple_of(i * block, block), block)
+        at = some(i, block)
         z, scale = normalize(res[at, :])
         d_h = dh[at, :]
         c32 = cot[at, :].astype(f32)
@@ -685,8 +734,9 @@
         da_send[at, :] = dot(d_low, half_rows(wo, 1 - c, half), 1, 1).astype(bf16)
 
     da_copy = push(da_send, da.at[pl.ds(rows, rows)], sibling)
-    d1.append(down_first(y))
-    u1 += up_first(1)
+    early = share_start(
+        n_items, it, lambda p: (p, bd), small.at[pl.ds(0, 8)], buf_i, send_i.at[0], recv_i.at[0]
+    )
 
     get_attn.wait()
     get_sib.wait()
@@ -694,20 +744,32 @@
         for xx in range(2):
             part_wo = dot(heads[:, xx * fourth : (xx + 1) * fourth], low[...], 0, 0).astype(bf16)
             for cc in range(2):
-                gw[i, xx, cc] = part_wo[cc * fourth // 2 : (cc + 1) * fourth // 2]
+                gw[i, xx, cc] = part_wo[cc * eighth : (cc + 1) * eighth]
     core_w = [push(gw.at[i, :, 1 - c], gw_core.at[1 - i], sibling) for i in range(2)]
-    early = share_start(
-        n_items, it, lambda p: (p, bd), small.at[pl.ds(0, 8)], buf_i, send_i.at[0], recv_i.at[0]
-    )
+
+    for copy in get_down + get_up:
+        copy.wait()
+    d1.wait_recv()
+    kd[0] += rd1[0]
+    kd[1, 0:half] += rd1[1, 0:half]
+    kd[1, half:width] += rdr[...]
+    d2 = push(kd.at[1 - y], rd2, to_y)
+    u1.wait_recv()
+    for s in range(3):
+        ku[block_order(s)] += ru1[block_order(s)]
+    ku[block_order(3)] += rur[...]
+    theirs, mine = some(1 - x, tile // 4), some(x, tile // 4)
+    u2 = push(ku.at[:, :, theirs], ru2, to_x)
 
     for copy in get_qkv:
         copy.wait()
+    get_h1.wait()
     da_copy.wait_recv()
     lane_k = lax.broadcasted_iota(jnp.int32, (2 * rows, 128), 1)
     lane_q = lax.broadcasted_iota(jnp.int32, (qt, 128), 1)
 
     def pair(i):
-        at_lanes = pl.ds(pl.multiple_of(i * 128, 128), 128)
+        at_lanes = some(i, 128)
         k_pair, v_pair = k[:, at_lanes], v[:, at_lanes]
         bias = key_bias(table, counts, k_pair.shape)
         keys = [with_spare(k_pair, bias, hd, lane_k) for hd in range(2)]
@@ -736,33 +798,63 @@
                     dk_acc[...] += dk_part
                 term = dot(keys_only[hd], ds, 0, 0)
                 dq_both = term if dq_both is None else dq_both + term
-            q[at, at_lanes] = (dq_both.T * score_scale).astype(bf16)
+            dq = dq_both.T * score_scale
+            q[at, at_lanes] = dq.astype(bf16)
+            d_pair[at, 0:128] = dq.astype(bf16)
         k[:, at_lanes] = dk_acc[...].astype(bf16)
         v[:, at_lanes] = dv_acc[...].astype(bf16)
-
-    @pl.loop(0, 2)
-    def _(i):
-        pair(i)
-
+        d_pair[:, 128:256] = dk_acc[...].astype(bf16)
+        d_pair[:, 256:384] = dv_acc[...].astype(bf16)
+        for j in range(4):
+            term = dot(h1[:, j * fourth : (j + 1) * fourth], d_pair[...], 0, 0).astype(bf16)
+            for cc in range(2):
+                gp[i, j, cc] = term[cc * eighth : (cc + 1) * eighth]
+
+    def pair_core(i):
+        return push(gp.at[i, :, 1 - c], gp_core.at[i], sibling)
+
+    def chips(i, first, second):
+        return 2 * second + first if i % 2 == 0 else 2 * first + second
+
+    def first_of(i):
+        return (x, y) if i % 2 == 0 else (y, x)
+
+    def pair_first(i, core):
+        core.wait_recv()
+        mine_first, _ = first_of(i)
+        to = to_x if i % 2 == 0 else to_y
+        got = []
+        for j in range(2):
+            there = chips(i, 1 - mine_first, j)
+            got.append(push(gp.at[i, there, c], gp1.at[i, j, 0], to))
+            got.append(push(gp_core.at[i, there], gp1.at[i, j, 1], to))
+        return got
+
+    def pair_second(i, got):
+        for copy in got:
+            copy.wait_recv()
+        mine_first, mine_second = first_of(i)
+        for j in range(2):
+            here = chips(i, mine_first, j)
+            gp[i, here, c] += gp1[i, j, 0]
+            gp_core[i, here] += gp1[i, j, 1]
+        there = chips(i, mine_first, 1 - mine_second)
+        to = to_y if i % 2 == 0 else to_x
+        return [
+            push(gp.at[i, there, c], gp2.at[i, 0], to),
+            push(gp_core.at[i, there], gp2.at[i, 1], to),
+        ]
+
+    def pair_third(i, got):
+        for copy in got:
+            copy.wait_recv()
+        gp[i, yx, c] += gp2[i, 0]
+        gp_core[i, yx] += gp2[i, 1]
+
+    pair(0)
+    core_p = [pair_core(0)]
     part[...] = share_end(n_items, early, buf_i)
-    early = share_start(
-        n_band, bd, lambda p: (it, p), part, buf_b, send_b.at[0], recv_b.at[0]
-    )
-    for copy in get_kd:
-        copy.wait()
-    d1[0].wait_recv()
-    kd[1 - y] += rd1[1 - y]
-    d2 = push(kd.at[1 - y], rd2, to_y)
-    for copy in get_ku:
-        copy.wait()
-
-    def up_second(high):
-        for copy in u1[4 * high : 4 * high + 4]:
-            copy.wait_recv()
-        ku[high] += ru1[high]
-        return push(ku.at[high, :, :, pl.ds(pl.multiple_of((1 - x) * tile // 4, 128), tile // 4)], ru2.at[high], to_x)
-
-    u2 = [up_second(0)]
+    early = share_start(n_band, bd, lambda p: (it, p), part, buf_b, send_b.at[0], recv_b.at[0])
     for i in range(2):
         core_w[i].wait_recv()
     for i in range(2):
@@ -770,45 +862,53 @@
     rel_y = lax.rem(y + c, 2)
     w1 = push(gw.at[1 - rel_y, :, c], gw1, to_y)
 
-    @pl.loop(2, q.shape[1] // 128)
-    def _(i):
-        pair(i)
-
+    pair(1)
+    core_p.append(pair_core(1))
+    p1 = [pair_first(0, core_p[0])]
     total[0:8, :] = share_end(n_band, early, buf_b)
 
-    get_h1.wait()
-    core_p = []
-    for j in range(4):
-        for i, d in enumerate((q, k, v)):
-            part_p = dot(h1[:, j * fourth : (j + 1) * fourth], d[...], 0, 0).astype(bf16)
-            for cc in range(2):
-                gp[i, j, cc] = part_p[cc * fourth // 2 : (cc + 1) * fourth // 2]
-        core_p.append(push(gp.at[:, j, 1 - c], gp_core.at[:, j], sibling))
+    pair(2)
+    core_p.append(pair_core(2))
+    p1.append(pair_first(1, core_p[1]))
+    d2.wait_recv()
+    kd[y] += rd2[...]
+    down = kd.reshape(2, 2, 2, fourth, tile)
+    d3 = push(down.at[y, :, 1 - bl], rd3, to_z1)
+    u2.wait_recv()
+    ku[:, :, mine] += ru2[...]
+    up = ku.reshape(2, 2, 2, tile // 2, tile)
+    u3 = push(up.at[:, 1 - bl, :, mine], ru3, to_z1)
+
+    pair(3)
+    core_p.append(pair_core(3))
+    p1.append(pair_first(2, core_p[2]))
     for i, d in ((0, q), (1, v)):
         row = jnp.sum(d[...].astype(f32), 0, keepdims=True)
-        small[12 + i : 13 + i, pl.ds(pl.multiple_of(c * half, 128), half)] = row
+        small[12 + i : 13 + i, some(c, half)] = row
+    w1.wait_recv()
+    gw[rel_y, :, c] += gw1[...]
+    w2 = push(gw.at[rel_y, 1 - x, c], gw2, to_x)
 
     for copy in get_w:
         copy.wait()
     dh1, dh1_sib = wo, low
 
-    @pl.loop(0, 2 * rows // block)
-    def _(i):
-        at = pl.ds(pl.multiple_of(lax.rem(i + rows // block, 2 * rows // block) * block, block), block)
+    def first_norm_terms(i):
+        at = some(i, block)
         term = dot(q[at, :], wq[...], 1, 1) + dot(k[at, :], wk[...], 1, 1)
         dh1[at, :] = (term + dot(v[at, :], wv[...], 1, 1)).astype(bf16)
 
+    @pl.loop(rows // block, 2 * rows // block)
+    def _(i):
+        first_norm_terms(i)
+
     dh_copy = push(dh1.at[pl.ds(rows, rows)], dh1_sib, sibling)
-    for copy in core_p:
-        copy.wait_recv()
-    qk1, v1 = [], []
-    for j in range(2):
-        yx_x = 2 * j + 1 - x
-        qk1.append(push(gp.at[pl.ds(0, 2), yx_x, c], gqk1.at[0, j], to_x))
-        qk1.append(push(gp_core.at[pl.ds(0, 2), yx_x], gqk1.at[1, j], to_x))
-        yx_y = 2 * (1 - y) + j
-        v1.append(push(gp.at[2, yx_y, c], gv1.at[0, j], to_y))
-        v1.append(push(gp_core.at[2, yx_y], gv1.at[1, j], to_y))
+    p1.append(pair_first(3, core_p[3]))
+    p2 = [pair_second(0, p1[0])]
+
+    @pl.loop(0, rows // block)
+    def _(i):
+        first_norm_terms(i)
 
     get_tok.wait()
     dh_copy.wait_recv()
@@ -816,7 +916,7 @@
 
     @pl.loop(0, rows // block)
     def _(i):
-        at = pl.ds(pl.multiple_of(i * block, block), block)
+        at = some(i, block)
         inv = stat[S_INV : S_INV + 1, :]
         centred = tok[at, :].astype(f32) - stat[S_MEAN : S_MEAN + 1, :]
         z, scale = normalize(centred * inv)
@@ -831,16 +931,53 @@
     )
     g_blocks = g_rows.reshape(4, rows // 4, width)
     rows_back(g_blocks, home, send_g, recv_g)
+    p2.append(pair_second(1, p1[1]))
     part2[...] = share_end(n_items, late, buf_i2)
-    late = share_start(
-        n_band, bd, lambda p: (it, p), part2, buf_b2, send_b.at[1], recv_b.at[1]
-    )
-
-    d1[1].wait_recv()
-    kd[y] += rd1[y]
-    u2.append(up_second(1))
+    late = share_start(n_band, bd, lambda p: (it, p), part2, buf_b2, send_b.at[1], recv_b.at[1])
+
+    d3.wait_recv()
+    for high in range(2):
+        down[y, high, bl] += rd3[high]
+    d4 = push(down.at[y, 1 - bh, bl], rd4, to_z2)
+    u3.wait_recv()
+    for high in range(2):
+        up[high, bl, :, mine] += ru3[high]
+    u4 = push(up.at[1 - bh, bl, :, mine], ru4, to_z2)
+    p2.append(pair_second(2, p1[2]))
+    w2.wait_recv()
+    gw[rel_y, x, c] += gw2[...]
+
+    def z_lanes(which):
+        return some(which, fourth)
+
+    w3 = [
+        push(gw.at[rel_y, x, c, :, z_lanes(2 * high + 1 - bl)], gw3.at[high], to_z1) for high in range(2)
+    ]
+    p2.append(pair_second(3, p1[3]))
     sums = share_end(n_band, late, buf_b2)
     total[8:16, :] = sums
+
+    for i in range(4):
+        pair_third(i, p2[i])
+    p3 = []
+    for i in range(2):
+        there = 2 * (1 - bl) + i
+        p3.append(push(gp.at[there, yx, c], gp3.at[i, 0], to_z1))
+        p3.append(push(gp_core.at[there, yx], gp3.at[i, 1], to_z1))
+
+    for high in range(2):
+        w3[high].wait_recv()
+    for high in range(2):
+        gw3[high] = gw[rel_y, x, c, :, z_lanes(2 * high + bl)] + gw3[high]
+    w4 = push(gw3.at[1 - bh], gw4, to_z2)
+    for copy in p3:
+        copy.wait_recv()
+    for i in range(2):
+        here = 2 * bl + i
+        gp3[i, 0] = gp[here, yx, c] + gp3[i, 0]
+        gp3[i, 1] = gp_core[here, yx] + gp3[i, 1]
+    rel_b = lax.rem(bh + c, 2)
+    p4 = push(gp3.at[:, 1 - rel_b], gp4, to_z2)
 
     count = patch_total(counts, (1, width))
     inv = stat[S_INV : S_INV + 1, :]
@@ -853,95 +990,22 @@
         rows_back_got(g_blocks, home, send_g, recv_g, i)
         now = pl.ds(h * cut, cut)
         valid = position + h * cut < counts[table[it * 2 + s]]
-        term = fix + slope * (tokens_h[s, now, :].astype(f32) - stat[S_BATCH : S_BATCH + 1, :])
+        term = fix + slope * (tokens[s, now, :].astype(f32) - stat[S_BATCH : S_BATCH + 1, :])
         d_tok[s, now, :] = (home[s, now, :].astype(f32) + jnp.where(valid, term, 0.0)).astype(bf16)
 
-    d2.wait_recv()
-    kd[y] += rd2[...]
-    blocks = kd.reshape(2, 2, 2, width // 4, tile)
-    d3 = push(blocks.at[y, :, 1 - bl], rd3, to_z1)
-    w1.wait_recv()
-    gw[rel_y, :, c] += gw1[...]
-    w2 = push(gw.at[rel_y, 1 - x, c], gw2, to_x)
-    for copy in v1:
-        copy.wait_recv()
-    for j in range(2):
-        gp[2, 2 * y + j, c] += gv1[0, j]
-        gp_core[2, 2 * y + j] += gv1[1, j]
-    v2 = [
-        push(gp.at[2, 2 * y + 1 - x, c], gv2.at[0], to_x),
-        push(gp_core.at[2, 2 * y + 1 - x], gv2.at[1], to_x),
-    ]
-    for copy in qk1:
-        copy.wait_recv()
-    for i in range(2):
-        for j in range(2):
-            gp[i, 2 * j + x, c] += gqk1[0, j, i]
-            gp_core[i, 2 * j + x] += gqk1[1, j, i]
-    qk2 = [
-        push(gp.at[pl.ds(0, 2), 2 * (1 - y) + x, c], gqk2.at[0], to_y),
-        push(gp_core.at[pl.ds(0, 2), 2 * (1 - y) + x], gqk2.at[1], to_y),
-    ]
-    for copy in u2:
-        copy.wait_recv()
-    mine = pl.ds(pl.multiple_of(x * tile // 4, 128), tile // 4)
-    for high in range(2):
-        ku[high, :, :, mine] += ru2[high]
-    u3 = push(ku.at[:, 1 - bl, :, mine], ru3, to_z1)
-    d3.wait_recv()
-    for high in range(2):
-        blocks[y, high, bl] += rd3[high]
-    d4 = push(blocks.at[y, 1 - bh, bl], rd4, to_z2)
-    w2.wait_recv()
-    gw[rel_y, x, c] += gw2[...]
-
-    def z_lanes(which):
-        return pl.ds(pl.multiple_of(which * fourth, 128), fourth)
-
-    w3 = [
-        push(gw.at[rel_y, x, c, :, z_lanes(2 * high + 1 - bl)], gw3.at[high], to_z1) for high in range(2)
-    ]
-    for copy in v2:
-        copy.wait_recv()
-    here = 2 * y + x
-    gp[2, here, c] += gv2[0]
-    gp_core[2, here] += gv2[1]
-    for copy in qk2:
-        copy.wait_recv()
-    for i in range(2):
-        gp[i, here, c] += gqk2[0, i]
-        gp_core[i, here] += gqk2[1, i]
-    p3 = [
-        push(gp.at[:, here, c, :, z_lanes(1 - bl)], gp3.at[0], to_z1),
-        push(gp_core.at[:, here, :, z_lanes(1 - bl)], gp3.at[1], to_z1),
-    ]
-    u3.wait_recv()
-    for high in range(2):
-        ku[high, bl, :, mine] += ru3[high]
-    u4 = push(ku.at[1 - bh, bl, :, mine], ru4, to_z2)
-    for high in range(2):
-        w3[high].wait_recv()
-    w_mine = [gw[rel_y, x, c, :, z_lanes(2 * high + bl)] + gw3[high] for high in range(2)]
-    gw3[0] = w_mine[0]
-    gw3[1] = w_mine[1]
-    w4 = push(gw3.at[1 - bh], gw4, to_z2)
-    for copy in p3:
-        copy.wait_recv()
-    gp3[0] = gp[:, here, c, :, z_lanes(bl)] + gp3[0]
-    gp3[1] = gp_core[:, here, :, z_lanes(bl)] + gp3[1]
-    rel_b = lax.rem(bh + c, 2)
-    p4 = push(gp3.at[1 - rel_b], gp4, to_z2)
     d4.wait_recv()
-    o_down[...] = (blocks[y, bh, bl].astype(f32) + rd4[...].astype(f32)).T
+    o_down[...] = (down[y, bh, bl].astype(f32) + rd4[...].astype(f32)).T
     u4.wait_recv()
-    up = ku[bh, bl, :, mine].astype(f32) + ru4[...].astype(f32)
+    up_sum = up[bh, bl, :, mine].astype(f32) + ru4[...].astype(f32)
     for i, h in ((0, 1 - c), (1, c)):
-        o_up[:, pl.ds(pl.multiple_of(h * tile, 128), tile)] = up[i]
+        o_up[:, some(h, tile)] = up_sum[i]
     w4.wait_recv()
     o_wo[...] = gw3[bh].astype(f32) + gw4[...].astype(f32)
     p4.wait_recv()
-    for i, ref in enumerate((o_wq, o_wk, o_wv)):
-        ref[...] = gp3[rel_b, i].astype(f32) + gp4[i].astype(f32)
+    for i in range(2):
+        all_three = gp3[i, rel_b].astype(f32) + gp4[i].astype(f32)
+        for j, ref in enumerate((o_wq, o_wk, o_wv)):
+            ref[:, i * 128 : (i + 1) * 128] = all_three[:, j * 128 : (j + 1) * 128]
 
     for i in range(4):
         rows_back_got(out_rows, out_home, send_r, recv_r, i)
@@ -951,12 +1015,12 @@
         copy.wait_send()
 
 
-def tail(table, counts, stat, vecs, dbu_a, dbu_b, log_total, res, dh, cot, out_rows, attn, attn_sib, wo, *rest, qt=512):
-    (q, k, v, h1, wq, wk, wv, tok, down, up_a, up_b, tokens) = rest
+def tail(table, counts, stat, vecs, dbu_a, dbu_b, log_total, res, dh, cot, out_rows, *rest, qt=512):
+    attn, attn_sib, wo, q, k, v, h1, wq, wk, wv, tok, kd, rd, rest_d, ku, ru, rest_u, tokens = rest
     n_items, n_band = lax.axis_size("items"), lax.axis_size("band")
     rows, width = res.shape
     half, fourth, cut = width // 2, width // 4, rows // 4
-    tile = down.shape[2]
+    tile = kd.shape[2]
     buf = lambda *shape: pltpu.VMEM(shape, bf16)
     buf32 = lambda *shape: pltpu.VMEM(shape, f32)
     out = lambda *shape: jax.ShapeDtypeStruct(shape, f32)
@@ -964,7 +1028,7 @@
     return pl.pallas_call(
         functools.partial(tail_kernel, n_items, n_band, qt),
         name="tail",
-        in_specs=[SMEM, SMEM] + [VMEM] * 5 + [HBM] * 18 + [VMEM],
+        in_specs=[SMEM, SMEM] + [VMEM] * 5 + [HBM] * 21 + [VMEM],
         out_specs=[HBM] + [VMEM] * 8,
         out_shape=[
             jax.ShapeDtypeStruct(tokens.shape, bf16),
@@ -980,20 +1044,21 @@
         scratch_shapes=[
             buf32(rows, width), buf32(rows, width), buf(rows, width), buf(rows, width),
             buf(width, width), buf(rows, half), buf(rows, half),
-            buf(2, width, tile), buf(2, width, tile), buf(width, tile), buf(2, s, tile), buf(s, tile),
-            buf(2, 2, 2, tile // 2, tile), buf(2, 2, 2, tile // 2, tile), buf(2, 2, 2, tile // 4, tile),
-            buf(2, 2, tile // 4, tile), buf(2, tile // 4, tile),
+            buf(2, width, tile), buf(2, width, tile), buf(half, tile), buf(width, tile), buf(2, s, tile),
+            buf(s, tile),
+            buf(4, 2, tile // 2, tile), buf(4, 2, tile // 2, tile), buf(2, tile // 2, tile),
+            buf(4, 2, tile // 4, tile), buf(2, 2, tile // 4, tile), buf(2, tile // 4, tile),
             buf(2 * rows, half), buf(2 * rows, half), buf(2 * rows, half),
             buf(2 * rows, half), buf(rows, half), buf32(2 * rows, 128), buf32(2 * rows, 128),
             buf(2 * rows, width), buf(width, half), buf(width, half), buf(width, half), buf(rows, width),
             buf(2, 2, 2, e, width), buf(2, 2, e, width), buf(2, e, width), buf(e, width),
             buf(2, e, s), buf(e, s),
-            buf(3, 4, 2, e, half), buf(3, 4, e, half), buf(2, 2, 2, e, half), buf(2, 2, e, half),
-            buf(2, 2, e, half), buf(2, e, half), buf(2, 3, e, s), buf(3, e, s),
+            buf(2 * rows, 384), buf(4, 4, 2, e, 384), buf(4, 4, e, 384), buf(4, 2, 2, e, 384),
+            buf(4, 2, e, 384), buf(2, 2, e, 384), buf(2, e, 384),
             buf(2, 2 * cut, width),
             buf32(16, width), buf32(n_items, 8, width), buf32(8, width), buf32(n_band, 8, width),
             buf32(n_items, 8, width), buf32(8, width), buf32(n_band, 8, width),
-            DMA((48,)), DMA((48,)), DMA((32,)),
+            DMA((64,)), DMA((64,)), DMA((24,)),
             DMA((4,)), DMA((4,)), DMA((4,)), DMA((4,)),
             DMA((2, n_items)), DMA((2, n_items)), DMA((2, n_band)), DMA((2, n_band)),
         ],
@@ -1004,7 +1069,7 @@
     )(
         table, counts, stat, vecs, dbu_a, dbu_b, log_total, res, dh, cot,
         out_rows.reshape(4, cut, width), attn, attn_sib, wo, q, k, v, h1, wq, wk, wv, tok,
-        down, up_a, up_b, tokens,
+        kd, rd, rest_d, ku, ru, rest_u, tokens,
     )
 
 
@@ -1024,13 +1089,13 @@
     attn, log_total, cot_rows, attn_sib = attend(slot_table, patch_counts, q, k, v, cotangent)
     cot_rows = cot_rows.reshape(rows, width)
     res, h2, h2p = join(stat, vecs, attn, attn_sib, w_out, tok)
-    out_rows, d_h2, d_down, d_up_a, d_up_b, dbu_a, dbu_b = mlp(
+    out_rows, d_h2, kd, rd, rest_d, ku, ru, rest_u, dbu_a, dbu_b = mlp(
         vecs, h2, h2p, cot_rows, res, w_up, w_down
     )
     output, d_tokens, small, d_w_down, d_w_up, d_w_out, d_wq, d_wk, d_wv = tail(
         slot_table, patch_counts, stat, vecs, dbu_a, dbu_b, log_total, res, d_h2, cot_rows,
         out_rows, attn, attn_sib, w_out, q, k, v, h1, w_query, w_key, w_value, tok,
-        d_down, d_up_a, d_up_b, tokens,
+        kd, rd, rest_d, ku, ru, rest_u, tokens,
     )
     d_gain_two, d_shift_two, d_bo, d_bdown = (small[i] for i in range(4))
     d_gain_one, d_shift_one, d_bq, d_bv = (small[i] for i in range(10, 14))

time: 312 us -> 288 us (0.923)
  the two profiles are of different devices: /device:TPU:0 before, /device:TPU:8 now
where the time goes in v4:
time: 288 us; the launch traced here: 282 us
  Pallas kernels  262 us (91%)
  local copies, waits for them, and re-layouts  13.1 us (5%)
  other arithmetic  6.16 us (2%)
    pallas_call x1, Pallas kernels, tail(): pl.pallas_call(functools.partial(tail_kernel, n_items, n_band, qt), name=...  135 us
    pallas_call x1, Pallas kernels, mlp(): pl.pallas_call(mlp_kernel, name='mlp', grid=(steps + 1,), in_specs=[VMEM]...  53.3 us
    pallas_call x1, Pallas kernels, gather(): pl.pallas_call(functools.partial(gather_kernel, n_items, n_band), name='g...  33.8 us
    pallas_call x1, Pallas kernels, attend(): pl.pallas_call(functools.partial(attend_kernel, qt), name='attend', grid=...  26.4 us
    unnamed x28, local copies, waits for them, and re-layouts  10.3 us
    pallas_call x1, Pallas kernels, project(): pl.pallas_call(project_kernel, name='project', grid=(rows // block,), in_...  8.1 us

profile of v4, /device:TPU:8, one launch (start us, length us, event | category | flops | bytes accessed | tf_op | source)
XLA Modules:
  0.0 282.4 jit_solution(118203373764263540)
XLA Ops:
  0.7 0.7 constant_dynamic-update-slice_fusion.9
  1.3 0.7 constant_dynamic-update-slice_fusion.8
  2.0 0.7 constant_dynamic-update-slice_fusion.7
  2.7 0.7 constant_dynamic-update-slice_fusion.6
  3.4 0.7 constant_dynamic-update-slice_fusion.5
  4.1 0.7 constant_dynamic-update-slice_fusion.4
  4.8 0.7 constant_dynamic-update-slice_fusion.3
  5.5 0.7 constant_dynamic-update-slice_fusion.2
  6.1 0.7 constant_dynamic-update-slice_fusion.1
  6.8 0.7 constant_dynamic-update-slice_fusion
  7.5 0.7 convert_dynamic-update-slice_fusion
  8.8 33.8 %gather.1 = (bf16[8,128,1024]{2,1,0:T(8,128)(2,1)}, f32[4,1024]{1,0:T(4,128)}) custom-call(s32[16]{0:T(128)} %refs_0_.3, s32[16]{0:T(128)} %refs_1_.3, f32[14,1024]{1,0:T(8,128)} %reshape.53.vecs.refs_3_, bf16[2,256,1024]{2,1,0:T(8,128)(2,1)} %refs_28_.1), custom_call_target="tpu_custom_call" | custom-call | tf_op jit(solution)/shard_map/gather/pallas_call | solution.py:217
  42.6 8.1 %project.1 = (bf16[1024,1024]{1,0:T(8,128)(2,1)}, bf16[1024,512]{1,0:T(8,128)(2,1)}, bf16[1024,512]{1,0:T(8,128)(2,1)}, bf16[1024,512]{1,0:T(8,128)(2,1)}) custom-call(f32[4,1024]{1,0:T(4,128)} %get-tuple-element.51.stat.refs_2_, f32[14,1024]{1,0:T(8,128)} %reshape.53.vecs.refs_3_, bf16[1024,1024]{1,0:T(8,128)(2,1)} %bitcast.18, ...), custom_call_target="tpu_custom_call" | custom-call | flops 3221225472 | bytes 12582912 | tf_op jit(solution)/shard_map/project/pallas_call | solution.py:263
  50.7 26.4 %attend.1 = (bf16[512,512]{1,0:T(8,128)(2,1)}, f32[4,2,1024]{2,1,0:T(2,128)}, bf16[4,128,1024]{2,1,0:T(8,128)(2,1)}, bf16[512,512]{1,0:T(8,128)(2,1)}) custom-call(s32[16]{0:T(128)} %refs_0_.3, s32[16]{0:T(128)} %refs_1_.3, bf16[1024,512]{1,0:T(8,128)(2,1)} %get-tuple-element.53.q.refs_14_, bf16[1024,512]{1,0:T(8,128)(2,1)} %get-tuple-element.54.k.refs_15_, ...), custom_call_target="tpu_custom_call" | custom-call | flops 8589934592 | bytes 5242880 | tf_op jit(solution)/shard_map/attend/pallas_call | solution.py:365
  77.2 5.3 %join.1 = (f32[512,1024]{1,0:T(8,128)}, bf16[512,1024]{1,0:T(8,128)(2,1)}, bf16[512,1024]{1,0:T(8,128)(2,1)}) custom-call(f32[4,1024]{1,0:T(4,128)} %get-tuple-element.51.stat.refs_2_, f32[14,1024]{1,0:T(8,128)} %reshape.53.vecs.refs_3_, bf16[512,512]{1,0:T(8,128)(2,1)} %get-tuple-element.56.attn_a.refs_11_, ...), custom_call_target="tpu_custom_call" | custom-call | flops 1073741824 | bytes 8388608 | tf_op jit(solution)/shard_map/join/pallas_call | solution.py:421
  82.5 53.3 %mlp.1 = (bf16[512,1024]{1,0:T(8,128)(2,1)}, f32[512,1024]{1,0:T(8,128)}, bf16[2,1024,512]{2,1,0:T(8,128)(2,1)}, bf16[2,1024,512]{2,1,0:T(8,128)(2,1)}, bf16[512...) custom-call(f32[14,1024]{1,0:T(8,128)} %reshape.53.vecs.refs_3_, ...), custom_call_target="tpu_custom_call" | custom-call | flops 25769803776 | bytes 41943040 | tf_op jit(solution)/shard_map/mlp/pallas_call | solution.py:603
  135.8 135.0 %tail.1 = (bf16[2,256,1024]{2,1,0:T(8,128)(2,1)}, bf16[2,256,1024]{2,1,0:T(8,128)(2,1)}, f32[16,1024]{1,0:T(8,128)}, f32[512,256]{1,0:T(8,128)}, f32[128,1024]{1...) custom-call(s32[16]{0:T(128)} %refs_0_.3, s32[16]{0:T(128)} %refs_1_.3, ...), custom_call_target="tpu_custom_call" | custom-call | flops 32212254720 | bytes 41943040 | tf_op jit(solution)/shard_map/tail/pallas_call | solution.py:1028
  270.8 1.6 fusion
  272.4 0.8 slice_bitcast_fusion
  274.4 2.3 copy.61
  276.8 1.0 copy.62
  277.8 0.7 copy.63
  280.4 0.8 copy.67
  281.2 0.8 copy.68
  (22 shorter events, 3.9 us)
Async XLA Ops:
  135.8 138.0 %copy-start.7 = (f32[4,1024]{1,0:T(4,128)S(1)}, f32[4,1024]{1,0:T(4,128)}, u32[]{:S(2)}) copy-start(f32[4,1024]{1,0:T(4,128)} %get-tuple-element.51.stat.refs_2_) | copy-start | bytes 49156
  270.8 6.0 %copy-start = (bf16[2,256,1024]{2,1,0:T(8,128)(2,1)S(1)}, bf16[2,256,1024]{2,1,0:T(8,128)(2,1)}, u32[]{:S(2)}) copy-start(bf16[2,256,1024]{2,1,0:T(8,128)(2,1)} %get-tuple-element.113) | copy-start | bytes 3145732
  274.4 3.3 %copy-start.6 = (f32[128,256]{1,0:T(8,128)S(1)}, f32[128,256]{1,0:T(8,128)}, u32[]{:S(2)}) copy-start(f32[128,256]{1,0:T(8,128)} %get-tuple-element.118) | copy-start | bytes 393220
  274.4 4.0 %copy-start.5 = (f32[128,256]{1,0:T(8,128)S(1)}, f32[128,256]{1,0:T(8,128)}, u32[]{:S(2)}) copy-start(f32[128,256]{1,0:T(8,128)} %get-tuple-element.120) | copy-start | bytes 393220
  274.4 4.7 %copy-start.4 = (f32[128,256]{1,0:T(8,128)S(1)}, f32[128,256]{1,0:T(8,128)}, u32[]{:S(2)}) copy-start(f32[128,256]{1,0:T(8,128)} %get-tuple-element.121) | copy-start | bytes 393220
  274.4 5.3 %copy-start.3 = (f32[128,256]{1,0:T(8,128)S(1)}, f32[128,256]{1,0:T(8,128)}, u32[]{:S(2)}) copy-start(f32[128,256]{1,0:T(8,128)} %get-tuple-element.123) | copy-start | bytes 393220
  274.4 6.0 %copy-start.2 = (f32[128,1024]{1,0:T(8,128)S(1)}, f32[128,1024]{1,0:T(8,128)}, u32[]{:S(2)}) copy-start(f32[128,1024]{1,0:T(8,128)} %get-tuple-element.127) | copy-start | bytes 1572868
  276.8 4.4 %copy-start.1 = (f32[512,256]{1,0:T(8,128)S(1)}, f32[512,256]{1,0:T(8,128)}, u32[]{:S(2)}) copy-start(f32[512,256]{1,0:T(8,128)} %get-tuple-element.129) | copy-start | bytes 1572868

commit v5 on v4

--- a/solution.py
+++ b/solution.py
@@ -159,13 +159,93 @@
     return column_peers() + others
 
 
-def gather_kernel(n_items, n_band, table, counts, vecs, tok, rows, stat, one, buf_i, part, buf_b, *sems):
-    (send_t, recv_t, send_s, recv_s, send_i, recv_i, send_b, recv_b) = sems
+def patch_total(counts, shape):
+    total = counts[0]
+    for i in range(1, counts.shape[0]):
+        total = total + counts[i]
+    return jnp.full(shape, total, jnp.int32).astype(f32)
+
+
+VMEM = pl.BlockSpec(memory_space=pltpu.VMEM)
+SMEM = pl.BlockSpec(memory_space=pltpu.SMEM)
+HBM = pl.BlockSpec(memory_space=pltpu.HBM)
+DMA = pltpu.SemaphoreType.DMA
+
+
+def half_lanes(ref, row, half):
+    at = pl.multiple_of(lax.rem(lax.axis_index("items"), 2) * half, 128)
+    return ref[row : row + 1, pl.ds(at, half)]
+
+
+def half_rows(ref, which, half):
+    return ref[pl.ds(pl.multiple_of(which * half, 128), half), :]
+
+
+def head_lanes(array, head, lane):
+    keep = (lane >= head * HEAD_DIM) & (lane < (head + 1) * HEAD_DIM)
+    return jnp.where(keep, array, jnp.zeros_like(array))
+
+
+def with_spare(array, spare_value, head, lane):
+    spare = (1 - head) * HEAD_DIM
+    return jnp.where(lane == spare, spare_value, head_lanes(array, head, lane))
+
+
+def ones_beside(array, head, lane):
+    return with_spare(array, jnp.ones_like(array), head, lane)
+
+
+def key_bias(table, counts, shape):
+    it, bd, c, yx = place()
+    cut = shape[0] // 8
+    row = lax.broadcasted_iota(jnp.int32, shape, 0)
+    there = row >= 4 * cut
+    row = jnp.where(there, row - 4 * cut, row)
+    band = row // cut
+    half = jnp.where(there, 1 - c, c)
+    position = band * (2 * cut) + half * cut + (row - band * cut)
+    return jnp.where(position < counts[table[yx * 4 + bd]], 0.0, masked_score).astype(bf16)
+
+
+def normalize(value):
+    centre = value - jnp.mean(value, -1, keepdims=True)
+    scale = lax.rsqrt(jnp.mean(centre * centre, -1, keepdims=True) + epsilon)
+    return centre * scale, scale
+
+
+def front_kernel(n_items, n_band, qt, table, counts, *refs):
+    singles = refs[:10]
+    (b_up, tok, cot, wq_h, wk_h, wv_h, wo_h) = refs[10:17]
+    (vecs, stat, rows_h, cot_rows, h1_h, q_h, k_h, v_h, log_total, attn_h, attn_sib_h) = refs[17:28]
+    (res, h2, h2p) = refs[28:31]
+    (rows, wq, wk, wv, wo, h1, q, k, v, attn, attn_sib, part_sib) = refs[31:43]
+    (one, buf_i, part, buf_b) = refs[43:47]
+    (send_t, recv_t, send_c, recv_c, send_s, recv_s, send_a, recv_a) = refs[47:55]
+    (send_i, recv_i, send_b, recv_b, lsem) = refs[55:60]
     it, bd, c, yx = place()
     sibling = (it + 1 - 2 * c, bd)
+    slots, band_rows, width = tok.shape
+    cut = band_rows // 2
+    half = width // 2
+    own = 4 * cut
+    local = []
+
+    def move(src, dst):
+        copy = pltpu.make_async_copy(src, dst, lsem.at[len(local)])
+        copy.start()
+        local.append(copy)
+        return copy
+
     greet(all_peers(n_items))
     rows_out(tok, rows, send_t, recv_t)
-    slots, band_rows, width = tok.shape
+    lanes = pl.ds(pl.multiple_of(c * half, 128), half)
+    get_w = [move(src.at[:, lanes], dst) for src, dst in ((wq_h, wq), (wk_h, wk), (wv_h, wv))]
+    get_wo = move(wo_h, wo)
+    for i, ref in enumerate(singles):
+        vecs[i : i + 1, :] = ref[...].astype(f32).reshape(1, width)
+    for i in range(b_up.shape[0] // width):
+        vecs[R_BU + i : R_BU + i + 1, :] = b_up[pl.ds(i * width, width)].astype(f32).reshape(1, width)
+
     at = lax.broadcasted_iota(jnp.int32, (band_rows, width), 0) + bd * band_rows
     first = jnp.zeros((1, width), f32)
     second = jnp.zeros((1, width), f32)
@@ -186,254 +266,171 @@
     stat[S_VAR : S_VAR + 1, :] = new_var
     stat[S_BATCH : S_BATCH + 1, :] = mean
     stat[S_INV : S_INV + 1, :] = lax.rsqrt(new_var + epsilon)
-    hand = []
-    for o in range(4):
-        band = lax.rem(bd + o, 4)
-        rows_out_got(tok, rows, send_t, recv_t, band)
-        copy = remote(rows.at[band], rows.at[4 + band], send_s.at[o], recv_s.at[o], sibling)
-        copy.start()
-        hand.append(copy)
-    for copy in hand:
+    for copy in get_w:
         copy.wait()
+
+    def hand(o):
+        band = jnp.bitwise_xor(bd, o)
+        return remote(rows.at[band], rows.at[4 + band], send_s.at[o], recv_s.at[o], sibling)
+
+    def project(o, base):
+        bands = [jnp.bitwise_xor(bd, o), jnp.bitwise_xor(bd, o + 1)]
+        x = jnp.concatenate([rows[base + band] for band in bands]).astype(f32)
+        start = (x - stat[S_MEAN : S_MEAN + 1, :]) * stat[S_INV : S_INV + 1, :]
+        z, _ = normalize(start)
+        h = (z * vecs[R_G1 : R_G1 + 1, :] + vecs[R_S1 : R_S1 + 1, :]).astype(bf16)
+        q_new = ((dot(h, wq[...]) + half_lanes(vecs, R_BQ, half)).astype(bf16) * score_scale).astype(bf16)
+        k_new = dot(h, wk[...]).astype(bf16)
+        v_new = (dot(h, wv[...]) + half_lanes(vecs, R_BV, half)).astype(bf16)
+        for i, band in enumerate(bands):
+            to = pl.ds(pl.multiple_of((base + band) * cut, 128), cut)
+            for ref, new in ((h1, h), (q, q_new), (k, k_new), (v, v_new)):
+                ref[to, :] = new[i * cut : (i + 1) * cut]
+
+    for o in (0, 2):
+        for i in (o, o + 1):
+            rows_out_got(tok, rows, send_t, recv_t, jnp.bitwise_xor(bd, i))
+            hand(i).start()
+        if o == 2:
+            rows_out(cot, cot_rows, send_c, recv_c)
+        project(o, 0)
+        for i in (o, o + 1):
+            hand(i).wait_recv()
+        project(o, 4)
+    move(rows.at[pl.ds(0, 4)], rows_h)
+    for src, dst in ((h1, h1_h), (q, q_h), (k, k_h), (v, v_h)):
+        move(src, dst)
+
+    lane_k = lax.broadcasted_iota(jnp.int32, (2 * own, 128), 1)
+    lane_q = lax.broadcasted_iota(jnp.int32, (qt, 128), 1)
+    row_out = lax.broadcasted_iota(jnp.int32, (128, qt), 0)
+
+    def hand_attn(i):
+        to = attn_sib.at[:, pl.ds(pl.multiple_of(i * 128, 128), 128)]
+        return remote(part_sib.at[i], to, send_a.at[i], recv_a.at[i], sibling)
+
+    @pl.loop(0, half // 128)
+    def _(i):
+        at_lanes = pl.ds(pl.multiple_of(i * 128, 128), 128)
+        k_pair, v_pair = k[:, at_lanes], v[:, at_lanes]
+        bias = key_bias(table, counts, k_pair.shape)
+        keys = [with_spare(k_pair, bias, hd, lane_k) for hd in range(2)]
+        values = [ones_beside(v_pair, hd, lane_k).T for hd in range(2)]
+        for t in range(2 * own // qt):
+            at = slice(t * qt, (t + 1) * qt)
+            q_tile = q[at, at_lanes]
+            scores = [dot(keys[hd], ones_beside(q_tile, hd, lane_q), 1, 1) for hd in range(2)]
+            tops = [jnp.max(s, 0, keepdims=True) for s in scores]
+            weights = [jnp.exp(s - top).astype(bf16) for s, top in zip(scores, tops)]
+            parts = []
+            for hd in range(2):
+                both = dot(values[hd], weights[hd])
+                spare = (1 - hd) * HEAD_DIM
+                total = both[spare : spare + 1, :]
+                log_total[i, hd : hd + 1, at] = tops[hd] + jnp.log(total)
+                parts.append(both * (1.0 / total))
+            both = jnp.where(row_out < HEAD_DIM, parts[0], parts[1]).T.astype(bf16)
+            if t * qt < own:
+                attn[at, at_lanes] = both
+            else:
+                part_sib[i, t * qt - own : (t + 1) * qt - own, :] = both
+        hand_attn(i).start()
+
+    move(attn, attn_h)
+    get_wo.wait()
+    for i in range(half // 128):
+        hand_attn(i).wait_recv()
+    move(attn_sib, attn_sib_h)
+
+    block = 256
+
+    @pl.loop(0, own // block)
+    def _(i):
+        at = pl.ds(pl.multiple_of(i * block, block), block)
+        x = rows[pl.ds(i * (block // cut), block // cut)].reshape(block, width).astype(f32)
+        start = (x - stat[S_MEAN : S_MEAN + 1, :]) * stat[S_INV : S_INV + 1, :]
+        r = dot(attn[at, :], half_rows(wo, c, half)) + dot(attn_sib[at, :], half_rows(wo, 1 - c, half))
+        r = start + r + vecs[R_BO : R_BO + 1, :]
+        res[at, :] = r
+        z, _ = normalize(r)
+        h = (z * vecs[R_G2 : R_G2 + 1, :] + vecs[R_S2 : R_S2 + 1, :]).astype(bf16)
+        h2[at, :] = h
+        e = width // 8
+        for j in range(4):
+            even = h[:, 2 * j * e : (2 * j + 1) * e]
+            odd = h[:, (2 * j + 1) * e : (2 * j + 2) * e]
+            h2p[at, j * e : (j + 1) * e] = jnp.where(c == 0, even, odd)
+            h2p[at, half + j * e : half + (j + 1) * e] = jnp.where(c == 0, odd, even)
+
+    for band in range(4):
+        rows_out_got(cot, cot_rows, send_c, recv_c, band)
+        hand(band).wait_send()
     rows_out_sent(tok, rows, send_t, recv_t)
-
-
-def patch_total(counts, shape):
-    total = counts[0]
-    for i in range(1, counts.shape[0]):
-        total = total + counts[i]
-    return jnp.full(shape, total, jnp.int32).astype(f32)
-
-
-VMEM = pl.BlockSpec(memory_space=pltpu.VMEM)
-SMEM = pl.BlockSpec(memory_space=pltpu.SMEM)
-HBM = pl.BlockSpec(memory_space=pltpu.HBM)
-DMA = pltpu.SemaphoreType.DMA
-
-
-def gather(table, counts, vecs, tok):
+    rows_out_sent(cot, cot_rows, send_c, recv_c)
+    for i in range(half // 128):
+        hand_attn(i).wait_send()
+    for copy in local[4:]:
+        copy.wait()
+
+
+def front(table, counts, singles, b_up, tok, cot, wq, wk, wv, wo, qt=512):
     n_items, n_band = lax.axis_size("items"), lax.axis_size("band")
     slots, band_rows, width = tok.shape
+    cut, half = band_rows // 2, width // 2
+    own = 4 * cut
+    pairs = half // 128
+    low = lambda *shape: jax.ShapeDtypeStruct(shape, bf16)
+    wide = lambda *shape: jax.ShapeDtypeStruct(shape, f32)
+    buf = lambda *shape: pltpu.VMEM(shape, bf16)
     return pl.pallas_call(
-        functools.partial(gather_kernel, n_items, n_band),
-        name="gather",
-        in_specs=[SMEM, SMEM, VMEM, VMEM],
-        out_specs=[HBM, VMEM],
+        functools.partial(front_kernel, n_items, n_band, qt),
+        name="front",
+        in_specs=[SMEM, SMEM] + [VMEM] * 13 + [HBM] * 4,
+        out_specs=[VMEM, VMEM] + [HBM] * 6 + [VMEM] + [HBM] * 2 + [VMEM] * 3,
         out_shape=[
-            jax.ShapeDtypeStruct((8, band_rows // 2, width), bf16),
-            jax.ShapeDtypeStruct((4, width), f32),
+            wide(16, width),
+            wide(4, width),
+            low(4, cut, width),
+            low(4, cut, width),
+            low(2 * own, width),
+            low(2 * own, half),
+            low(2 * own, half),
+            low(2 * own, half),
+            wide(pairs, 2, 2 * own),
+            low(own, half),
+            low(own, half),
+            wide(own, width),
+            low(own, width),
+            low(own, width),
         ],
         scratch_shapes=[
+            buf(8, cut, width),
+            buf(width, half),
+            buf(width, half),
+            buf(width, half),
+            buf(width, width),
+            buf(2 * own, width),
+            buf(2 * own, half),
+            buf(2 * own, half),
+            buf(2 * own, half),
+            buf(own, half),
+            buf(own, half),
+            buf(pairs, own, 128),
             pltpu.VMEM((2, width), f32),
             pltpu.VMEM((n_items, 2, width), f32),
             pltpu.VMEM((2, width), f32),
             pltpu.VMEM((n_band, 2, width), f32),
         ]
-        + [DMA((4,))] * 4
+        + [DMA((4,))] * 6
+        + [DMA((pairs,))] * 2
         + [DMA((n_items,))] * 2
-        + [DMA((n_band,))] * 2,
+        + [DMA((n_band,))] * 2
+        + [DMA((12,))],
         compiler_params=params(collective_id=1, has_side_effects=True),
-    )(table, counts, vecs, tok)
-
-
-def half_lanes(ref, row, half):
-    at = pl.multiple_of(lax.rem(lax.axis_index("items"), 2) * half, 128)
-    return ref[row : row + 1, pl.ds(at, half)]
-
-
-def project_kernel(stat, vecs, tok, wq, wk, wv, h1, q, k, v):
-    half = q.shape[1]
-    start = (tok[...].astype(f32) - stat[S_MEAN : S_MEAN + 1, :]) * stat[S_INV : S_INV + 1, :]
-    centre = start - jnp.mean(start, -1, keepdims=True)
-    spread = jnp.mean(centre * centre, -1, keepdims=True)
-    h = centre * lax.rsqrt(spread + epsilon) * vecs[R_G1 : R_G1 + 1, :] + vecs[R_S1 : R_S1 + 1, :]
-    h = h.astype(bf16)
-    h1[...] = h
-    q[...] = ((dot(h, wq[...]) + half_lanes(vecs, R_BQ, half)).astype(bf16) * score_scale).astype(bf16)
-    k[...] = dot(h, wk[...]).astype(bf16)
-    v[...] = (dot(h, wv[...]) + half_lanes(vecs, R_BV, half)).astype(bf16)
-
-
-def project(stat, vecs, tok, wq, wk, wv, block=256):
-    rows, width = tok.shape
-    half = width // 2
-    w = pl.BlockSpec((width, half), lambda i: (0, lax.rem(lax.axis_index("items"), 2)))
-    full = pl.BlockSpec((block, width), lambda i: (i, 0))
-    part = pl.BlockSpec((block, half), lambda i: (i, 0))
-    return pl.pallas_call(
-        project_kernel,
-        name="project",
-        grid=(rows // block,),
-        in_specs=[VMEM, VMEM, full, w, w, w],
-        out_specs=[full] + [part] * 3,
-        out_shape=[jax.ShapeDtypeStruct((rows, width), bf16)]
-        + [jax.ShapeDtypeStruct((rows, half), bf16)] * 3,
-        compiler_params=params(),
         cost_estimate=pl.CostEstimate(
-            flops=6 * rows * width * half, bytes_accessed=12 * 2**20, transcendentals=0
+            flops=16 * own * own * width, bytes_accessed=30 * 2**20, transcendentals=0
         ),
-    )(stat, vecs, tok, wq, wk, wv)
-
-
-def head_lanes(array, head, lane):
-    keep = (lane >= head * HEAD_DIM) & (lane < (head + 1) * HEAD_DIM)
-    return jnp.where(keep, array, jnp.zeros_like(array))
-
-
-def with_spare(array, spare_value, head, lane):
-    spare = (1 - head) * HEAD_DIM
-    return jnp.where(lane == spare, spare_value, head_lanes(array, head, lane))
-
-
-def ones_beside(array, head, lane):
-    return with_spare(array, jnp.ones_like(array), head, lane)
-
-
-def key_bias(table, counts, shape):
-    it, bd, c, yx = place()
-    cut = shape[0] // 8
-    row = lax.broadcasted_iota(jnp.int32, shape, 0)
-    there = row >= 4 * cut
-    row = jnp.where(there, row - 4 * cut, row)
-    band = row // cut
-    half = jnp.where(there, 1 - c, c)
-    position = band * (2 * cut) + half * cut + (row - band * cut)
-    return jnp.where(position < counts[table[yx * 4 + bd]], 0.0, masked_score).astype(bf16)
-
-
-def attend_kernel(qt, table, counts, q, k, v, cot, out, log_total, cot_rows, out_sib, part_sib, *sems):
-    (send, recv, send_s, recv_s) = sems
-    step = pl.program_id(0)
-    rows, lanes = q.shape
-    own = rows // 2
-    it, bd, c, yx = place()
-    sibling = (it + 1 - 2 * c, bd)
-
-    @pl.when(step == 0)
-    def _():
-        greet(column_peers())
-        rows_out(cot, cot_rows, send, recv)
-
-    lane_k = lax.broadcasted_iota(jnp.int32, (rows, lanes), 1)
-    lane_q = lax.broadcasted_iota(jnp.int32, (qt, lanes), 1)
-    row_out = lax.broadcasted_iota(jnp.int32, (lanes, qt), 0)
-    bias = key_bias(table, counts, (rows, lanes))
-    keys = [with_spare(k[...], bias, hd, lane_k) for hd in range(2)]
-    values = [ones_beside(v[...], hd, lane_k).T for hd in range(2)]
-    for t in range(rows // qt):
-        at = slice(t * qt, (t + 1) * qt)
-        scores = [dot(keys[hd], ones_beside(q[at, :], hd, lane_q), 1, 1) for hd in range(2)]
-        tops = [jnp.max(s, 0, keepdims=True) for s in scores]
-        weights = [jnp.exp(s - top).astype(bf16) for s, top in zip(scores, tops)]
-        parts = []
-        for hd in range(2):
-            part = dot(values[hd], weights[hd])
-            spare = (1 - hd) * HEAD_DIM
-            total = part[spare : spare + 1, :]
-            log_total[0, hd : hd + 1, at] = tops[hd] + jnp.log(total)
-            parts.append(part * (1.0 / total))
-        both = jnp.where(row_out < HEAD_DIM, parts[0], parts[1]).T.astype(bf16)
-        if t * qt < own:
-            out[at, :] = both
-        else:
-            part_sib[step, t * qt - own : (t + 1) * qt - own, :] = both
-
-    def hand(i):
-        return remote(
-            part_sib.at[i],
-            out_sib.at[:, pl.ds(pl.multiple_of(i * lanes, lanes), lanes)],
-            send_s.at[i],
-            recv_s.at[i],
-            sibling,
-        )
-
-    hand(step).start()
-
-    @pl.when(step == pl.num_programs(0) - 1)
-    def _():
-        for i in range(part_sib.shape[0]):
-            hand(i).wait()
-        for band in range(4):
-            rows_out_got(cot, cot_rows, send, recv, band)
-        rows_out_sent(cot, cot_rows, send, recv)
-
-
-def attend(table, counts, q, k, v, cot, qt=512):
-    rows, width = q.shape
-    pairs = width // 128
-    blk = pl.BlockSpec((rows, 128), lambda i: (0, i))
-    return pl.pallas_call(
-        functools.partial(attend_kernel, qt),
-        name="attend",
-        grid=(pairs,),
-        in_specs=[SMEM, SMEM, blk, blk, blk, HBM],
-        out_specs=[
-            pl.BlockSpec((rows // 2, 128), lambda i: (0, i)),
-            pl.BlockSpec((1, 2, rows), lambda i: (i, 0, 0)),
-            HBM,
-            HBM,
-        ],
-        out_shape=[
-            jax.ShapeDtypeStruct((rows // 2, width), bf16),
-            jax.ShapeDtypeStruct((pairs, 2, rows), f32),
-            jax.ShapeDtypeStruct((4, cot.shape[1] // 2, cot.shape[2]), bf16),
-            jax.ShapeDtypeStruct((rows // 2, width), bf16),
-        ],
-        scratch_shapes=[pltpu.VMEM((pairs, rows // 2, 128), bf16)]
-        + [DMA((4,))] * 2
-        + [DMA((pairs,))] * 2,
-        compiler_params=params(collective_id=3, has_side_effects=True),
-        cost_estimate=pl.CostEstimate(
-            flops=16 * rows * rows * width, bytes_accessed=5 * 2**20, transcendentals=0
-        ),
-    )(table, counts, q, k, v, cot)
-
-
-def half_rows(ref, which, half):
-    return ref[pl.ds(pl.multiple_of(which * half, 128), half), :]
-
-
-def join_kernel(stat, vecs, attn_a, attn_b, wo, tok, res, h2, h2p):
-    it, bd, c, yx = place()
-    half = attn_a.shape[1]
-    start = (tok[...].astype(f32) - stat[S_MEAN : S_MEAN + 1, :]) * stat[S_INV : S_INV + 1, :]
-    r = dot(attn_a[...], half_rows(wo, c, half)) + dot(attn_b[...], half_rows(wo, 1 - c, half))
-    r = start + r + vecs[R_BO : R_BO + 1, :]
-    res[...] = r
-    centre = r - jnp.mean(r, -1, keepdims=True)
-    spread = jnp.mean(centre * centre, -1, keepdims=True)
-    h = centre * lax.rsqrt(spread + epsilon) * vecs[R_G2 : R_G2 + 1, :] + vecs[R_S2 : R_S2 + 1, :]
-    h = h.astype(bf16)
-    h2[...] = h
-    width = h.shape[1] // 8
-    for x in range(4):
-        first = h[:, 2 * x * width : (2 * x + 1) * width]
-        second = h[:, (2 * x + 1) * width : (2 * x + 2) * width]
-        h2p[:, x * width : (x + 1) * width] = jnp.where(c == 0, first, second)
-        h2p[:, half + x * width : half + (x + 1) * width] = jnp.where(c == 0, second, first)
-
-
-def join(stat, vecs, attn, attn_sib, w_out, tok, block=256):
-    rows, half = attn.shape
-    width = 2 * half
-    act = pl.BlockSpec((block, half), lambda i: (i, 0))
-    full = pl.BlockSpec((block, width), lambda i: (i, 0))
-    return pl.pallas_call(
-        join_kernel,
-        name="join",
-        grid=(rows // block,),
-        in_specs=[VMEM, VMEM, act, act, VMEM, full],
-        out_specs=[full] * 3,
-        out_shape=[
-            jax.ShapeDtypeStruct((rows, width), f32),
-            jax.ShapeDtypeStruct((rows, width), bf16),
-            jax.ShapeDtypeStruct((rows, width), bf16),
-        ],
-        compiler_params=params(),
-        cost_estimate=pl.CostEstimate(
-            flops=2 * rows * width * width, bytes_accessed=8 * 2**20, transcendentals=0
-        ),
-    )(stat, vecs, attn, attn_sib, w_out, tok)
+    )(table, counts, *singles, b_up, tok, cot, wq, wk, wv, wo)
 
 
 def gelu_and_slope(u):
@@ -647,12 +644,6 @@
     return scale * (dz - jnp.mean(dz, -1, keepdims=True) - z * jnp.mean(dz * z, -1, keepdims=True))
 
 
-def normalize(value):
-    centre = value - jnp.mean(value, -1, keepdims=True)
-    scale = lax.rsqrt(jnp.mean(centre * centre, -1, keepdims=True) + epsilon)
-    return centre * scale, scale
-
-
 def tail_kernel(n_items, n_band, qt, *refs):
     (table, counts, stat, vecs, dbu_a, dbu_b, log_total) = refs[:7]
     (res_h, dh_h, cot_h, out_rows, attn_h, attn_sib_h, wo_h, q_h, k_h, v_h, h1_h) = refs[7:18]
@@ -698,7 +689,9 @@
     greet(all_peers(n_items))
     d1 = push(rest_d, rdr, to_x)
     u1 = push(rest_u, rur, to_y)
-    rows_back(out_rows, out_home, send_r, recv_r)
+    load(out_rows, tok).wait()
+    out_blocks = tok.reshape(4, rows // 4, width)
+    rows_back(out_blocks, out_home, send_r, recv_r)
 
     get_res, get_dh, get_cot = load(res_h, res), load(dh_h, dh), load(cot_h, cot)
     get_wo, get_attn, get_sib = load(wo_h, wo), load(attn_h, attn), load(attn_sib_h, attn_sib)
@@ -708,7 +701,6 @@
     get_h1 = load(h1_h, h1)
     lanes = some(c, half)
     get_w = [load(src.at[:, lanes], dst) for src, dst in ((wq_h, wq), (wk_h, wk), (wv_h, wv))]
-    get_tok = load(tok_h.at[pl.ds(0, rows)], tok)
 
     small[...] = jnp.zeros_like(small)
     for i in range(4):
@@ -903,6 +895,10 @@
         first_norm_terms(i)
 
     dh_copy = push(dh1.at[pl.ds(rows, rows)], dh1_sib, sibling)
+    for i in range(4):
+        rows_back_got(out_blocks, out_home, send_r, recv_r, i)
+    rows_back_sent(out_blocks, out_home, send_r, recv_r)
+    get_tok = load(tok_h, tok)
     p1.append(pair_first(3, core_p[3]))
     p2 = [pair_second(0, p1[0])]
 
@@ -1007,9 +1003,6 @@
         for j, ref in enumerate((o_wq, o_wk, o_wv)):
             ref[:, i * 128 : (i + 1) * 128] = all_three[:, j * 128 : (j + 1) * 128]
 
-    for i in range(4):
-        rows_back_got(out_rows, out_home, send_r, recv_r, i)
-    rows_back_sent(out_rows, out_home, send_r, recv_r)
     rows_back_sent(g_blocks, home, send_g, recv_g)
     for copy in sent:
         copy.wait_send()
@@ -1068,9 +1061,35 @@
         ),
     )(
         table, counts, stat, vecs, dbu_a, dbu_b, log_total, res, dh, cot,
-        out_rows.reshape(4, cut, width), attn, attn_sib, wo, q, k, v, h1, wq, wk, wv, tok,
+        out_rows, attn, attn_sib, wo, q, k, v, h1, wq, wk, wv, tok,
         kd, rd, rest_d, ku, ru, rest_u, tokens,
     )
+
+
+def emit_kernel(stat, small, *refs):
+    n = (len(refs) - 11) // 2
+    sources, singles, targets = refs[:n], refs[n : n + 11], refs[n + 11 :]
+    for source, target in zip(sources, targets):
+        target[...] = source[...]
+    singles[0][...] = stat[S_MEAN, :]
+    singles[1][...] = stat[S_VAR, :]
+    for ref, row in zip(singles[2:10], (10, 11, 12, 13, 2, 0, 1, 3)):
+        ref[...] = small[row, :]
+    singles[10][...] = small[4:8, :].reshape(4 * small.shape[1])
+
+
+def emit(stat, small, arrays):
+    width = stat.shape[1]
+    return pl.pallas_call(
+        emit_kernel,
+        name="emit",
+        in_specs=[VMEM] * (2 + len(arrays)),
+        out_specs=[VMEM] * (11 + len(arrays)),
+        out_shape=[jax.ShapeDtypeStruct((width,), f32)] * 10
+        + [jax.ShapeDtypeStruct((4 * width,), f32)]
+        + [jax.ShapeDtypeStruct(a.shape, a.dtype) for a in arrays],
+        compiler_params=params(),
+    )(stat, small, *arrays)
 
 
 def column_layer(
@@ -1080,15 +1099,12 @@
 ):
     slots, band_rows, width = tokens.shape
     rows = slots * band_rows
-    parts = (running_mean, running_var, ln1_gain, ln1_bias, b_query, b_value, b_out)
-    parts += (ln2_gain, ln2_bias, b_down, b_up)
-    vecs = jnp.concatenate([part.astype(f32) for part in parts]).reshape(-1, width)
-    gathered, stat = gather(slot_table, patch_counts, vecs, tokens)
-    tok = gathered.reshape(2 * rows, width)
-    h1, q, k, v = project(stat, vecs, tok, w_query, w_key, w_value)
-    attn, log_total, cot_rows, attn_sib = attend(slot_table, patch_counts, q, k, v, cotangent)
-    cot_rows = cot_rows.reshape(rows, width)
-    res, h2, h2p = join(stat, vecs, attn, attn_sib, w_out, tok)
+    singles = (running_mean, running_var, ln1_gain, ln1_bias, b_query, b_value, b_out)
+    singles += (ln2_gain, ln2_bias, b_down)
+    vecs, stat, tok, cot_rows, h1, q, k, v, log_total, attn, attn_sib, res, h2, h2p = front(
+        slot_table, patch_counts, singles, b_up, tokens, cotangent, w_query, w_key, w_value, w_out
+    )
+    tok, cot_rows = tok.reshape(rows, width), cot_rows.reshape(rows, width)
     out_rows, d_h2, kd, rd, rest_d, ku, ru, rest_u, dbu_a, dbu_b = mlp(
         vecs, h2, h2p, cot_rows, res, w_up, w_down
     )
@@ -1097,12 +1113,14 @@
         out_rows, attn, attn_sib, w_out, q, k, v, h1, w_query, w_key, w_value, tok,
         kd, rd, rest_d, ku, ru, rest_u, tokens,
     )
-    d_gain_two, d_shift_two, d_bo, d_bdown = (small[i] for i in range(4))
-    d_gain_one, d_shift_one, d_bq, d_bv = (small[i] for i in range(10, 14))
+    singles = emit(
+        stat, small, (output, d_tokens, d_wq, d_wk, d_wv, d_w_out, d_w_up, d_w_down)
+    )
+    (new_mean, new_var, d_g1, d_s1, d_bq, d_bv, d_bo, d_g2, d_s2, d_bd, d_bu) = singles[:11]
+    output, d_tokens, d_wq, d_wk, d_wv, d_w_out, d_w_up, d_w_down = singles[11:]
     return (
-        output, d_tokens, stat[S_MEAN], stat[S_VAR], d_gain_one, d_shift_one,
-        d_wq, d_bq, d_wk, d_wv, d_bv, d_w_out, d_bo, d_gain_two, d_shift_two,
-        d_w_up, small[4:8].reshape(-1), d_w_down, d_bdown,
+        output, d_tokens, new_mean, new_var, d_g1, d_s1, d_wq, d_bq, d_wk, d_wv, d_bv,
+        d_w_out, d_bo, d_g2, d_s2, d_w_up, d_bu, d_w_down, d_bd,
     )
 
 

time: 288 us -> 256 us (0.89)
  the two profiles are of different devices: /device:TPU:8 before, /device:TPU:0 now
where the time goes in v5:
time: 256 us; the launch traced here: 251 us
  Pallas kernels  250 us (98%)
    pallas_call x1, Pallas kernels, tail(): pl.pallas_call(functools.partial(tail_kernel, n_items, n_band, qt), name=...  137 us
    pallas_call x1, Pallas kernels, front(): pl.pallas_call(functools.partial(front_kernel, n_items, n_band, qt), name...  58.4 us
    pallas_call x1, Pallas kernels, mlp(): pl.pallas_call(mlp_kernel, name='mlp', grid=(steps + 1,), in_specs=[VMEM]...  50.7 us

profile of v5, /device:TPU:0, one launch (start us, length us, event | category | flops | bytes accessed | tf_op | source)
XLA Modules:
  0.0 250.9 jit_solution(5272692188971977493)
XLA Ops:
  0.7 58.4 %front.1 = (f32[16,1024]{1,0:T(8,128)}, f32[4,1024]{1,0:T(4,128)}, bf16[4,128,1024]{2,1,0:T(8,128)(2,1)}, bf16[4,128,1024]{2,1,0:T(8,128)(2,1)}, bf16[1024,1024]...) custom-call(s32[16]{0:T(128)} %refs_0_.5, ...), custom_call_target="tpu_custom_call" | custom-call | flops 4294967296 | bytes 31457280 | tf_op jit(solution)/shard_map/front/pallas_call | solution.py:385
  59.1 50.7 %mlp.1 = (bf16[512,1024]{1,0:T(8,128)(2,1)}, f32[512,1024]{1,0:T(8,128)}, bf16[2,1024,512]{2,1,0:T(8,128)(2,1)}, bf16[2,1024,512]{2,1,0:T(8,128)(2,1)}, bf16[512...) custom-call(f32[16,1024]{1,0:T(8,128)} %get-tuple-element.72.vecs.re, ...), custom_call_target="tpu_custom_call" | custom-call | flops 25769803776 | bytes 41943040 | tf_op jit(solution)/shard_map/mlp/pallas_call | solution.py:600
  109.8 136.8 %tail.1 = (bf16[2,256,1024]{2,1,0:T(8,128)(2,1)}, bf16[2,256,1024]{2,1,0:T(8,128)(2,1)}, f32[16,1024]{1,0:T(8,128)}, f32[512,256]{1,0:T(8,128)}, f32[128,1024]{1...) custom-call(s32[16]{0:T(128)} %refs_0_.5, s32[16]{0:T(128)} %refs_1_.5, ...), custom_call_target="tpu_custom_call" | custom-call | flops 32212254720 | bytes 41943040 | tf_op jit(solution)/shard_map/tail/pallas_call | solution.py:1021
  246.6 4.1 %emit.1 = (f32[1024]{0:T(1024)}, f32[1024]{0:T(1024)}, f32[1024]{0:T(1024)}, f32[1024]{0:T(1024)}, f32[1024]{0:T(1024)}, /*index=5*/f32[1024]{0:T(1024)}, f32[10...) custom-call(f32[4,1024]{1,0:T(4,128)} %get-tuple-element.71.refs_2_., ...), custom_call_target="tpu_custom_call" | custom-call | tf_op jit(solution)/shard_map/emit/pallas_call | solution.py:1083

commit v6 on v5

--- a/solution.py
+++ b/solution.py
@@ -93,14 +93,14 @@
     pltpu.make_async_copy(src.at[0, pl.ds(0, cut)], dst.at[band], recv.at[band]).wait()
 
 
-def rows_back(src, dst, send, recv):
+def rows_back(src, dst, send, recv, which=range(4)):
     it, bd, c, yx = place()
     cut = src.shape[1]
     home = bd // 2
     s = lax.rem(bd, 2)
     target = dst.at[s, pl.ds(pl.multiple_of(c * cut, cut), cut)]
     got = recv.at[2 * s + c]
-    for r in range(4):
+    for r in which:
         own = (home == c) & (bd == r)
 
         @pl.when(own)
@@ -316,22 +316,21 @@
         bias = key_bias(table, counts, k_pair.shape)
         keys = [with_spare(k_pair, bias, hd, lane_k) for hd in range(2)]
         values = [ones_beside(v_pair, hd, lane_k).T for hd in range(2)]
+        units = [(slice(t * qt, (t + 1) * qt), hd) for t in range(2 * own // qt) for hd in range(2)]
+        scores = [dot(keys[hd], ones_beside(q[at, at_lanes], hd, lane_q), 1, 1) for at, hd in units]
+        tops = [jnp.max(s, 0, keepdims=True) for s in scores]
+        weights = [jnp.exp(s - top).astype(bf16) for s, top in zip(scores, tops)]
+        parts = []
+        for (at, hd), top, weight in zip(units, tops, weights):
+            both = dot(values[hd], weight)
+            spare = (1 - hd) * HEAD_DIM
+            total = both[spare : spare + 1, :]
+            log_total[i, hd : hd + 1, at] = top + jnp.log(total)
+            parts.append(both * (1.0 / total))
         for t in range(2 * own // qt):
-            at = slice(t * qt, (t + 1) * qt)
-            q_tile = q[at, at_lanes]
-            scores = [dot(keys[hd], ones_beside(q_tile, hd, lane_q), 1, 1) for hd in range(2)]
-            tops = [jnp.max(s, 0, keepdims=True) for s in scores]
-            weights = [jnp.exp(s - top).astype(bf16) for s, top in zip(scores, tops)]
-            parts = []
-            for hd in range(2):
-                both = dot(values[hd], weights[hd])
-                spare = (1 - hd) * HEAD_DIM
-                total = both[spare : spare + 1, :]
-                log_total[i, hd : hd + 1, at] = tops[hd] + jnp.log(total)
-                parts.append(both * (1.0 / total))
-            both = jnp.where(row_out < HEAD_DIM, parts[0], parts[1]).T.astype(bf16)
+            both = jnp.where(row_out < HEAD_DIM, parts[2 * t], parts[2 * t + 1]).T.astype(bf16)
             if t * qt < own:
-                attn[at, at_lanes] = both
+                attn[t * qt : (t + 1) * qt, at_lanes] = both
             else:
                 part_sib[i, t * qt - own : (t + 1) * qt - own, :] = both
         hand_attn(i).start()
@@ -463,7 +462,7 @@
     to_x, to_y = (it + 2 - 4 * x, bd), (it + 4 - 8 * y, bd)
     slot = lax.rem(step, 2)
     before = 1 - slot
-    some = gd.shape[1] // 2
+    some = gd.shape[2] // 2
     part = gu.shape[2] // 2
 
     def copies(at, which=(0, 1, 2)):
@@ -479,8 +478,8 @@
         if at == 1:
             first, second = pl.ds(0, some), pl.ds(some, some)
             return [
-                remote(gd.at[1, first], rd.at[1, first], send_d.at[1], recv_d.at[1], to_x),
-                pltpu.make_async_copy(gd.at[1, second], rest_d, rest_sem.at[2]),
+                remote(gd.at[1, :, first], rd.at[1, :, first], send_d.at[1], recv_d.at[1], to_x),
+                pltpu.make_async_copy(gd.at[1, :, second], rest_d, rest_sem.at[2]),
             ]
         return [pltpu.make_async_copy(gd.at[at], kd.at[at - 2], keep_d.at[at - 2])]
 
@@ -556,7 +555,7 @@
         copies(slot, (2,))[0].start()
         for copy in copies(slot, (0, 1)):
             copy.wait_recv()
-        gd[step] = d_wd + got_wd[slot]
+        gd[step] = (d_wd + got_wd[slot]).reshape(gd.shape[1:])
         gu[step, 1] = d_wu[:half] + got_wua[slot]
         up_ready(step, 1)
 
@@ -606,9 +605,9 @@
         out_shape=[
             low(rows, width),
             jax.ShapeDtypeStruct((rows, width), f32),
-            low(2, width, tile),
-            low(2, width, tile),
-            low(width // 2, tile),
+            low(2, 4, width // 4, tile),
+            low(2, 4, width // 4, tile),
+            low(4, width // 8, tile),
             low(4, 2, half // 2, tile),
             low(4, 2, half // 2, tile),
             low(2, half // 2, tile),
@@ -621,7 +620,7 @@
         + [
             pltpu.VMEM((2, half, tile), bf16),
             pltpu.VMEM((rows, width), f32),
-            pltpu.VMEM((steps, width, tile), bf16),
+            pltpu.VMEM((steps, 4, width // 4, tile), bf16),
             pltpu.VMEM((steps, 2, half, tile), bf16),
             DMA((3, 2)),
             DMA((3, 2)),
@@ -676,10 +675,11 @@
         loads.append(copy)
         return copy
 
-    def push(src, dst, to):
+    def push(src, dst, to, start=True):
         i = len(sent)
         copy = remote(src, dst, send.at[i], recv.at[i], to)
-        copy.start()
+        if start:
+            copy.start()
         sent.append(copy)
         return copy
 
@@ -710,8 +710,7 @@
         copy.wait()
     block = 256
 
-    @pl.loop(0, rows // block)
-    def _(i):
+    def second_norm(i):
         at = some(i, block)
         z, scale = normalize(res[at, :])
         d_h = dh[at, :]
@@ -725,6 +724,50 @@
         da[at, :] = dot(d_low, half_rows(wo, c, half), 1, 1).astype(bf16)
         da_send[at, :] = dot(d_low, half_rows(wo, 1 - c, half), 1, 1).astype(bf16)
 
+    theirs, mine = some(1 - x, tile // 4), some(x, tile // 4)
+    cuts = [some(0, eighth), some(1, eighth)]
+    down, up = kd.reshape(2, 2, 2, fourth, tile), ku.reshape(2, 2, 2, tile // 2, tile)
+
+    def down_second(i):
+        return push(kd.at[1 - y, :, cuts[i]], rd2.at[:, cuts[i]], to_y)
+
+    def up_second(s, i):
+        b = block_order(s)
+        ku[b, i] += ru1[b, i] if s < 3 else rur[i]
+        return push(ku.at[b, i, theirs], ru2.at[b, i], to_x)
+
+    def down_third(i):
+        d2[i].wait_recv()
+        kd[y, :, cuts[i]] += rd2[:, cuts[i]]
+        return push(down.at[y, :, 1 - bl, cuts[i]], rd3.at[:, cuts[i]], to_z1)
+
+    def up_third(i):
+        for copy in u2[i]:
+            copy.wait_recv()
+        ku[:, i, mine] += ru2[:, i]
+        return push(up.at[:, 1 - bl, i, mine], ru3.at[:, i], to_z1)
+
+    def down_fourth(i):
+        d3[i].wait_recv()
+        for high in range(2):
+            down[y, high, bl, cuts[i]] += rd3[high, cuts[i]]
+        return push(down.at[y, 1 - bh, bl, cuts[i]], rd4.at[cuts[i]], to_z2)
+
+    def up_fourth(i):
+        u3[i].wait_recv()
+        for high in range(2):
+            up[high, bl, i, mine] += ru3[high, i]
+        return push(up.at[1 - bh, bl, i, mine], ru4.at[i], to_z2)
+
+    second_norm(0)
+    for copy in get_down + get_up:
+        copy.wait()
+    for yy in range(2):
+        kd[yy, :, cuts[0]] += rd1[yy, :, cuts[0]]
+    d2 = [down_second(0)]
+    u2 = [[up_second(s, 0) for s in range(3)], []]
+    second_norm(1)
+
     da_copy = push(da_send, da.at[pl.ds(rows, rows)], sibling)
     early = share_start(
         n_items, it, lambda p: (p, bd), small.at[pl.ds(0, 8)], buf_i, send_i.at[0], recv_i.at[0]
@@ -739,19 +782,13 @@
                 gw[i, xx, cc] = part_wo[cc * eighth : (cc + 1) * eighth]
     core_w = [push(gw.at[i, :, 1 - c], gw_core.at[1 - i], sibling) for i in range(2)]
 
-    for copy in get_down + get_up:
-        copy.wait()
     d1.wait_recv()
-    kd[0] += rd1[0]
-    kd[1, 0:half] += rd1[1, 0:half]
-    kd[1, half:width] += rdr[...]
-    d2 = push(kd.at[1 - y], rd2, to_y)
+    kd[0, :, cuts[1]] += rd1[0, :, cuts[1]]
+    kd[1, :, cuts[1]] += rdr[...]
+    d2.append(down_second(1))
     u1.wait_recv()
-    for s in range(3):
-        ku[block_order(s)] += ru1[block_order(s)]
-    ku[block_order(3)] += rur[...]
-    theirs, mine = some(1 - x, tile // 4), some(x, tile // 4)
-    u2 = push(ku.at[:, :, theirs], ru2, to_x)
+    u2[0].append(up_second(3, 0))
+    u2[1] = [up_second(s, 1) for s in range(4)]
 
     for copy in get_qkv:
         copy.wait()
@@ -853,6 +890,8 @@
         gw[i, :, c] += gw_core[i]
     rel_y = lax.rem(y + c, 2)
     w1 = push(gw.at[1 - rel_y, :, c], gw1, to_y)
+    d3 = [down_third(0)]
+    u3 = [up_third(0)]
 
     pair(1)
     core_p.append(pair_core(1))
@@ -861,15 +900,11 @@
 
     pair(2)
     core_p.append(pair_core(2))
+    d4 = [down_fourth(0)]
+    u4 = [up_fourth(0)]
+    d3.append(down_third(1))
+    u3.append(up_third(1))
     p1.append(pair_first(1, core_p[1]))
-    d2.wait_recv()
-    kd[y] += rd2[...]
-    down = kd.reshape(2, 2, 2, fourth, tile)
-    d3 = push(down.at[y, :, 1 - bl], rd3, to_z1)
-    u2.wait_recv()
-    ku[:, :, mine] += ru2[...]
-    up = ku.reshape(2, 2, 2, tile // 2, tile)
-    u3 = push(up.at[:, 1 - bl, :, mine], ru3, to_z1)
 
     pair(3)
     core_p.append(pair_core(3))
@@ -895,23 +930,20 @@
         first_norm_terms(i)
 
     dh_copy = push(dh1.at[pl.ds(rows, rows)], dh1_sib, sibling)
+    p1.append(pair_first(3, core_p[3]))
     for i in range(4):
         rows_back_got(out_blocks, out_home, send_r, recv_r, i)
     rows_back_sent(out_blocks, out_home, send_r, recv_r)
     get_tok = load(tok_h, tok)
-    p1.append(pair_first(3, core_p[3]))
-    p2 = [pair_second(0, p1[0])]
-
-    @pl.loop(0, rows // block)
-    def _(i):
+    d4.append(down_fourth(1))
+    u4.append(up_fourth(1))
+    p2 = [pair_second(0, p1[0]), pair_second(1, p1[1])]
+
+    g_rows = cot
+    g_blocks = g_rows.reshape(4, rows // 4, width)
+
+    def first_norm(i):
         first_norm_terms(i)
-
-    get_tok.wait()
-    dh_copy.wait_recv()
-    g_rows = cot
-
-    @pl.loop(0, rows // block)
-    def _(i):
         at = some(i, block)
         inv = stat[S_INV : S_INV + 1, :]
         centred = tok[at, :].astype(f32) - stat[S_MEAN : S_MEAN + 1, :]
@@ -922,24 +954,33 @@
         for j, term in enumerate((d_start, d_start * centred, d_h * z, d_h)):
             small[8 + j : 9 + j, :] += jnp.sum(term, 0, keepdims=True)
 
+    get_tok.wait()
+    dh_copy.wait_recv()
+    first_norm(0)
+    rows_back(g_blocks, home, send_g, recv_g, (0, 1))
+    first_norm(1)
+    rows_back(g_blocks, home, send_g, recv_g, (2, 3))
     late = share_start(
         n_items, it, lambda p: (p, bd), small.at[pl.ds(8, 8)], buf_i2, send_i.at[1], recv_i.at[1]
     )
-    g_blocks = g_rows.reshape(4, rows // 4, width)
-    rows_back(g_blocks, home, send_g, recv_g)
-    p2.append(pair_second(1, p1[1]))
+    p2.append(pair_second(2, p1[2]))
     part2[...] = share_end(n_items, late, buf_i2)
     late = share_start(n_band, bd, lambda p: (it, p), part2, buf_b2, send_b.at[1], recv_b.at[1])
 
-    d3.wait_recv()
-    for high in range(2):
-        down[y, high, bl] += rd3[high]
-    d4 = push(down.at[y, 1 - bh, bl], rd4, to_z2)
-    u3.wait_recv()
-    for high in range(2):
-        up[high, bl, :, mine] += ru3[high]
-    u4 = push(up.at[1 - bh, bl, :, mine], ru4, to_z2)
-    p2.append(pair_second(2, p1[2]))
+    pair_third(0, p2[0])
+    pair_third(1, p2[1])
+    p3 = []
+    for i in range(2):
+        there = 2 * (1 - bl) + i
+        p3.append(push(gp.at[there, yx, c], gp3.at[i, 0], to_z1, False))
+        p3.append(push(gp_core.at[there, yx], gp3.at[i, 1], to_z1, False))
+
+    @pl.when(bl == 1)
+    def _():
+        for copy in p3:
+            copy.start()
+
+    p2.append(pair_second(3, p1[3]))
     w2.wait_recv()
     gw[rel_y, x, c] += gw2[...]
 
@@ -949,18 +990,16 @@
     w3 = [
         push(gw.at[rel_y, x, c, :, z_lanes(2 * high + 1 - bl)], gw3.at[high], to_z1) for high in range(2)
     ]
-    p2.append(pair_second(3, p1[3]))
+    pair_third(2, p2[2])
+    pair_third(3, p2[3])
+
+    @pl.when(bl == 0)
+    def _():
+        for copy in p3:
+            copy.start()
+
     sums = share_end(n_band, late, buf_b2)
     total[8:16, :] = sums
-
-    for i in range(4):
-        pair_third(i, p2[i])
-    p3 = []
-    for i in range(2):
-        there = 2 * (1 - bl) + i
-        p3.append(push(gp.at[there, yx, c], gp3.at[i, 0], to_z1))
-        p3.append(push(gp_core.at[there, yx], gp3.at[i, 1], to_z1))
-
     for high in range(2):
         w3[high].wait_recv()
     for high in range(2):
@@ -989,9 +1028,9 @@
         term = fix + slope * (tokens[s, now, :].astype(f32) - stat[S_BATCH : S_BATCH + 1, :])
         d_tok[s, now, :] = (home[s, now, :].astype(f32) + jnp.where(valid, term, 0.0)).astype(bf16)
 
-    d4.wait_recv()
+    for copy in d4 + u4:
+        copy.wait_recv()
     o_down[...] = (down[y, bh, bl].astype(f32) + rd4[...].astype(f32)).T
-    u4.wait_recv()
     up_sum = up[bh, bl, :, mine].astype(f32) + ru4[...].astype(f32)
     for i, h in ((0, 1 - c), (1, c)):
         o_up[:, some(h, tile)] = up_sum[i]
@@ -1013,7 +1052,7 @@
     n_items, n_band = lax.axis_size("items"), lax.axis_size("band")
     rows, width = res.shape
     half, fourth, cut = width // 2, width // 4, rows // 4
-    tile = kd.shape[2]
+    tile = kd.shape[3]
     buf = lambda *shape: pltpu.VMEM(shape, bf16)
     buf32 = lambda *shape: pltpu.VMEM(shape, f32)
     out = lambda *shape: jax.ShapeDtypeStruct(shape, f32)
@@ -1037,7 +1076,7 @@
         scratch_shapes=[
             buf32(rows, width), buf32(rows, width), buf(rows, width), buf(rows, width),
             buf(width, width), buf(rows, half), buf(rows, half),
-            buf(2, width, tile), buf(2, width, tile), buf(half, tile), buf(width, tile), buf(2, s, tile),
+            buf(2, 4, s, tile), buf(2, 4, s, tile), buf(4, e, tile), buf(4, s, tile), buf(2, s, tile),
             buf(s, tile),
             buf(4, 2, tile // 2, tile), buf(4, 2, tile // 2, tile), buf(2, tile // 2, tile),
             buf(4, 2, tile // 4, tile), buf(2, 2, tile // 4, tile), buf(2, tile // 4, tile),
@@ -1051,7 +1090,7 @@
             buf(2, 2 * cut, width),
             buf32(16, width), buf32(n_items, 8, width), buf32(8, width), buf32(n_band, 8, width),
             buf32(n_items, 8, width), buf32(8, width), buf32(n_band, 8, width),
-            DMA((64,)), DMA((64,)), DMA((24,)),
+            DMA((80,)), DMA((80,)), DMA((24,)),
             DMA((4,)), DMA((4,)), DMA((4,)), DMA((4,)),
             DMA((2, n_items)), DMA((2, n_items)), DMA((2, n_band)), DMA((2, n_band)),
         ],

time: 256 us -> 241 us (0.941)
  Pallas kernels: 250 us -> 236 us
    pallas_call x1, Pallas kernels: 137 us -> 124 us  [tail(): pl.pallas_call(functools.partial(tail_kernel, n_items, n_band, qt), name=...]
where the time goes in v6:
time: 241 us; the launch traced here: 237 us
  Pallas kernels  236 us (98%)
    pallas_call x1, Pallas kernels, tail(): pl.pallas_call(functools.partial(tail_kernel, n_items, n_band, qt), name=...  124 us
    pallas_call x1, Pallas kernels, front(): pl.pallas_call(functools.partial(front_kernel, n_items, n_band, qt), name...  56.6 us
    pallas_call x1, Pallas kernels, mlp(): pl.pallas_call(mlp_kernel, name='mlp', grid=(steps + 1,), in_specs=[VMEM]...  51.5 us

profile of v6, /device:TPU:0, one launch (start us, length us, event | category | flops | bytes accessed | tf_op | source)
XLA Modules:
  0.0 237.1 jit_solution(18349207468462707566)
XLA Ops:
  0.7 56.6 %front.1 = (f32[16,1024]{1,0:T(8,128)}, f32[4,1024]{1,0:T(4,128)}, bf16[4,128,1024]{2,1,0:T(8,128)(2,1)}, bf16[4,128,1024]{2,1,0:T(8,128)(2,1)}, bf16[1024,1024]...) custom-call(s32[16]{0:T(128)} %refs_0_.5, ...), custom_call_target="tpu_custom_call" | custom-call | flops 4294967296 | bytes 31457280 | tf_op jit(solution)/shard_map/front/pallas_call | solution.py:384
  57.3 51.5 %mlp.1 = (bf16[512,1024]{1,0:T(8,128)(2,1)}, f32[512,1024]{1,0:T(8,128)}, bf16[2,4,256,512]{3,2,1,0:T(8,128)(2,1)}, bf16[2,4,256,512]{3,2,1,0:T(8,128)(2,1)}, bf...) custom-call(f32[16,1024]{1,0:T(8,128)} %get-tuple-element.72.vecs.re, ...), custom_call_target="tpu_custom_call" | custom-call | flops 25769803776 | bytes 41943040 | tf_op jit(solution)/shard_map/mlp/pallas_call | solution.py:599
  108.7 124.1 %tail.1 = (bf16[2,256,1024]{2,1,0:T(8,128)(2,1)}, bf16[2,256,1024]{2,1,0:T(8,128)(2,1)}, f32[16,1024]{1,0:T(8,128)}, f32[512,256]{1,0:T(8,128)}, f32[128,1024]{1...) custom-call(s32[16]{0:T(128)} %refs_0_.5, s32[16]{0:T(128)} %refs_1_.5, ...), custom_call_target="tpu_custom_call" | custom-call | flops 32212254720 | bytes 41943040 | tf_op jit(solution)/shard_map/tail/pallas_call | solution.py:1060
  232.9 4.1 %emit.1 = (f32[1024]{0:T(1024)}, f32[1024]{0:T(1024)}, f32[1024]{0:T(1024)}, f32[1024]{0:T(1024)}, f32[1024]{0:T(1024)}, /*index=5*/f32[1024]{0:T(1024)}, f32[10...) custom-call(f32[4,1024]{1,0:T(4,128)} %get-tuple-element.71.refs_2_., ...), custom_call_target="tpu_custom_call" | custom-call | tf_op jit(solution)/shard_map/emit/pallas_call | solution.py:1122

commit v7 on v6

--- a/solution.py
+++ b/solution.py
@@ -785,10 +785,8 @@
     d1.wait_recv()
     kd[0, :, cuts[1]] += rd1[0, :, cuts[1]]
     kd[1, :, cuts[1]] += rdr[...]
-    d2.append(down_second(1))
     u1.wait_recv()
     u2[0].append(up_second(3, 0))
-    u2[1] = [up_second(s, 1) for s in range(4)]
 
     for copy in get_qkv:
         copy.wait()
@@ -889,13 +887,15 @@
     for i in range(2):
         gw[i, :, c] += gw_core[i]
     rel_y = lax.rem(y + c, 2)
-    w1 = push(gw.at[1 - rel_y, :, c], gw1, to_y)
     d3 = [down_third(0)]
+    d2.append(down_second(1))
     u3 = [up_third(0)]
+    u2[1] = [up_second(s, 1) for s in range(4)]
 
     pair(1)
     core_p.append(pair_core(1))
     p1 = [pair_first(0, core_p[0])]
+    w1 = push(gw.at[1 - rel_y, :, c], gw1, to_y)
     total[0:8, :] = share_end(n_band, early, buf_b)
 
     pair(2)

time: 241 us -> 239 us (level)
  the two profiles are of different devices: /device:TPU:0 before, /device:TPU:8 now
where the time goes in v7:
time: 239 us; the launch traced here: 235 us
  Pallas kernels  234 us (98%)
    pallas_call x1, Pallas kernels, tail(): pl.pallas_call(functools.partial(tail_kernel, n_items, n_band, qt), name=...  119 us
    pallas_call x1, Pallas kernels, front(): pl.pallas_call(functools.partial(front_kernel, n_items, n_band, qt), name...  57.2 us
    pallas_call x1, Pallas kernels, mlp(): pl.pallas_call(mlp_kernel, name='mlp', grid=(steps + 1,), in_specs=[VMEM]...  54 us

profile of v7, /device:TPU:8, one launch (start us, length us, event | category | flops | bytes accessed | tf_op | source)
XLA Modules:
  0.0 234.7 jit_solution(8288656230902194005)
XLA Ops:
  0.7 57.2 %front.1 = (f32[16,1024]{1,0:T(8,128)}, f32[4,1024]{1,0:T(4,128)}, bf16[4,128,1024]{2,1,0:T(8,128)(2,1)}, bf16[4,128,1024]{2,1,0:T(8,128)(2,1)}, bf16[1024,1024]...) custom-call(s32[16]{0:T(128)} %refs_0_.5, ...), custom_call_target="tpu_custom_call" | custom-call | flops 4294967296 | bytes 31457280 | tf_op jit(solution)/shard_map/front/pallas_call | solution.py:384
  57.8 54.0 %mlp.1 = (bf16[512,1024]{1,0:T(8,128)(2,1)}, f32[512,1024]{1,0:T(8,128)}, bf16[2,4,256,512]{3,2,1,0:T(8,128)(2,1)}, bf16[2,4,256,512]{3,2,1,0:T(8,128)(2,1)}, bf...) custom-call(f32[16,1024]{1,0:T(8,128)} %get-tuple-element.72.vecs.re, ...), custom_call_target="tpu_custom_call" | custom-call | flops 25769803776 | bytes 41943040 | tf_op jit(solution)/shard_map/mlp/pallas_call | solution.py:599
  111.8 118.7 %tail.1 = (bf16[2,256,1024]{2,1,0:T(8,128)(2,1)}, bf16[2,256,1024]{2,1,0:T(8,128)(2,1)}, f32[16,1024]{1,0:T(8,128)}, f32[512,256]{1,0:T(8,128)}, f32[128,1024]{1...) custom-call(s32[16]{0:T(128)} %refs_0_.5, s32[16]{0:T(128)} %refs_1_.5, ...), custom_call_target="tpu_custom_call" | custom-call | flops 32212254720 | bytes 41943040 | tf_op jit(solution)/shard_map/tail/pallas_call | solution.py:1060
  230.5 4.1 %emit.1 = (f32[1024]{0:T(1024)}, f32[1024]{0:T(1024)}, f32[1024]{0:T(1024)}, f32[1024]{0:T(1024)}, f32[1024]{0:T(1024)}, /*index=5*/f32[1024]{0:T(1024)}, f32[10...) custom-call(f32[4,1024]{1,0:T(4,128)} %get-tuple-element.71.refs_2_., ...), custom_call_target="tpu_custom_call" | custom-call | tf_op jit(solution)/shard_map/emit/pallas_call | solution.py:1122

commit v8 on v7

--- a/solution.py
+++ b/solution.py
@@ -1117,13 +1117,20 @@
     singles[10][...] = small[4:8, :].reshape(4 * small.shape[1])
 
 
+def quarter(array):
+    lead = array.shape[:-2]
+    block = lead + (array.shape[-2] // 4, array.shape[-1])
+    return pl.BlockSpec(block, lambda i: (0,) * len(lead) + (i, 0))
+
+
 def emit(stat, small, arrays):
     width = stat.shape[1]
     return pl.pallas_call(
         emit_kernel,
         name="emit",
-        in_specs=[VMEM] * (2 + len(arrays)),
-        out_specs=[VMEM] * (11 + len(arrays)),
+        grid=(4,),
+        in_specs=[VMEM] * 2 + [quarter(a) for a in arrays],
+        out_specs=[VMEM] * 11 + [quarter(a) for a in arrays],
         out_shape=[jax.ShapeDtypeStruct((width,), f32)] * 10
         + [jax.ShapeDtypeStruct((4 * width,), f32)]
         + [jax.ShapeDtypeStruct(a.shape, a.dtype) for a in arrays],

time: 239 us -> 240 us (level)
  no operation moved by 1% of the time
where the time goes in v8:
time: 240 us; the launch traced here: 235 us
  Pallas kernels  234 us (98%)
    pallas_call x1, Pallas kernels, tail(): pl.pallas_call(functools.partial(tail_kernel, n_items, n_band, qt), name=...  119 us
    pallas_call x1, Pallas kernels, front(): pl.pallas_call(functools.partial(front_kernel, n_items, n_band, qt), name...  57.2 us
    pallas_call x1, Pallas kernels, mlp(): pl.pallas_call(mlp_kernel, name='mlp', grid=(steps + 1,), in_specs=[VMEM]...  54 us

profile of v8, /device:TPU:8, one launch (start us, length us, event | category | flops | bytes accessed | tf_op | source)
XLA Modules:
  0.0 235.2 jit_solution(7220943192897861208)
XLA Ops:
  0.7 57.2 %front.1 = (f32[16,1024]{1,0:T(8,128)}, f32[4,1024]{1,0:T(4,128)}, bf16[4,128,1024]{2,1,0:T(8,128)(2,1)}, bf16[4,128,1024]{2,1,0:T(8,128)(2,1)}, bf16[1024,1024]...) custom-call(s32[16]{0:T(128)} %refs_0_.5, ...), custom_call_target="tpu_custom_call" | custom-call | flops 4294967296 | bytes 31457280 | tf_op jit(solution)/shard_map/front/pallas_call | solution.py:384
  57.8 54.0 %mlp.1 = (bf16[512,1024]{1,0:T(8,128)(2,1)}, f32[512,1024]{1,0:T(8,128)}, bf16[2,4,256,512]{3,2,1,0:T(8,128)(2,1)}, bf16[2,4,256,512]{3,2,1,0:T(8,128)(2,1)}, bf...) custom-call(f32[16,1024]{1,0:T(8,128)} %get-tuple-element.72.vecs.re, ...), custom_call_target="tpu_custom_call" | custom-call | flops 25769803776 | bytes 41943040 | tf_op jit(solution)/shard_map/mlp/pallas_call | solution.py:599
  111.8 118.7 %tail.1 = (bf16[2,256,1024]{2,1,0:T(8,128)(2,1)}, bf16[2,256,1024]{2,1,0:T(8,128)(2,1)}, f32[16,1024]{1,0:T(8,128)}, f32[512,256]{1,0:T(8,128)}, f32[128,1024]{1...) custom-call(s32[16]{0:T(128)} %refs_0_.5, s32[16]{0:T(128)} %refs_1_.5, ...), custom_call_target="tpu_custom_call" | custom-call | flops 32212254720 | bytes 41943040 | tf_op jit(solution)/shard_map/tail/pallas_call | solution.py:1060
  230.5 4.5 %emit.1 = (f32[1024]{0:T(1024)}, f32[1024]{0:T(1024)}, f32[1024]{0:T(1024)}, f32[1024]{0:T(1024)}, f32[1024]{0:T(1024)}, /*index=5*/f32[1024]{0:T(1024)}, f32[10...) custom-call(f32[4,1024]{1,0:T(4,128)} %get-tuple-element.71.refs_2_., ...), custom_call_target="tpu_custom_call" | custom-call | tf_op jit(solution)/shard_map/emit/pallas_call | solution.py:1128
